TPU v7x, 32 devices: a whole 2x2x4 slice. The times are simulated.
32 devices in a mesh: tok: 4 (over y, core), wide: 8 (over z, x).
Axes of the slice: x: 2, y: 2, z: 4, core: 2. Of those that a mesh axis runs over, the one named last changes fastest.
Arguments:
- tokens: bfloat16 [8192, 2048], P('tok', 'wide'), may hold values from -6 to 6
- cotangent: bfloat16 [8192, 2048], P('tok', 'wide'), may hold values from -6 to 6
- gain_attn: float32 [2048], P('wide'), may hold values from 0.5 to 1.5
- gain_ffn: float32 [2048], P('wide'), may hold values from 0.5 to 1.5
- w_query: bfloat16 [2048, 2048], P('wide'), may hold values from -0.125 to 0.125
- w_key: bfloat16 [2048, 256], P('wide'), may hold values from -0.125 to 0.125
- w_value: bfloat16 [2048, 256], P('wide'), may hold values from -0.125 to 0.125
- w_output: bfloat16 [2048, 2048], P('wide'), may hold values from -0.125 to 0.125
- w_gate: bfloat16 [2048, 5632], P('wide'), may hold values from -0.125 to 0.125
- w_up: bfloat16 [2048, 5632], P('wide'), may hold values from -0.125 to 0.125
- w_down: bfloat16 [5632, 2048], P('wide'), may hold values from -0.078125 to 0.078125
- adapt_main: float32 [2048, 96], P('wide'), may hold values from -0.125 to 0.125
- adapt_down: float32 [5632, 16], P('wide'), may hold values from -0.078125 to 0.078125
- adapt_outer: float32 [16, 17920], replicated, may hold values from -0.375 to 0.375
- magnitudes: float32 [17920], replicated, may hold values from 0.5 to 12
- main_first: float32 [2048, 96], P('wide', 'tok'), may hold values from -0.001953125 to 0.001953125
- main_second: float32 [2048, 96], P('wide', 'tok'), may hold values from 1.6910173e-09 to 6.7640693e-09
- down_first: float32 [5632, 16], P('wide', 'tok'), may hold values from -0.001953125 to 0.001953125
- down_second: float32 [5632, 16], P('wide', 'tok'), may hold values from 1.6910173e-09 to 6.7640693e-09
- outer_first: float32 [16, 17920], P(None, ('tok', 'wide')), may hold values from -0.001953125 to 0.001953125
- outer_second: float32 [16, 17920], P(None, ('tok', 'wide')), may hold values from 1.6910173e-09 to 6.7640693e-09
- mag_first: float32 [17920], P(('tok', 'wide')), may hold values from -0.0078125 to 0.0078125
- mag_second: float32 [17920], P(('tok', 'wide')), may hold values from 1.3528139e-09 to 5.4112554e-09
- segments: int32 [4, 2048], P('tok'), may hold values from 0 to 7, never falling along the last dimension, each value on 1 to 1024 neighbouring positions
Outputs:
- layer_out: bfloat16 [8192, 2048], P('tok', 'wide')
- grad_tokens: bfloat16 [8192, 2048], P('tok', 'wide')
- grad_norm: float32 [], replicated
- main_new: float32 [2048, 96], P('wide', 'tok')
- main_first_new: float32 [2048, 96], P('wide', 'tok')
- main_second_new: float32 [2048, 96], P('wide', 'tok')
- down_new: float32 [5632, 16], P('wide', 'tok')
- down_first_new: float32 [5632, 16], P('wide', 'tok')
- down_second_new: float32 [5632, 16], P('wide', 'tok')
- outer_new: float32 [16, 17920], P(None, ('tok', 'wide'))
- outer_first_new: float32 [16, 17920], P(None, ('tok', 'wide'))
- outer_second_new: float32 [16, 17920], P(None, ('tok', 'wide'))
- mag_new: float32 [17920], P(('tok', 'wide'))
- mag_clipped: float32 [17920], P(('tok', 'wide'))
- mag_second_new: float32 [17920], P(('tok', 'wide'))
Inputs may be any that keep to these rules, and one draw needn't show every extreme that they name: `segments`: segment numbers along a row never fall; each segment holds 1 to 1024 positions, and one holds exactly that many.
All inputs are finite; a program needn't handle non-finite values.
Results may differ from a plain program's by a relative error of at most 0.023.
Values may be sent and summed in bfloat16 or wider, within the bound.
No kernel may reach another device: no remote copies, remote signals or barrier semaphores. Data moves between devices by JAX's collectives and lax.ppermute only.
A program may use at most 448 MiB of HBM per device.

v0:
```python
import jax
import jax.numpy as jnp
from jax import lax
from jax.sharding import PartitionSpec as P

D = 2048
HEADS = 32
HD = 64
KVH = 4
FF = 5632
STEP = 10


EPS_NORM = 1e-05
ROPE_BASE = 10000.0
DORA_SCALE = 2.0
CLIP_MAX = 1.0
BETA_FIRST = 0.9
BETA_SECOND = 0.999
ADAM_EPS = 1e-08
WEIGHT_DECAY = 0.01
RATE_ADAPT = 0.02
RATE_OUTER = 0.05
RATE_MAGNITUDE = 0.4
PRECISE = lax.Precision.HIGHEST
MASKED = -1e30
LAST_LAST = (((1,), (1,)), ((), ()))
FIRST_FIRST = (((0,), (0,)), ((), ()))


def column_spans():
    widths = [D, KVH * HD, KVH * HD, D, FF, FF, D]
    col_spans = []
    offset = 0
    for col_width in widths:
        col_spans.append((offset, col_width))
        offset = offset + col_width
    return col_spans


def rotary_tables(segment_row):
    length = segment_row.shape[0]
    places = jnp.arange(length, dtype=jnp.int32)
    earlier = jnp.concatenate([segment_row[:1] - 1, segment_row[:-1]])
    starts = lax.cummax(jnp.where(segment_row != earlier, places, 0), axis=0)
    offsets = (places - starts).astype(jnp.float32)
    half_dim = HD // 2
    frequency = ROPE_BASE ** (-2.0 * jnp.arange(half_dim, dtype=jnp.float32) / HD)
    angles = offsets[:, None] * frequency[None, :]
    allowed = (places[None, :] <= places[:, None]) & (segment_row[:, None] == segment_row[None, :])
    return (jnp.cos(angles), jnp.sin(angles), allowed)


def rotate_forward(values, cosine_table, sine_table):
    half_dim = values.shape[-1] // 2
    first_half = values[..., :half_dim]
    second_half = values[..., half_dim:]
    cos_wide = cosine_table[:, None, :]
    sin_wide = sine_table[:, None, :]
    return jnp.concatenate(
        [
            first_half * cos_wide - second_half * sin_wide,
            second_half * cos_wide + first_half * sin_wide,
        ],
        axis=-1,
    )


def rotate_backward(grad_values, cosine_table, sine_table):
    half_dim = grad_values.shape[-1] // 2
    first_half = grad_values[..., :half_dim]
    second_half = grad_values[..., half_dim:]
    cos_wide = cosine_table[:, None, :]
    sin_wide = sine_table[:, None, :]
    return jnp.concatenate(
        [
            first_half * cos_wide + second_half * sin_wide,
            second_half * cos_wide - first_half * sin_wide,
        ],
        axis=-1,
    )


def rounded_copy(values):
    return values.astype(jnp.bfloat16).astype(jnp.float32)


def dora_partial(inputs_low, base, adapter, outer_cols):
    reduced = jnp.dot(inputs_low, adapter.astype(jnp.bfloat16), preferred_element_type=jnp.float32)
    direct = jnp.dot(inputs_low, base, preferred_element_type=jnp.float32)
    return direct + DORA_SCALE * jnp.dot(reduced, rounded_copy(outer_cols), precision=PRECISE)


def dora_back(grad_low, inputs_low, base, adapter, outer_cols):
    outer_low = outer_cols.astype(jnp.bfloat16)
    adapter_low = rounded_copy(adapter)
    through = lax.dot_general(grad_low, base, LAST_LAST, preferred_element_type=jnp.float32)
    narrow = lax.dot_general(grad_low, outer_low, LAST_LAST, preferred_element_type=jnp.float32)
    grad_inputs = through + DORA_SCALE * lax.dot_general(
        narrow, adapter_low, LAST_LAST, precision=PRECISE
    )
    gram_matrix = lax.dot_general(
        inputs_low, grad_low, FIRST_FIRST, preferred_element_type=jnp.float32
    )
    grad_adapter = DORA_SCALE * lax.dot_general(
        gram_matrix, outer_low.astype(jnp.float32), LAST_LAST, precision=PRECISE
    )
    grad_outer = DORA_SCALE * lax.dot_general(
        adapter_low, gram_matrix, FIRST_FIRST, precision=PRECISE
    )
    return (grad_inputs, grad_adapter, grad_outer)


def norm_terms(merged, adapter, outer_cols, norm_weight):
    weighted = merged * norm_weight[None, :]
    grad_adapter = DORA_SCALE * lax.dot_general(weighted, outer_cols, LAST_LAST, precision=PRECISE)
    grad_outer = DORA_SCALE * lax.dot_general(adapter, weighted, FIRST_FIRST, precision=PRECISE)
    return (grad_adapter, grad_outer)


def adam(param, grad, first, second, rate, clip_factor):
    clipped = grad * clip_factor
    first_new = BETA_FIRST * first + (1.0 - BETA_FIRST) * clipped
    second_new = BETA_SECOND * second + (1.0 - BETA_SECOND) * clipped * clipped
    first_hat = first_new / (1.0 - BETA_FIRST**STEP)
    second_hat = second_new / (1.0 - BETA_SECOND**STEP)
    param_new = param - rate * (
        first_hat / (jnp.sqrt(second_hat) + ADAM_EPS) + WEIGHT_DECAY * param
    )
    return (param_new, first_new, second_new)


def squared_sum(values):
    return jnp.sum(values * values)


def shards(
    tokens,
    cotangent,
    gain_attn,
    gain_ffn,
    w_query,
    w_key,
    w_value,
    w_output,
    w_gate,
    w_up,
    w_down,
    adapt_main,
    adapt_down,
    adapt_outer,
    magnitudes,
    main_first,
    main_second,
    down_first,
    down_second,
    outer_first,
    outer_second,
    mag_first,
    mag_second,
    segments,
):
    wide_count = lax.axis_size("wide")
    tok_count = lax.axis_size("tok")
    wide_index = lax.axis_index("wide")
    tok_index = lax.axis_index("tok")
    col_spans = column_spans()
    feature_share = tokens.shape[1]
    hidden_share = w_down.shape[0]
    heads_here = HEADS // wide_count
    group_index = wide_index * heads_here // (HEADS // KVH)
    key_start = group_index * HD
    rank_width = adapt_down.shape[1]
    outs_width = adapt_outer.shape[1]
    bases = [w_query, w_key, w_value, w_output, w_gate, w_up, w_down]
    adapters = [
        adapt_main[:, number * rank_width : (number + 1) * rank_width] for number in range(6)
    ] + [adapt_down]
    outers = [
        adapt_outer[:, col_start : col_start + col_width] for col_start, col_width in col_spans
    ]
    merged_all = [
        bases[number].astype(jnp.float32)
        + DORA_SCALE * jnp.dot(adapters[number], outers[number], precision=PRECISE)
        for number in range(7)
    ]
    partial_norms = jnp.concatenate([jnp.sum(merged * merged, axis=0) for merged in merged_all])
    col_norms = jnp.sqrt(lax.psum(partial_norms, "wide"))
    scales = magnitudes / col_norms
    own_starts = [
        col_spans[0][0] + wide_index * feature_share,
        col_spans[1][0],
        col_spans[2][0],
        col_spans[3][0] + wide_index * feature_share,
        col_spans[4][0] + wide_index * hidden_share,
        col_spans[5][0] + wide_index * hidden_share,
        col_spans[6][0] + wide_index * feature_share,
    ]
    own_widths = [
        feature_share,
        KVH * HD,
        KVH * HD,
        feature_share,
        hidden_share,
        hidden_share,
        feature_share,
    ]
    own_scales = [
        lax.dynamic_slice_in_dim(scales, own_starts[number], own_widths[number])
        for number in range(7)
    ]
    cosine_table, sine_table, allowed = rotary_tables(segments[0])
    score_scale = HD ** (-0.5)

    def spread(partial_sum):
        return lax.psum_scatter(partial_sum, "wide", scatter_dimension=1, tiled=True)

    def collect(grad_low):
        return lax.all_gather(grad_low, "wide", axis=1, tiled=True)

    def norm_rows(values, gain_row):
        row_total = lax.psum(jnp.sum(values * values, axis=1), "wide")
        inverse = lax.rsqrt(row_total / D + EPS_NORM)
        return ((values * inverse[:, None] * gain_row[None, :]).astype(jnp.bfloat16), inverse)

    def norm_rows_back(values, gain_row, inverse, grad_normed):
        row_inner = lax.psum(jnp.sum(values * gain_row[None, :] * grad_normed, axis=1), "wide")
        return (
            grad_normed * gain_row[None, :] * inverse[:, None]
            - values * (inverse * inverse * inverse * row_inner / D)[:, None]
        )

    residual = tokens.astype(jnp.float32)
    length = residual.shape[0]
    normed_one, inverse_one = norm_rows(residual, gain_attn)
    query_z = spread(dora_partial(normed_one, w_query, adapters[0], outers[0]))
    key_z, value_z = lax.psum(
        (
            dora_partial(normed_one, w_key, adapters[1], outers[1]),
            dora_partial(normed_one, w_value, adapters[2], outers[2]),
        ),
        "wide",
    )
    queries = rotate_forward(
        (query_z * own_scales[0]).reshape(length, heads_here, HD), cosine_table, sine_table
    ).astype(jnp.bfloat16)
    key_group = lax.dynamic_slice_in_dim(key_z * own_scales[1], key_start, HD, 1)
    value_group = lax.dynamic_slice_in_dim(value_z * own_scales[2], key_start, HD, 1)
    keys_low = (
        rotate_forward(key_group.reshape(length, 1, HD), cosine_table, sine_table)
        .reshape(length, HD)
        .astype(jnp.bfloat16)
    )
    values_low = value_group.astype(jnp.bfloat16)
    scores = (
        jnp.einsum("thd,sd->hts", queries, keys_low, preferred_element_type=jnp.float32)
        * score_scale
    )
    scores = jnp.where(allowed[None], scores, MASKED)
    score_peak = jnp.max(scores, axis=-1, keepdims=True)
    exp_scores = jnp.exp(scores - score_peak)
    exp_total = jnp.sum(exp_scores, axis=-1, keepdims=True)
    weights = exp_scores / exp_total
    log_total = (score_peak + jnp.log(exp_total))[..., 0]
    mixed_heads = jnp.einsum(
        "hts,sd->thd", weights.astype(jnp.bfloat16), values_low, preferred_element_type=jnp.float32
    )
    attended = mixed_heads.reshape(length, heads_here * HD).astype(jnp.bfloat16)
    output_z = spread(dora_partial(attended, w_output, adapters[3], outers[3]))
    hidden_one = residual + output_z * own_scales[3]
    normed_two, inverse_two = norm_rows(hidden_one, gain_ffn)
    gate_z = lax.psum_scatter(
        dora_partial(normed_two, w_gate, adapters[4], outers[4]).astype(jnp.bfloat16),
        "wide",
        scatter_dimension=1,
        tiled=True,
    ).astype(jnp.float32)
    up_z = lax.psum_scatter(
        dora_partial(normed_two, w_up, adapters[5], outers[5]).astype(jnp.bfloat16),
        "wide",
        scatter_dimension=1,
        tiled=True,
    ).astype(jnp.float32)
    gate_act = gate_z * own_scales[4]
    up_act = up_z * own_scales[5]
    hidden = (jax.nn.silu(gate_act) * up_act).astype(jnp.bfloat16)
    down_z = spread(dora_partial(hidden, w_down, adapters[6], outers[6]))
    layer_sum = hidden_one + down_z * own_scales[6]
    stored = {
        "residual": residual,
        "normed_one": normed_one,
        "inverse_one": inverse_one,
        "query_z": query_z,
        "key_z": key_z,
        "value_z": value_z,
        "queries": queries,
        "keys_low": keys_low,
        "values_low": values_low,
        "log_total": log_total,
        "attended": attended,
        "output_z": output_z,
        "hidden_one": hidden_one,
        "normed_two": normed_two,
        "inverse_two": inverse_two,
        "gate_z": gate_z,
        "up_z": up_z,
        "hidden": hidden,
        "down_z": down_z,
        "layer_sum": layer_sum,
    }
    layer_out = stored["layer_sum"].astype(jnp.bfloat16)
    length = tokens.shape[0]
    resid_grad = cotangent.astype(jnp.float32)
    scale_down = jnp.sum(resid_grad * stored["down_z"], axis=0)
    full_down = collect((resid_grad * own_scales[6]).astype(jnp.bfloat16))
    grad_hidden, prod_a_down, prod_b_down = dora_back(
        full_down, stored["hidden"], w_down, adapters[6], outers[6]
    )
    gate_act = stored["gate_z"] * own_scales[4]
    up_act = stored["up_z"] * own_scales[5]
    gate_sigmoid = jax.nn.sigmoid(gate_act)
    grad_up_act = grad_hidden * gate_act * gate_sigmoid
    grad_gate_act = grad_hidden * up_act * gate_sigmoid * (1.0 + gate_act * (1.0 - gate_sigmoid))
    scale_gate = jnp.sum(grad_gate_act * stored["gate_z"], axis=0)
    scale_up = jnp.sum(grad_up_act * stored["up_z"], axis=0)
    full_gate, full_up = (
        lax.all_gather(
            (grad_gate_act * own_scales[4]).astype(jnp.bfloat16), "wide", axis=1, tiled=True
        ),
        lax.all_gather(
            (grad_up_act * own_scales[5]).astype(jnp.bfloat16), "wide", axis=1, tiled=True
        ),
    )
    in_gate, prod_a_gate, prod_b_gate = dora_back(
        full_gate, stored["normed_two"], w_gate, adapters[4], outers[4]
    )
    in_up, prod_a_up, prod_b_up = dora_back(
        full_up, stored["normed_two"], w_up, adapters[5], outers[5]
    )
    grad_mid = resid_grad + norm_rows_back(
        stored["hidden_one"], gain_ffn, stored["inverse_two"], in_gate + in_up
    )
    scale_output = jnp.sum(grad_mid * stored["output_z"], axis=0)
    full_output = collect((grad_mid * own_scales[3]).astype(jnp.bfloat16))
    in_output, prod_a_output, prod_b_output = dora_back(
        full_output, stored["attended"], w_output, adapters[3], outers[3]
    )
    grad_mixed = in_output.astype(jnp.bfloat16).reshape(length, heads_here, HD)
    queries = stored["queries"]
    keys_low = stored["keys_low"]
    values_low = stored["values_low"]
    scores = (
        jnp.einsum("thd,sd->hts", queries, keys_low, preferred_element_type=jnp.float32)
        * score_scale
    )
    scores = jnp.where(allowed[None], scores, MASKED)
    weights = jnp.exp(scores - stored["log_total"][..., None])
    grad_weights = jnp.einsum(
        "thd,sd->hts", grad_mixed, values_low, preferred_element_type=jnp.float32
    )
    weight_inner = jnp.sum(weights * grad_weights, axis=-1, keepdims=True)
    grad_scores = (weights * (grad_weights - weight_inner)).astype(jnp.bfloat16)
    grad_queries = (
        jnp.einsum("hts,sd->thd", grad_scores, keys_low, preferred_element_type=jnp.float32)
        * score_scale
    )
    grad_keys = (
        jnp.einsum("hts,thd->sd", grad_scores, queries, preferred_element_type=jnp.float32)
        * score_scale
    )
    grad_values = jnp.einsum(
        "hts,thd->sd", weights.astype(jnp.bfloat16), grad_mixed, preferred_element_type=jnp.float32
    )
    query_grad = rotate_backward(grad_queries, cosine_table, sine_table).reshape(
        length, heads_here * HD
    )
    key_grad = rotate_backward(grad_keys.reshape(length, 1, HD), cosine_table, sine_table).reshape(
        length, HD
    )
    scale_query = jnp.sum(query_grad * stored["query_z"], axis=0)
    key_pad = lax.dynamic_update_slice_in_dim(
        jnp.zeros((length, KVH * HD), jnp.float32), key_grad, key_start, 1
    )
    value_pad = lax.dynamic_update_slice_in_dim(
        jnp.zeros((length, KVH * HD), jnp.float32), grad_values, key_start, 1
    )
    scale_key = jnp.sum(key_pad * stored["key_z"], axis=0)
    scale_value = jnp.sum(value_pad * stored["value_z"], axis=0)
    key_total, value_total = (
        lax.psum((key_pad * own_scales[1]).astype(jnp.bfloat16), "wide").astype(jnp.float32),
        lax.psum((value_pad * own_scales[2]).astype(jnp.bfloat16), "wide").astype(jnp.float32),
    )
    full_query = collect((query_grad * own_scales[0]).astype(jnp.bfloat16))
    in_query, prod_a_query, prod_b_query = dora_back(
        full_query, stored["normed_one"], w_query, adapters[0], outers[0]
    )
    in_key, prod_a_key, prod_b_key = dora_back(
        key_total.astype(jnp.bfloat16), stored["normed_one"], w_key, adapters[1], outers[1]
    )
    in_value, prod_a_value, prod_b_value = dora_back(
        value_total.astype(jnp.bfloat16), stored["normed_one"], w_value, adapters[2], outers[2]
    )
    grad_tokens = (
        grad_mid
        + norm_rows_back(
            stored["residual"], gain_attn, stored["inverse_one"], in_query + in_key + in_value
        )
    ).astype(jnp.bfloat16)
    scale_parts = [
        scale_query,
        scale_key,
        scale_value,
        scale_output,
        scale_gate,
        scale_up,
        scale_down,
    ]
    scale_local = jnp.zeros((outs_width,), jnp.float32)
    for number in range(7):
        scale_local = lax.dynamic_update_slice_in_dim(
            scale_local, scale_parts[number], own_starts[number], 0
        )
    scale_wide = lax.psum(scale_local.astype(jnp.bfloat16), "wide").astype(jnp.float32)
    norm_weight = -scale_wide * magnitudes / (col_norms * col_norms * col_norms)
    mag_grad = scale_local / col_norms
    prod_a = [
        prod_a_query,
        prod_a_key,
        prod_a_value,
        prod_a_output,
        prod_a_gate,
        prod_a_up,
        prod_a_down,
    ]
    prod_b = [
        prod_b_query,
        prod_b_key,
        prod_b_value,
        prod_b_output,
        prod_b_gate,
        prod_b_up,
        prod_b_down,
    ]
    grads_a = []
    grads_b = []
    for number in range(7):
        col_start, col_width = col_spans[number]
        term_a, term_b = norm_terms(
            merged_all[number],
            adapters[number],
            outers[number],
            norm_weight[col_start : col_start + col_width],
        )
        grads_a.append(prod_a[number] + term_a)
        grads_b.append(prod_b[number] + term_b)
    grad_main = jnp.concatenate(grads_a[:6], axis=1)
    grad_down = grads_a[6]
    grad_outer = jnp.concatenate(grads_b, axis=1)
    main_cols = adapt_main.shape[1] // tok_count
    down_cols = rank_width // tok_count
    outer_share = outs_width // (tok_count * wide_count)
    block_index = tok_index * wide_count + wide_index
    main_part, down_part = (
        lax.psum_scatter(
            grad_main.astype(jnp.bfloat16), "tok", scatter_dimension=1, tiled=True
        ).astype(jnp.float32),
        lax.psum_scatter(
            grad_down.astype(jnp.bfloat16), "tok", scatter_dimension=1, tiled=True
        ).astype(jnp.float32),
    )
    outer_part, mag_rows = (
        lax.psum_scatter(grad_outer, ("tok", "wide"), scatter_dimension=1, tiled=True),
        lax.psum_scatter(mag_grad[None, :], ("tok", "wide"), scatter_dimension=1, tiled=True),
    )
    mag_part = mag_rows[0]
    local_squares = (
        squared_sum(main_part)
        + squared_sum(down_part)
        + squared_sum(outer_part)
        + squared_sum(mag_part)
    )
    grad_total = lax.psum(local_squares, ("tok", "wide"))
    grad_norm = jnp.sqrt(grad_total)
    clip_factor = CLIP_MAX / jnp.maximum(grad_norm, CLIP_MAX)
    main_param = lax.dynamic_slice_in_dim(adapt_main, tok_index * main_cols, main_cols, 1)
    down_param = lax.dynamic_slice_in_dim(adapt_down, tok_index * down_cols, down_cols, 1)
    outer_param = lax.dynamic_slice_in_dim(adapt_outer, block_index * outer_share, outer_share, 1)
    mag_param = lax.dynamic_slice_in_dim(magnitudes, block_index * outer_share, outer_share, 0)
    main_new, main_first_new, main_second_new = adam(
        main_param, main_part, main_first, main_second, RATE_ADAPT, clip_factor
    )
    down_new, down_first_new, down_second_new = adam(
        down_param, down_part, down_first, down_second, RATE_ADAPT, clip_factor
    )
    outer_new, outer_first_new, outer_second_new = adam(
        outer_param, outer_part, outer_first, outer_second, RATE_OUTER, clip_factor
    )
    mag_new, mag_first_new, mag_second_new = adam(
        mag_param, mag_part, mag_first, mag_second, RATE_MAGNITUDE, clip_factor
    )
    mag_clipped = mag_part * clip_factor
    return (
        layer_out,
        grad_tokens,
        grad_norm,
        main_new,
        main_first_new,
        main_second_new,
        down_new,
        down_first_new,
        down_second_new,
        outer_new,
        outer_first_new,
        outer_second_new,
        mag_new,
        mag_clipped,
        mag_second_new,
    )


def solution(mesh):
    return jax.shard_map(
        shards,
        mesh=mesh,
        in_specs=(
            P("tok", "wide"),
            P("tok", "wide"),
            P("wide"),
            P("wide"),
            P("wide", None),
            P("wide", None),
            P("wide", None),
            P("wide", None),
            P("wide", None),
            P("wide", None),
            P("wide", None),
            P("wide", None),
            P("wide", None),
            P(),
            P(),
            P("wide", "tok"),
            P("wide", "tok"),
            P("wide", "tok"),
            P("wide", "tok"),
            P(None, ("tok", "wide")),
            P(None, ("tok", "wide")),
            P(("tok", "wide")),
            P(("tok", "wide")),
            P("tok", None),
        ),
        out_specs=(
            P("tok", "wide"),
            P("tok", "wide"),
            P(),
            P("wide", "tok"),
            P("wide", "tok"),
            P("wide", "tok"),
            P("wide", "tok"),
            P("wide", "tok"),
            P("wide", "tok"),
            P(None, ("tok", "wide")),
            P(None, ("tok", "wide")),
            P(None, ("tok", "wide")),
            P(("tok", "wide")),
            P(("tok", "wide")),
            P(("tok", "wide")),
        ),
        check_vma=False,
    )
```

profile of v0, /device:TPU:0, one launch (start us, length us, event | category | flops | bytes accessed | tf_op | source)
XLA Modules:
  0.0 4038.7 jit_solution(10129928691143130938)
XLA Ops:
  9.0 23.4 psum.77
  97.9 130.0 %all-reduce.6.cloned.1.call-done = (f32[17920]{0:T(1024)}, f32[2048,256]{0,1:T(8,128)}, f32[2048,256]{0,1:T(8,128)}) async-done(((f32[17920]{0:T(1024)}, f32[2048,256]{0,1:T(8,128)}, f32[2048,256]{0,1:T(8,128)}), (f32[17920]{0:T(1024)}, f32[2048,256]{0,1:T(8,128)}, f32[2048,256]{0,1:T(8,128)})) %all-reduce.6.cloned.1.call-update) | async-done | bytes 4266000 | tf_op jit(solution)/shard_map/psum | solution.py:188
  231.4 281.9 %reduce-scatter.13.cloned.1.call-done = f32[2048,256]{0,1:T(8,128)} async-done(((f32[2048,2048]{0,1:T(8,128)}), f32[2048,256]{0,1:T(8,128)}) %reduce-scatter.13.cloned.1.call-update) | async-done | bytes 2097168 | tf_op jit(solution)/shard_map/reduce_scatter | solution.py:216
  516.1 23.7 fusion.290
  539.9 21.2 fusion.3
  561.1 23.8 fusion.65
  606.9 276.8 %reduce-scatter.15.cloned.1.call-done = f32[2048,256]{0,1:T(8,128)} async-done(((f32[2048,2048]{0,1:T(8,128)}), f32[2048,256]{0,1:T(8,128)}) %reduce-scatter.15.cloned.1.call-update) | async-done | bytes 2097168 | tf_op jit(solution)/shard_map/reduce_scatter | solution.py:216
  887.3 20.4 psum.81
  909.8 23.2 fusion.276
  933.0 25.9 add_convert_fusion
  959.3 23.4 fusion.273
  982.7 23.6 add_convert_fusion.1
  1024.5 360.9 %reduce-scatter.19.cloned.1.call-done = bf16[2048,704]{0,1:T(8,128)(2,1)} async-done(((bf16[2048,5632]{0,1:T(8,128)(2,1)}), bf16[2048,704]{0,1:T(8,128)(2,1)}) %reduce-scatter.19.cloned.1.call-update) | async-done | bytes 2883600 | tf_op jit(solution)/shard_map/reduce_scatter | solution.py:278
  1385.4 376.5 %reduce-scatter.17.cloned.1.call-done = bf16[2048,704]{0,1:T(8,128)(2,1)} async-done(((bf16[2048,5632]{0,1:T(8,128)(2,1)}), bf16[2048,704]{0,1:T(8,128)(2,1)}) %reduce-scatter.17.cloned.1.call-update) | async-done | bytes 2883600 | tf_op jit(solution)/shard_map/reduce_scatter | solution.py:272
  1806.2 410.9 %all-gather.10.cloned.1.call-done = bf16[2048,5632]{0,1:T(8,128)(2,1)} async-done(((bf16[2048,704]{0,1:T(8,128)(2,1)}), bf16[2048,5632]{0,1:T(8,128)(2,1)}) %all-gather.10.cloned.1.call-update) | async-done | bytes 23068688 | tf_op jit(solution)/shard_map/all_gather | solution.py:330
  2244.9 414.9 %all-gather.8.cloned.1.call-done = bf16[2048,5632]{0,1:T(8,128)(2,1)} async-done(((bf16[2048,704]{0,1:T(8,128)(2,1)}), bf16[2048,5632]{0,1:T(8,128)(2,1)}) %all-gather.8.cloned.1.call-update) | async-done | bytes 23068688 | tf_op jit(solution)/shard_map/all_gather | solution.py:327
  2689.1 21.8 psum.82
  2710.9 236.0 %reduce-scatter.21.cloned.1.call-done = f32[2048,256]{0,1:T(8,128)} async-done(((f32[2048,2048]{0,1:T(8,128)}), f32[2048,256]{0,1:T(8,128)}) %reduce-scatter.21.cloned.1.call-update) | async-done | bytes 2097168 | tf_op jit(solution)/shard_map/reduce_scatter | solution.py:216
  2955.6 124.0 %all-gather.12.cloned.1.call-done = bf16[2048,2048]{0,1:T(8,128)(2,1)} async-done(((bf16[2048,256]{0,1:T(8,128)(2,1)}), bf16[2048,2048]{0,1:T(8,128)(2,1)}) %all-gather.12.cloned.1.call-update) | async-done | bytes 8388624 | tf_op jit(solution)/shard_map/all_gather | solution.py:219
  3089.4 43.7 %fusion = (f32[4,2048]{1,0:T(4,128)S(1)}, f32[2048,2048,4]{1,0,2:T(8,128)}) fusion(f32[4,2048,2048]{1,2,0:T(8,128)} %get-tuple-element.108, f32[4,2048]{1,0:T(4,128)S(1)} %log_add_fusion, bf16[2048,4,64]{0,2,1:T(8,128)(2,1)S(1)} %bitcast.204, f32[2048,256]{0,1:T(8,128)S(1)} %copy-done.39, s32[]{:T(128)S(6)} %select_n.52, f32[64]{0:T(128)S(1)} %copy-done.135), kind=kOutput, calls=%fused_computation.2 | convolution fusion | flops 2198069248 | bytes 135856640 | tf_op jit(solution)/shard_map/thd,sd->hts/dot_general | solution.py:358
  3133.1 53.4 %fusion.2 = bf16[4,2048,2048]{1,2,0:T(8,128)(2,1)} fusion(f32[2048,2048,4]{1,0,2:T(8,128)} %get-tuple-element.112, f32[4,2048,2048]{1,2,0:T(8,128)} %get-tuple-element.108, f32[4,2048]{1,0:T(4,128)S(1)} %get-tuple-element.111, f32[4,2048]{1,0:T(4,128)S(1)} %log_add_fusion), kind=kLoop, calls=%fused_computation.4 | loop fusion | flops 67108864 | bytes 167837696 | tf_op jit(solution)/shard_map/convert_element_type | solution.py:362
  3186.5 16.5 fusion.73
  3203.1 13.6 fusion.53
  3216.9 23.2 fusion.69
  3248.8 34.4 psum.86
  3311.4 13.7 fusion.298
  3389.9 100.9 %reduce-scatter.27.cloned.1.call-done = f32[560,1]{1,0:T(8,128)} async-done(((f32[17920,1]{1,0:T(8,128)}), f32[560,1]{1,0:T(8,128)}) %reduce-scatter.27.cloned.1.call-update) | async-done | bytes 2256
  3492.6 103.6 %all-reduce.8.cloned.1.call-done = (bf16[2048,256]{0,1:T(8,128)(2,1)}, bf16[2048,256]{0,1:T(8,128)(2,1)}) async-done(((bf16[2048,256]{0,1:T(8,128)(2,1)}, bf16[2048,256]{0,1:T(8,128)(2,1)}), (bf16[2048,256]{0,1:T(8,128)(2,1)}, bf16[2048,256]{0,1:T(8,128)(2,1)})) %all-reduce.8.cloned.1.call-update) | async-done | bytes 2097168 | tf_op jit(solution)/shard_map/psum | solution.py:391
  3608.3 115.0 %all-gather.14.cloned.1.call-done = bf16[2048,2048]{0,1:T(8,128)(2,1)} async-done(((bf16[2048,256]{0,1:T(8,128)(2,1)}), bf16[2048,2048]{0,1:T(8,128)(2,1)}) %all-gather.14.cloned.1.call-update) | async-done | bytes 8388624 | tf_op jit(solution)/shard_map/all_gather | solution.py:219
  3795.0 19.1 psum.85
  3820.9 160.3 %reduce-scatter.25.cloned.1.call-done = f32[560,16]{1,0:T(8,128)} async-done(((f32[17920,16]{1,0:T(8,128)}), f32[560,16]{1,0:T(8,128)}) %reduce-scatter.25.cloned.1.call-update) | async-done | bytes 35856
  3986.4 39.5 psum.87
  (476 shorter events, 438.0 us)
Async XLA Ops:
  7.2 220.7 %all-reduce.6.cloned.1.call-start = ((), (), s32[]{:S(2)}) async-start(), calls=%async_computation.21 | async-start | bytes 8536064 | tf_op jit(solution)/shard_map/psum | solution.py:188
  71.6 441.7 %reduce-scatter.13.cloned.1.call-start = ((), (), s32[]{:S(2)}) async-start(), calls=%async_computation.8 | async-start | bytes 18874368 | tf_op jit(solution)/shard_map/reduce_scatter | solution.py:216
  88.9 794.8 %reduce-scatter.15.cloned.1.call-start = ((), (), s32[]{:S(2)}) async-start(), calls=%async_computation.9 | async-start | bytes 18874368 | tf_op jit(solution)/shard_map/reduce_scatter | solution.py:216
  92.4 422.9 %copy-start.46 = (f32[2048,32]{0,1:T(8,128)}, f32[2048,32]{0,1:T(8,128)S(1)}, u32[]{:S(2)}) copy-start(f32[2048,32]{0,1:T(8,128)S(1)} %get-tuple-element.91) | copy-start | bytes 786436
  92.4 422.9 %copy-start.48 = (f32[2048,32]{0,1:T(8,128)}, f32[2048,32]{0,1:T(8,128)S(1)}, u32[]{:S(2)}) copy-start(f32[2048,32]{0,1:T(8,128)S(1)} %get-tuple-element.92) | copy-start | bytes 786436
  228.8 286.5 %copy-start.80 = (f32[17920]{0:T(1024)}, f32[17920]{0:T(1024)S(1)}, u32[]{:S(2)}) copy-start(f32[17920]{0:T(1024)S(1)} %sqrt_divide_fusion.1) | copy-start | bytes 215044
  228.9 286.4 %copy-start.110 = (f32[256]{0:T(256)}, f32[256]{0:T(256)S(1)}, u32[]{:S(2)}) copy-start(f32[256]{0:T(256)S(1)} %get-tuple-element.86) | copy-start | bytes 3076
  228.9 286.4 %copy-start.124 = (f32[256]{0:T(256)}, f32[256]{0:T(256)S(1)}, u32[]{:S(2)}) copy-start(f32[256]{0:T(256)S(1)} %get-tuple-element.87) | copy-start | bytes 3076
  228.9 286.4 %copy-start.126 = (f32[256]{0:T(256)}, f32[256]{0:T(256)S(1)}, u32[]{:S(2)}) copy-start(f32[256]{0:T(256)S(1)} %get-tuple-element.88) | copy-start | bytes 3076
  228.9 375.4 %copy-start.112 = (f32[256]{0:T(256)}, f32[256]{0:T(256)S(1)}, u32[]{:S(2)}) copy-start(f32[256]{0:T(256)S(1)} %get-tuple-element.84) | copy-start | bytes 3076
  228.9 654.8 %copy-start.118 = (f32[256]{0:T(256)}, f32[256]{0:T(256)S(1)}, u32[]{:S(2)}) copy-start(f32[256]{0:T(256)S(1)} %get-tuple-element.85) | copy-start | bytes 3076
  229.0 332.1 %copy-start.134 = (f32[64]{0:T(128)}, f32[64]{0:T(128)S(1)}, u32[]{:S(2)}) copy-start(f32[64]{0:T(128)S(1)} %dynamic-slice.2) | copy-start | bytes 772
  231.4 284.2 %copy-start.64 = (bf16[2048,1,32]{0,2,1:T(8,128)(2,1)}, bf16[2048,1,32]{0,2,1:T(8,128)(2,1)S(1)}, u32[]{:S(2)}) copy-start(bf16[2048,1,32]{0,2,1:T(8,128)(2,1)S(1)} %get-tuple-element.73) | copy-start | bytes 393220
  231.4 284.2 %copy-start.66 = (bf16[2048,1,32]{0,2,1:T(8,128)(2,1)}, bf16[2048,1,32]{0,2,1:T(8,128)(2,1)S(1)}, u32[]{:S(2)}) copy-start(bf16[2048,1,32]{0,2,1:T(8,128)(2,1)S(1)} %get-tuple-element.74) | copy-start | bytes 393220
  601.7 408.2 %all-gather.6.cloned.1.call-start = ((), (), s32[]{:S(2)}) async-start(), calls=%async_computation.13 | async-start | bytes 9437184 | tf_op jit(solution)/shard_map/all_gather | solution.py:219
  604.3 279.4 %copy-start.5 = (bf16[2048,256]{0,1:T(8,128)(2,1)S(1)}, bf16[2048,256]{0,1:T(8,128)(2,1)}, u32[]{:S(2)}) copy-start(bf16[2048,256]{0,1:T(8,128)(2,1)} %copy-done.4) | copy-start | bytes 3145732
  606.8 778.6 %reduce-scatter.19.cloned.1.call-start = ((), (), s32[]{:S(2)}) async-start(), calls=%async_computation.11 | async-start | bytes 25952256 | tf_op jit(solution)/shard_map/reduce_scatter | solution.py:278
  959.0 803.0 %reduce-scatter.17.cloned.1.call-start = ((), (), s32[]{:S(2)}) async-start(), calls=%async_computation.10 | async-start | bytes 25952256 | tf_op jit(solution)/shard_map/reduce_scatter | solution.py:272
  1006.3 1210.9 %all-gather.10.cloned.1.call-start = ((), (), s32[]{:S(2)}) async-start(), calls=%async_computation.15 | async-start | bytes 25952256 | tf_op jit(solution)/shard_map/all_gather | solution.py:330
  1016.5 745.4 %copy-start.62 = (f32[704,16]{0,1:T(8,128)S(1)}, f32[704,16]{0,1:T(8,128)}, u32[]{:S(2)}) copy-start(f32[704,16]{0,1:T(8,128)} %param.36) | copy-start | bytes 135172
  1776.7 883.1 %all-gather.8.cloned.1.call-start = ((), (), s32[]{:S(2)}) async-start(), calls=%async_computation.14 | async-start | bytes 25952256 | tf_op jit(solution)/shard_map/all_gather | solution.py:327
  1781.4 1165.5 %reduce-scatter.21.cloned.1.call-start = ((), (), s32[]{:S(2)}) async-start(), calls=%async_computation.12 | async-start | bytes 18874368 | tf_op jit(solution)/shard_map/reduce_scatter | solution.py:216
  1805.7 1273.9 %all-gather.12.cloned.1.call-start = ((), (), s32[]{:S(2)}) async-start(), calls=%async_computation.16 | async-start | bytes 9437184 | tf_op jit(solution)/shard_map/all_gather | solution.py:219
  2683.3 263.5 %copy-start.24 = (bf16[2048,256]{0,1:T(8,128)(2,1)S(1)}, bf16[2048,256]{0,1:T(8,128)(2,1)}, u32[]{:S(2)}) copy-start(bf16[2048,256]{0,1:T(8,128)(2,1)} %copy.118) | copy-start | bytes 3145732
  2683.3 263.5 %copy-start.92 = (f32[2048]{0:T(1024)S(1)}, f32[2048]{0:T(1024)}, u32[]{:S(2)}) copy-start(f32[2048]{0:T(1024)} %copy-done.91) | copy-start | bytes 24580
  2683.3 263.5 %copy-start.113 = (f32[256]{0:T(256)S(1)}, f32[256]{0:T(256)}, u32[]{:S(2)}) copy-start(f32[256]{0:T(256)} %copy-done.112) | copy-start | bytes 3076
  2955.5 535.4 %reduce-scatter.27.cloned.1.call-start = ((), (), s32[]{:S(2)}) async-start(), calls=%async_computation.20 | async-start | bytes 9461760
  3292.0 304.2 %all-reduce.8.cloned.1.call-start = ((), (), s32[]{:S(2)}) async-start(), calls=%async_computation.22 | async-start | bytes 4194304 | tf_op jit(solution)/shard_map/psum | solution.py:391
  3292.6 430.7 %all-gather.14.cloned.1.call-start = ((), (), s32[]{:S(2)}) async-start(), calls=%async_computation.17 | async-start | bytes 9437184 | tf_op jit(solution)/shard_map/all_gather | solution.py:219
  3293.3 524.8 %reduce-scatter.23.cloned.1.call-start = ((), (), s32[]{:S(2)}) async-start(), calls=%async_computation.18 | async-start | bytes 61440 | tf_op jit(solution)/shard_map/reduce_scatter | solution.py:464
  3750.5 230.6 %reduce-scatter.25.cloned.1.call-start = ((), (), s32[]{:S(2)}) async-start(), calls=%async_computation.19 | async-start | bytes 9461760
  3818.1 212.0 %copy-start.103 = (f32[256,24]{0,1:T(8,128)S(1)}, f32[256,24]{0,1:T(8,128)}, u32[]{:S(2)}) copy-start(f32[256,24]{0,1:T(8,128)} %param.39) | copy-start | bytes 73732
  (124 other events, 3796.9 us)
Sparse Core Ops, SparseCore 0:
  71.7 156.0 all-reduce.5
  231.6 281.6 reduce-scatter.12
  601.8 281.7 reduce-scatter.14
  885.6 124.2 all-gather.5
  1013.6 371.7 reduce-scatter.18
  1389.2 372.7 reduce-scatter.16
  1776.8 440.2 all-gather.9
  2218.7 441.0 all-gather.7
  2663.6 283.2 reduce-scatter.20
  2955.6 123.9 all-gather.11
  3292.1 198.7 reduce-scatter.26
  3494.9 101.3 all-reduce.7
  3598.6 124.6 all-gather.13
  3750.7 17.5 reduce-scatter.22
  3781.5 199.6 reduce-scatter.24
where the time goes:
time: 4050 us; the launch traced here: 4040 us
  waiting for transfers between devices  3100 us (77%)
  matrix products  570 us (14%)
  blocking collectives  170 us (4%)
  other arithmetic  126 us (3%)
  local copies, waits for them, and re-layouts  53.4 us (1%)
    reduce_scatter x3, waiting for transfers between devices, spread(): lax.psum_scatter(partial_sum, 'wide', scatter_dimension=1, tiled=True)  795 us
    all_gather x1, waiting for transfers between devices, shards(): lax.all_gather((grad_gate_act * own_scales[4]).astype(jnp.bfloat16), 'wid...  415 us
    all_gather x1, waiting for transfers between devices, shards(): lax.all_gather((grad_up_act * own_scales[5]).astype(jnp.bfloat16), 'wide'...  411 us
    reduce_scatter x1, waiting for transfers between devices, shards(): lax.psum_scatter(dora_partial(normed_two, w_gate, adapters[4], outers[4])...  376 us
    reduce_scatter x1, waiting for transfers between devices, shards(): lax.psum_scatter(dora_partial(normed_two, w_up, adapters[5], outers[5]).a...  361 us
    unnamed x17, waiting for transfers between devices  263 us
    all_gather x3, waiting for transfers between devices, collect(): return lax.all_gather(grad_low, 'wide', axis=1, tiled=True)  242 us
    psum x1, waiting for transfers between devices, shards(): col_norms = jnp.sqrt(lax.psum(partial_norms, 'wide'))  130 us
  transfers between devices with their start and end apart: 15, of which 14 were waited for; matrix products, arithmetic and copies ran while one was open for 9% of the time, Pallas kernels for 0%

commit v1 on v0

v1 whole, which is shorter than its diff:
```python
import jax
import jax.numpy as jnp
from jax import lax
from jax.sharding import PartitionSpec as P

D = 2048
HEADS = 32
HD = 64
KVH = 4
FF = 5632
STEP = 10
RANK = 16
CHUNKS = 8
EXTRA = 128

EPS_NORM = 1e-05
ROPE_BASE = 10000.0
CLIP_MAX = 1.0
BETA_FIRST = 0.9
BETA_SECOND = 0.999
ADAM_EPS = 1e-08
WEIGHT_DECAY = 0.01
RATE_ADAPT = 0.02
RATE_OUTER = 0.05
RATE_MAGNITUDE = 0.4
PRECISE = lax.Precision.HIGHEST
MASKED = -1e30
BF = jnp.bfloat16
F32 = jnp.float32
WIDTHS = [D, KVH * HD, KVH * HD, D, FF, FF, D]
STARTS = [sum(WIDTHS[:number]) for number in range(7)]
OUTS = sum(WIDTHS)


def bits_of(count):
    return [1 << place for place in range(count.bit_length() - 1)]


def swap(array, axis, distance):
    count = lax.axis_size(axis)
    return lax.ppermute(array, axis, [(i, i ^ distance) for i in range(count)])


def mm(left, right):
    return jnp.dot(left, right, preferred_element_type=F32)


def mm_t(left, right):
    return lax.dot_general(left, right, (((1,), (1,)), ((), ())), preferred_element_type=F32)


def t_mm(left, right):
    return lax.dot_general(left, right, (((0,), (0,)), ((), ())), preferred_element_type=F32)


def two_parts(values):
    high = lax.reduce_precision(values, 8, 7)
    return high.astype(BF), (values - high).astype(BF)


def fold_parts(stacked, count):
    return stacked[:count] + stacked[count : 2 * count]


def adam(param, grad, first, second, rate, clip_factor):
    clipped = grad * clip_factor
    first_new = BETA_FIRST * first + (1.0 - BETA_FIRST) * clipped
    second_new = BETA_SECOND * second + (1.0 - BETA_SECOND) * clipped * clipped
    first_hat = first_new / (1.0 - BETA_FIRST**STEP)
    second_hat = second_new / (1.0 - BETA_SECOND**STEP)
    param_new = param - rate * (
        first_hat / (jnp.sqrt(second_hat) + ADAM_EPS) + WEIGHT_DECAY * param
    )
    return (param_new, first_new, second_new)


def squared_sum(values):
    return jnp.sum(values * values)


def all_sum(values, axes):
    for axis in axes:
        for bit in bits_of(lax.axis_size(axis)):
            values = values + swap(values, axis, bit)
    return values


def all_blocks(block, axis):
    stacked = block[None]
    index = lax.axis_index(axis)
    for bit in bits_of(lax.axis_size(axis)):
        upper = (index // bit) % 2 == 1
        received = swap(stacked, axis, bit)
        stacked = jnp.concatenate(
            [jnp.where(upper, received, stacked), jnp.where(upper, stacked, received)]
        )
    return stacked


def scatter_sum(blocks, axis, wire=F32):
    index = lax.axis_index(axis)
    for bit in reversed(bits_of(lax.axis_size(axis))):
        halves = blocks.reshape((2, bit) + blocks.shape[1:])
        side = (index // bit) % 2
        keep = lax.dynamic_index_in_dim(halves, side, 0, keepdims=False)
        send = lax.dynamic_index_in_dim(halves, 1 - side, 0, keepdims=False)
        blocks = keep + swap(send.astype(wire), axis, bit).astype(blocks.dtype)
    return blocks[0]


def gather_rows(shard, extra):
    count = lax.axis_size("wide")
    index = lax.axis_index("wide")
    rows = shard.shape[0]
    slots = {0: shard}
    for slot in range(1, count):
        low = slot & -slot
        slots[slot] = swap(slots[slot ^ low], "wide", low)
    whole = jnp.zeros((count * rows + extra.shape[0], shard.shape[1]), shard.dtype)
    whole = lax.dynamic_update_slice(whole, extra, (count * rows, 0))
    for slot, held in slots.items():
        whole = lax.dynamic_update_slice(whole, held, ((index ^ slot) * rows, 0))
    return whole


def rotate_half(values):
    half = HD // 2
    return jnp.concatenate([-values[..., half:], values[..., :half]], axis=-1)


def turn(values, cosine, sine):
    shaped = values.reshape(values.shape[0], -1, HD)
    turned = shaped * cosine[:, None, :] + rotate_half(shaped) * sine[:, None, :]
    return turned.reshape(values.shape)


def pad_rows(rows, count):
    return jnp.concatenate([rows, jnp.zeros((count - rows.shape[0], rows.shape[1]), rows.dtype)])


def extended(inputs, reduced):
    high, low = two_parts(reduced)
    parts = jnp.concatenate(
        [inputs, high, low, jnp.zeros((inputs.shape[0], EXTRA - 2 * reduced.shape[1]), BF)], axis=1
    )
    return parts


def block_rows(blocks):
    total = sum(block.shape[1] for block in blocks)
    rows = []
    start = 0
    for block in blocks:
        rows.append(jnp.pad(block, ((0, 0), (start, total - start - block.shape[1]))))
        start = start + block.shape[1]
    return jnp.concatenate(rows)


def extra_rows(outer_blocks):
    doubled = block_rows([2.0 * block.astype(BF) for block in outer_blocks]).astype(BF)
    return pad_rows(jnp.concatenate([doubled, doubled]), EXTRA)


def stacked_back(grad_low, weighted, weights):
    high, low = two_parts(weighted)
    return mm_t(jnp.concatenate([grad_low, high, low]), weights)


def attend(queries, keys, values, places, starts):
    count = queries.shape[0]
    grouped = queries.reshape(count, KVH, HEADS // KVH, HD)
    keys = keys.reshape(-1, KVH, HD)
    values = values.reshape(-1, KVH, HD)
    spots = jnp.arange(keys.shape[0], dtype=jnp.int32)
    allowed = (spots[None, :] <= places[:, None]) & (spots[None, :] >= starts[:, None])
    scores = jnp.einsum("tkgd,skd->kgts", grouped, keys, preferred_element_type=F32) * HD**-0.5
    scores = jnp.where(allowed[None, None], scores, MASKED)
    peak = jnp.max(scores, axis=-1, keepdims=True)
    powers = jnp.exp(scores - peak)
    total = jnp.sum(powers, axis=-1, keepdims=True)
    mixed = jnp.einsum(
        "kgts,skd->tkgd", (powers / total).astype(BF), values, preferred_element_type=F32
    )
    return mixed.reshape(count, HEADS * HD).astype(BF), peak + jnp.log(total)


def attend_back(queries, keys, values, places, starts, log_total, attended, grad_mixed):
    count = queries.shape[0]
    grouped = queries.reshape(count, KVH, HEADS // KVH, HD)
    grads = grad_mixed.reshape(count, KVH, HEADS // KVH, HD)
    keys = keys.reshape(-1, KVH, HD)
    values = values.reshape(-1, KVH, HD)
    spots = jnp.arange(keys.shape[0], dtype=jnp.int32)
    allowed = (spots[None, :] <= places[:, None]) & (spots[None, :] >= starts[:, None])
    scores = jnp.einsum("tkgd,skd->kgts", grouped, keys, preferred_element_type=F32) * HD**-0.5
    weights = jnp.where(allowed[None, None], jnp.exp(scores - log_total), 0.0)
    grad_weights = jnp.einsum("tkgd,skd->kgts", grads, values, preferred_element_type=F32)
    inner = jnp.sum(weights * grad_weights, axis=-1, keepdims=True)
    grad_scores = (weights * (grad_weights - inner)).astype(BF)
    grad_queries = jnp.einsum("kgts,skd->tkgd", grad_scores, keys, preferred_element_type=F32)
    grad_keys = jnp.einsum("kgts,tkgd->skd", grad_scores, grouped, preferred_element_type=F32)
    grad_values = jnp.einsum(
        "kgts,tkgd->skd", weights.astype(BF), grads, preferred_element_type=F32
    )
    return (
        grad_queries.reshape(count, HEADS * HD) * HD**-0.5,
        grad_keys.reshape(-1, KVH * HD) * HD**-0.5,
        grad_values.reshape(-1, KVH * HD),
    )


def shards(
    tokens,
    cotangent,
    gain_attn,
    gain_ffn,
    w_query,
    w_key,
    w_value,
    w_output,
    w_gate,
    w_up,
    w_down,
    adapt_main,
    adapt_down,
    adapt_outer,
    magnitudes,
    main_first,
    main_second,
    down_first,
    down_second,
    outer_first,
    outer_second,
    mag_first,
    mag_second,
    segments,
):
    wide_count = lax.axis_size("wide")
    tok_count = lax.axis_size("tok")
    wide = lax.axis_index("wide")
    tok = lax.axis_index("tok")
    core = tok % 2
    length, share = tokens.shape
    hidden_share = w_down.shape[0]
    part = hidden_share // 4
    block = length // (wide_count * CHUNKS)
    count = CHUNKS * block
    block_cols = wide_count * part

    def partner(array):
        return swap(array, "tok", 2)

    def other_core(array):
        return swap(array, "tok", 1)

    def to_tokens(features):
        pieces = features.reshape(CHUNKS, wide_count, block, share)
        whole = jnp.zeros((count, D), features.dtype)
        for slot in range(wide_count):
            piece = lax.dynamic_index_in_dim(pieces, wide ^ slot, 1, keepdims=False)
            piece = piece.reshape(count, share)
            if slot:
                piece = swap(piece, "wide", slot)
            whole = lax.dynamic_update_slice(whole, piece, (0, (wide ^ slot) * share))
        return whole

    def from_tokens(rows):
        whole = jnp.zeros((CHUNKS, wide_count, block, share), rows.dtype)
        for slot in range(wide_count):
            piece = lax.dynamic_slice(rows, (0, (wide ^ slot) * share), (count, share))
            if slot:
                piece = swap(piece, "wide", slot)
            piece = piece.reshape(CHUNKS, 1, block, share)
            whole = lax.dynamic_update_slice(whole, piece, (0, wide ^ slot, 0, 0))
        return whole.reshape(length, share)

    residual = to_tokens(tokens).astype(F32)
    gains = all_blocks(jnp.stack([gain_attn, gain_ffn]), "wide")
    gains = jnp.swapaxes(gains, 0, 1).reshape(2, D)

    bases = [w_query, w_key, w_value, w_output, w_gate, w_up, w_down]
    own_main = [adapt_main[:, n * RANK : (n + 1) * RANK] for n in range(6)] + [adapt_down]
    outers = [adapt_outer[:, STARTS[n] : STARTS[n] + WIDTHS[n]] for n in range(7)]
    norm_parts = []
    cross_parts = []
    for n in range(7):
        cols = WIDTHS[n] // tok_count
        merged = lax.dynamic_slice_in_dim(bases[n], tok * cols, cols, 1).astype(F32) + 2.0 * jnp.dot(
            own_main[n], lax.dynamic_slice_in_dim(outers[n], tok * cols, cols, 1), precision=PRECISE
        )
        norm_parts.append(jnp.sum(merged * merged, axis=0))
        cross_parts.append(
            lax.dot_general(own_main[n], merged, (((0,), (0,)), ((), ())), precision=PRECISE)
        )

    def by_matrix(blocks):
        pieces = []
        start = 0
        for n in range(7):
            cols = WIDTHS[n] // tok_count
            piece = blocks[..., start : start + cols]
            start = start + cols
            pieces.append(jnp.moveaxis(piece, 0, -2).reshape(piece.shape[1:-1] + (WIDTHS[n],)))
        return jnp.concatenate(pieces, axis=-1)

    norm_block = all_sum(jnp.concatenate(norm_parts)[None], ["wide"])
    col_norms = jnp.sqrt(by_matrix(all_blocks(norm_block, "tok"))[0])
    scales = magnitudes / col_norms
    cross_block = all_sum(jnp.concatenate(cross_parts, axis=1), ["wide"])
    cross = by_matrix(all_blocks(cross_block, "tok"))
    norm_slope = -magnitudes / (col_norms * col_norms * col_norms)

    first_main = all_blocks(adapt_main, "wide").reshape(D, 6 * RANK)
    first_down = all_blocks(adapt_down, "wide").reshape(wide_count, 4, part, RANK)
    low_main = first_main.astype(BF)

    def columns(array, n):
        return array[..., STARTS[n] : STARTS[n] + WIDTHS[n]]

    def hidden_part(array, quarter, axis=-1):
        shape = array.shape[:-1] + (wide_count, 4, part)
        picked = lax.dynamic_index_in_dim(
            array.reshape(shape), quarter, len(shape) - 2, keepdims=False
        )
        return picked.reshape(array.shape[:-1] + (block_cols,))

    quarters = [tok % 4, (tok % 4) ^ 1]
    halves = [core, 1 - core]

    qkv_cols = WIDTHS[0] + WIDTHS[1] + WIDTHS[2]
    qkv_half = qkv_cols // 2
    out_half = D // 2
    qkv_shard = lax.dynamic_slice_in_dim(
        jnp.concatenate([w_query, w_key, w_value], axis=1), core * qkv_half, qkv_half, 1
    )
    qkv_extra = lax.dynamic_slice_in_dim(extra_rows(outers[:3]), core * qkv_half, qkv_half, 1)
    qkv_weights = [gather_rows(qkv_shard, qkv_extra)]
    qkv_weights.append(other_core(qkv_weights[0]))
    out_shard = lax.dynamic_slice_in_dim(w_output, core * out_half, out_half, 1)
    out_extra = lax.dynamic_slice_in_dim(extra_rows(outers[3:4]), core * out_half, out_half, 1)
    out_weights = [gather_rows(out_shard, out_extra)]
    out_weights.append(other_core(out_weights[0]))
    down_shard = lax.dynamic_slice_in_dim(w_down, quarters[0] * part, part, 0)
    down_weights = [gather_rows(down_shard, extra_rows(outers[6:]))]
    down_weights.append(other_core(down_weights[0]))
    mlp_shard = jnp.concatenate(
        [hidden_part(w_gate, quarters[0]), hidden_part(w_up, quarters[0])], axis=1
    )
    mlp_extra = extra_rows([hidden_part(outers[4], quarters[0]), hidden_part(outers[5], quarters[0])])
    mlp_weights = [gather_rows(mlp_shard, mlp_extra)]
    mlp_weights.append(other_core(mlp_weights[0]))

    def in_order(blocks):
        return jnp.where(
            core == 0, jnp.concatenate(blocks, axis=1), jnp.concatenate(blocks[::-1], axis=1)
        )

    def half_of(array, side):
        width = array.shape[-1] // 2
        return lax.dynamic_slice_in_dim(array, side * width, width, array.ndim - 1)

    def norm_rows(values, gain_row):
        inverse = lax.rsqrt(jnp.mean(values * values, axis=1, keepdims=True) + EPS_NORM)
        return (values * inverse * gain_row[None, :]).astype(BF), inverse

    def norm_rows_back(values, gain_row, inverse, grad_normed):
        inner = jnp.sum(values * gain_row[None, :] * grad_normed, axis=1, keepdims=True)
        return (
            grad_normed * gain_row[None, :] * inverse
            - values * (inverse * inverse * inverse * inner / D)
        )

    own_places = (
        jnp.arange(CHUNKS, dtype=jnp.int32)[:, None] * (wide_count * block)
        + wide * block
        + jnp.arange(block, dtype=jnp.int32)[None, :]
    ).reshape(count)
    segment_row = segments[0]
    own_segment = lax.dynamic_index_in_dim(
        segment_row.reshape(CHUNKS, wide_count, block), wide, 1, keepdims=False
    ).reshape(count)
    own_starts = jnp.sum(
        (segment_row[None, :] < own_segment[:, None]).astype(jnp.int32), axis=1
    )
    frequency = ROPE_BASE ** (-2.0 * jnp.arange(HD // 2, dtype=F32) / HD)
    angles = (own_places - own_starts).astype(F32)[:, None] * frequency[None, :]
    cosine = jnp.tile(jnp.cos(angles), (1, 2))
    sine = jnp.tile(jnp.sin(angles), (1, 2))

    normed_one, inverse_one = norm_rows(residual, gains[0])
    reduced_qkv = mm(normed_one, low_main[:, : 3 * RANK])
    inputs_one = extended(normed_one, reduced_qkv)
    qkv_z = in_order([mm(inputs_one, weights) for weights in qkv_weights])
    qkv = qkv_z * scales[None, :qkv_cols]
    queries = turn(qkv[:, :D], cosine, sine).astype(BF)
    keys_low = turn(qkv[:, D : D + KVH * HD], cosine, sine).astype(BF)
    values_low = qkv[:, D + KVH * HD :].astype(BF)
    both = all_blocks(jnp.concatenate([keys_low, values_low], axis=1), "wide")
    both = jnp.swapaxes(both.reshape(wide_count, CHUNKS, block, -1), 0, 1).reshape(length, -1)
    all_keys, all_values = both[:, : KVH * HD], both[:, KVH * HD :]
    attended, log_total = attend(queries, all_keys, all_values, own_places, own_starts)
    reduced_out = mm(attended, low_main[:, 3 * RANK : 4 * RANK])
    inputs_out = extended(attended, reduced_out)
    output_z = in_order([mm(inputs_out, weights) for weights in out_weights])
    hidden_one = residual + output_z * columns(scales, 3)[None, :]

    normed_own, inverse_two = norm_rows(hidden_one, gains[1])
    normed_two = jnp.concatenate([normed_own, partner(normed_own)])
    reduced_mlp = mm(normed_two, low_main[:, 4 * RANK :])
    inputs_two = extended(normed_two, reduced_mlp)
    upstream = to_tokens(cotangent).astype(F32)
    down_low = (upstream * columns(scales, 6)[None, :]).astype(BF)
    down_low = jnp.concatenate([down_low, partner(down_low)])
    low_down = [
        lax.dynamic_index_in_dim(first_down, quarter, 1, keepdims=False)
        .reshape(block_cols, RANK)
        for quarter in quarters
    ]
    mlp_scales = []
    mlp_slopes = []
    mlp_outers = []
    for quarter in quarters:
        mlp_scales.append([hidden_part(columns(scales, n), quarter) for n in (4, 5)])
        mlp_slopes.append([hidden_part(columns(norm_slope, n), quarter) for n in (4, 5)])
        mlp_outers.append([hidden_part(outers[n], quarter) for n in (4, 5)])
    hiddens = []
    reduced_down = jnp.zeros((2 * count, RANK), F32)
    kept = []
    for k in range(2):
        z = mm(inputs_two, mlp_weights[k])
        gate_z, up_z = z[:, :block_cols], z[:, block_cols:]
        gate_act = gate_z * mlp_scales[k][0][None, :]
        up_act = up_z * mlp_scales[k][1][None, :]
        hidden = (jax.nn.silu(gate_act) * up_act).astype(BF)
        hiddens.append(hidden)
        kept.append((gate_z, up_z, gate_act, up_act))
        reduced_down = reduced_down + mm(hidden, low_down[k].astype(BF))
    down_sum = mm(extended(hiddens[0], reduced_down), down_weights[0]) + mm(
        hiddens[1], down_weights[1][:block_cols]
    )
    down_z = down_sum[:count] + partner(down_sum[count:].astype(BF)).astype(F32)
    layer_out = from_tokens((hidden_one + down_z * columns(scales, 6)[None, :]).astype(BF))

    scale_down = jnp.sum(upstream * down_z, axis=0)
    narrow_mlp = jnp.zeros((2 * count, 2 * RANK), F32)
    grad_normed = jnp.zeros((2 * count, D), F32)
    first_mlp = jnp.zeros((2 * RANK, D), F32)
    mid_mlp = [jnp.zeros((RANK, RANK), F32) for _ in range(2)]
    outer_mlp = []
    scale_mlp = []
    first_down_parts = []
    reduced_mlp_parts = jnp.concatenate(two_parts(reduced_mlp), axis=1)
    for k in range(2):
        gate_z, up_z, gate_act, up_act = kept[k]
        through = mm_t(down_low, down_weights[k])
        narrow_down = through[:, block_cols : block_cols + RANK]
        narrow_parts = jnp.concatenate(two_parts(narrow_down), axis=1)
        low_twice = jnp.concatenate([low_down[k].astype(BF)] * 2, axis=1)
        grad_hidden = through[:, :block_cols] + mm_t(narrow_parts, low_twice)
        first_down_parts.append(fold_parts(t_mm(narrow_parts, hiddens[k]), RANK))
        gate_sigmoid = jax.nn.sigmoid(gate_act)
        grad_up = grad_hidden * gate_act * gate_sigmoid
        grad_gate = grad_hidden * up_act * gate_sigmoid * (1.0 + gate_act * (1.0 - gate_sigmoid))
        scale_pair = [jnp.sum(grad_gate * gate_z, axis=0), jnp.sum(grad_up * up_z, axis=0)]
        scale_mlp.append(scale_pair)
        mlp_low = jnp.concatenate(
            [
                (grad_gate * mlp_scales[k][0][None, :]).astype(BF),
                (grad_up * mlp_scales[k][1][None, :]).astype(BF),
            ],
            axis=1,
        )
        weighted = [
            (scale_pair[i] * mlp_slopes[k][i])[None, :] * mlp_outers[k][i] for i in range(2)
        ]
        back = stacked_back(mlp_low, block_rows(weighted), mlp_weights[k])
        grad_normed = grad_normed + back[: 2 * count, :D]
        narrow_mlp = narrow_mlp + back[: 2 * count, D : D + 2 * RANK]
        first_mlp = first_mlp + fold_parts(back[2 * count :, :D], 2 * RANK)
        mid_mlp = [
            mid_mlp[i]
            + lax.dot_general(
                weighted[i], mlp_outers[k][i], (((1,), (1,)), ((), ())), precision=PRECISE
            )
            for i in range(2)
        ]
        pair_grads = 2.0 * fold_parts(t_mm(reduced_mlp_parts, mlp_low), 2 * RANK)
        outer_mlp.append([pair_grads[:RANK, :block_cols], pair_grads[RANK:, block_cols:]])
    narrow_parts = jnp.concatenate(two_parts(narrow_mlp), axis=1)
    low_twice = jnp.concatenate([low_main[:, 4 * RANK :]] * 2, axis=1)
    grad_normed = grad_normed + mm_t(narrow_parts, low_twice)
    first_mlp_product = fold_parts(t_mm(narrow_parts, normed_two), 2 * RANK)
    grad_normed = grad_normed[:count] + partner(grad_normed[count:].astype(BF)).astype(F32)
    grad_mid = upstream + norm_rows_back(hidden_one, gains[1], inverse_two, grad_normed)

    def first_term(product, weight_term, middles, first_cols):
        mids = jnp.concatenate(
            [
                jnp.dot(middle, first.T, precision=PRECISE)
                for middle, first in zip(middles, first_cols)
            ]
        )
        return product + 2.0 * (weight_term + 2.0 * mids)

    def main_cols(n):
        return first_main[:, n * RANK : (n + 1) * RANK]

    first_grad_mlp = first_term(
        first_mlp_product, first_mlp, mid_mlp, [main_cols(4), main_cols(5)]
    )

    pair_down = scale_down + partner(scale_down[None])[0]
    weighted = (pair_down * columns(norm_slope, 6))[None, :] * outers[6]
    middle = lax.dot_general(weighted, outers[6], (((1,), (1,)), ((), ())), precision=PRECISE)
    weighted_parts = jnp.concatenate(two_parts(weighted))
    first_grad_down = []
    for k in range(2):
        term = fold_parts(mm_t(weighted_parts, down_weights[k])[:, :block_cols], RANK)
        first_grad_down.append(
            first_term(first_down_parts[k], term, [middle], [low_down[k]])
        )
    outer_down = 2.0 * fold_parts(
        t_mm(jnp.concatenate(two_parts(reduced_down), axis=1), down_low), RANK
    )

    scale_out = jnp.sum(grad_mid * output_z, axis=0)
    out_low = (grad_mid * columns(scales, 3)[None, :]).astype(BF)
    weighted = (scale_out * columns(norm_slope, 3))[None, :] * outers[3]
    middle = lax.dot_general(weighted, outers[3], (((1,), (1,)), ((), ())), precision=PRECISE)
    back = sum(
        stacked_back(half_of(out_low, halves[k]), half_of(weighted, halves[k]), out_weights[k])
        for k in range(2)
    )
    narrow_parts = jnp.concatenate(two_parts(back[:count, D : D + RANK]), axis=1)
    low_twice = jnp.concatenate([low_main[:, 3 * RANK : 4 * RANK]] * 2, axis=1)
    grad_mixed = (back[:count, :D] + mm_t(narrow_parts, low_twice)).astype(BF)
    first_grad_out = first_term(
        fold_parts(t_mm(narrow_parts, attended), RANK),
        fold_parts(back[count:, :D], RANK),
        [middle],
        [main_cols(3)],
    )
    outer_out = 2.0 * fold_parts(
        t_mm(jnp.concatenate(two_parts(reduced_out), axis=1), out_low), RANK
    )

    grad_queries, grad_keys, grad_values = attend_back(
        queries, all_keys, all_values, own_places, own_starts, log_total, attended, grad_mixed
    )
    partial = jnp.concatenate([grad_keys, grad_values], axis=1)
    partial = jnp.swapaxes(partial.reshape(CHUNKS, wide_count, block, -1), 0, 1)
    partial = scatter_sum(partial.reshape(wide_count, count, -1), "wide", BF)
    query_grad = turn(grad_queries, cosine, -sine)
    key_grad = turn(partial[:, : KVH * HD], cosine, -sine)
    value_grad = partial[:, KVH * HD :]
    qkv_grad = jnp.concatenate([query_grad, key_grad, value_grad], axis=1)
    scale_qkv = jnp.sum(qkv_grad * qkv_z, axis=0)
    qkv_low = (qkv_grad * scales[None, :qkv_cols]).astype(BF)
    qkv_outers = outers[:3]
    weighted = [
        (columns(scale_qkv, n) * columns(norm_slope, n))[None, :] * outers[n] for n in range(3)
    ]
    middles = [
        lax.dot_general(weighted[n], outers[n], (((1,), (1,)), ((), ())), precision=PRECISE)
        for n in range(3)
    ]
    weighted_rows = block_rows(weighted)
    back = sum(
        stacked_back(half_of(qkv_low, halves[k]), half_of(weighted_rows, halves[k]), qkv_weights[k])
        for k in range(2)
    )
    narrow_parts = jnp.concatenate(two_parts(back[:count, D : D + 3 * RANK]), axis=1)
    low_twice = jnp.concatenate([low_main[:, : 3 * RANK]] * 2, axis=1)
    grad_normed = back[:count, :D] + mm_t(narrow_parts, low_twice)
    first_grad_qkv = first_term(
        fold_parts(t_mm(narrow_parts, normed_one), 3 * RANK),
        fold_parts(back[count:, :D], 3 * RANK),
        middles,
        [main_cols(n) for n in range(3)],
    )
    all_outer = 2.0 * fold_parts(
        t_mm(jnp.concatenate(two_parts(reduced_qkv), axis=1), qkv_low), 3 * RANK
    )
    outer_qkv = [
        columns(all_outer, n)[n * RANK : (n + 1) * RANK] for n in range(3)
    ]
    grad_tokens = from_tokens(
        (grad_mid + norm_rows_back(residual, gains[0], inverse_one, grad_normed)).astype(BF)
    )

    def spread_hidden(pair):
        rows = pair[0].shape[0]
        whole = jnp.zeros((rows, wide_count, 4, part), F32)
        for quarter, values in zip(quarters, pair):
            whole = lax.dynamic_update_slice(
                whole, values.reshape(rows, wide_count, 1, part), (0, 0, quarter, 0)
            )
        return whole.reshape(rows, FF)

    main_rows = jnp.concatenate([first_grad_qkv, first_grad_out, first_grad_mlp])
    down_rows = spread_hidden(first_grad_down)
    outer_cols = jnp.concatenate(
        outer_qkv
        + [
            outer_out,
            spread_hidden([outer_mlp[k][0] for k in range(2)]),
            spread_hidden([outer_mlp[k][1] for k in range(2)]),
            outer_down,
        ],
        axis=1,
    )
    scale_all = jnp.concatenate(
        [
            scale_qkv,
            scale_out,
            spread_hidden([scale_mlp[k][0][None] for k in range(2)])[0],
            spread_hidden([scale_mlp[k][1][None] for k in range(2)])[0],
            scale_down,
        ]
    )
    outer_cols = outer_cols + 2.0 * (scale_all * norm_slope)[None, :] * cross
    outer_cols = jnp.concatenate([outer_cols, scale_all[None]])

    main_width = 6 * RANK // tok_count
    down_width = RANK // tok_count
    outer_share = OUTS // (tok_count * wide_count)

    def to_owner(rows, tok_rows, wide_cols):
        shaped = rows.reshape(tok_count, tok_rows, wide_count, wide_cols)
        summed = scatter_sum(shaped, "tok")
        return scatter_sum(jnp.swapaxes(summed, 0, 1), "wide")

    main_part = to_owner(main_rows, main_width, share).T
    down_part = to_owner(down_rows, down_width, hidden_share).T
    outer_blocks = jnp.moveaxis(
        outer_cols.reshape(RANK + 1, tok_count, wide_count, outer_share), 0, 2
    )
    outer_sum = scatter_sum(scatter_sum(outer_blocks, "tok"), "wide")
    outer_part = outer_sum[:RANK]
    block_start = (tok * wide_count + wide) * outer_share
    mag_part = outer_sum[RANK] / lax.dynamic_slice_in_dim(col_norms, block_start, outer_share)

    local_squares = (
        squared_sum(main_part)
        + squared_sum(down_part)
        + squared_sum(outer_part)
        + squared_sum(mag_part)
    )
    grad_total = all_sum(jnp.full((8, 128), local_squares), ["tok", "wide"])[0, 0]
    grad_norm = jnp.sqrt(grad_total)
    clip_factor = CLIP_MAX / jnp.maximum(grad_norm, CLIP_MAX)
    main_param = lax.dynamic_slice_in_dim(adapt_main, tok * main_width, main_width, 1)
    down_param = lax.dynamic_slice_in_dim(adapt_down, tok * down_width, down_width, 1)
    outer_param = lax.dynamic_slice_in_dim(adapt_outer, block_start, outer_share, 1)
    mag_param = lax.dynamic_slice_in_dim(magnitudes, block_start, outer_share, 0)
    main_new, main_first_new, main_second_new = adam(
        main_param, main_part, main_first, main_second, RATE_ADAPT, clip_factor
    )
    down_new, down_first_new, down_second_new = adam(
        down_param, down_part, down_first, down_second, RATE_ADAPT, clip_factor
    )
    outer_new, outer_first_new, outer_second_new = adam(
        outer_param, outer_part, outer_first, outer_second, RATE_OUTER, clip_factor
    )
    mag_new, mag_first_new, mag_second_new = adam(
        mag_param, mag_part, mag_first, mag_second, RATE_MAGNITUDE, clip_factor
    )
    mag_clipped = mag_part * clip_factor
    return (
        layer_out,
        grad_tokens,
        grad_norm,
        main_new,
        main_first_new,
        main_second_new,
        down_new,
        down_first_new,
        down_second_new,
        outer_new,
        outer_first_new,
        outer_second_new,
        mag_new,
        mag_clipped,
        mag_second_new,
    )


def solution(mesh):
    return jax.shard_map(
        shards,
        mesh=mesh,
        in_specs=(
            P("tok", "wide"),
            P("tok", "wide"),
            P("wide"),
            P("wide"),
            P("wide", None),
            P("wide", None),
            P("wide", None),
            P("wide", None),
            P("wide", None),
            P("wide", None),
            P("wide", None),
            P("wide", None),
            P("wide", None),
            P(),
            P(),
            P("wide", "tok"),
            P("wide", "tok"),
            P("wide", "tok"),
            P("wide", "tok"),
            P(None, ("tok", "wide")),
            P(None, ("tok", "wide")),
            P(("tok", "wide")),
            P(("tok", "wide")),
            P("tok", None),
        ),
        out_specs=(
            P("tok", "wide"),
            P("tok", "wide"),
            P(),
            P("wide", "tok"),
            P("wide", "tok"),
            P("wide", "tok"),
            P("wide", "tok"),
            P("wide", "tok"),
            P("wide", "tok"),
            P(None, ("tok", "wide")),
            P(None, ("tok", "wide")),
            P(None, ("tok", "wide")),
            P(("tok", "wide")),
            P(("tok", "wide")),
            P(("tok", "wide")),
        ),
        check_vma=False,
    )
```

time: 4050 us -> 1430 us (0.35)
  waiting for transfers between devices: 3100 us -> 463 us
  local copies, waits for them, and re-layouts: 53.4 us -> 306 us
  matrix products: 570 us -> 351 us
  blocking collectives: 170 us -> 0 us
  starting transfers between devices: 2.17 us -> 100 us
  other arithmetic: 126 us -> 185 us
    reduce_scatter x6 -> x0, waiting for transfers between devices: 1530 us -> none  [the longest x3 795 us: spread(): lax.psum_scatter(partial_sum, 'wide', scatter_dimension=1, tiled=True)]
    all_gather x5 -> x0, waiting for transfers between devices: 1070 us -> none  [the longest x1 415 us: shards(): lax.all_gather((grad_gate_act * own_scales[4]).astype(jnp.bfloat16), 'wid...]
    ppermute x0 -> x110, waiting for transfers between devices: none -> 463 us  [swap(): return lax.ppermute(array, axis, [(i, i ^ distance) for i in range(count)])]
    unnamed x17 -> x0, waiting for transfers between devices: 263 us -> none
    psum x2 -> x0, waiting for transfers between devices: 234 us -> none  [the longest x1 130 us: shards(): col_norms = jnp.sqrt(lax.psum(partial_norms, 'wide'))]
    dot_general x90 -> x75, matrix products: 570 us -> 351 us  [the longest x15 80.4 us: mm_t(): lax.dot_general(left, right, (((1,), (1,)), ((), ())), preferred_element_...]
    psum x6 -> x0, blocking collectives: 159 us -> none  [the longest x2 43.7 us: norm_rows(): row_total = lax.psum(jnp.sum(values * values, axis=1), 'wide')]
    dynamic_update_slice x7 -> x76, local copies, waits for them, and re-layouts: 1.38 us -> 110 us  [the longest x30 51.6 us: gather_rows(): whole = lax.dynamic_update_slice(whole, held, ((index ^ slot) * rows, 0))]
  transfers between devices with their start and end apart: 15 -> 110, of which waited for: 14 -> 62; matrix products, arithmetic and copies ran while one was open for 9% -> 39% of each run, Pallas kernels for 0% -> 0%
where the time goes in v1:
time: 1430 us; the launch traced here: 1410 us
  waiting for transfers between devices  463 us (32%)
  matrix products  351 us (25%)
  local copies, waits for them, and re-layouts  306 us (21%)
  other arithmetic  185 us (13%)
  starting transfers between devices  100 us (7%)
    ppermute x110, waiting for transfers between devices, swap(): return lax.ppermute(array, axis, [(i, i ^ distance) for i in range(count)])  463 us
    ppermute x110, starting transfers between devices, swap(): return lax.ppermute(array, axis, [(i, i ^ distance) for i in range(count)])  100 us
    dot_general x15, matrix products, mm_t(): lax.dot_general(left, right, (((1,), (1,)), ((), ())), preferred_element_...  80.4 us
    dot_general x13, matrix products, mm(): return jnp.dot(left, right, preferred_element_type=F32)  56.8 us
    convert_element_type x1, other arithmetic, attend_back(): grad_scores = (weights * (grad_weights - inner)).astype(BF)  53.5 us
    dynamic_update_slice x30, local copies, waits for them, and re-layouts, gather_rows(): whole = lax.dynamic_update_slice(whole, held, ((index ^ slot) * rows, 0))  51.6 us
    dot_general x1, matrix products, attend_back(): jnp.einsum('tkgd,skd->kgts', grads, values, preferred_element_type=F32)  46.5 us
    unnamed x516, local copies, waits for them, and re-layouts  41.5 us
  transfers between devices with their start and end apart: 110, of which 62 were waited for; matrix products, arithmetic and copies ran while one was open for 39% of the time, Pallas kernels for 0%

profile of v1, /device:TPU:0, one launch (start us, length us, event | category | flops | bytes accessed | tf_op | source)
XLA Modules:
  0.0 1414.2 jit_solution(7526779306438665878)
XLA Ops:
  168.4 7.4 collective-permute-done.3
  201.9 7.7 collective-permute-done.68
  235.8 12.9 collective-permute-done.47
  273.4 50.4 %collective-permute-done.12 = f32[4,256,96]{1,2,0:T(8,128)S(1)} collective-permute-done((f32[4,256,96]{1,2,0:T(8,128)}, f32[4,256,96]{1,2,0:T(8,128)S(1)}, u32[]{:S(2)}, u32[]{:S(2)}) %collective-permute-start.12) | collective-permute-done | bytes 393248 | tf_op jit(solution)/shard_map/ppermute | solution.py:41
  337.2 16.7 %collective-permute-done.97 = f32[16,4480]{1,0:T(8,128)S(1)} collective-permute-done((f32[16,4480]{1,0:T(8,128)S(1)}, f32[16,4480]{1,0:T(8,128)S(1)}, u32[]{:S(2)}, u32[]{:S(2)}) %collective-permute-start.97) | collective-permute-done | bytes 286752 | tf_op jit(solution)/shard_map/ppermute | solution.py:41
  357.3 7.9 collective-permute-done.33
  369.1 45.5 %collective-permute-done.15 = bf16[256,1280]{1,0:T(8,128)(2,1)S(1)} collective-permute-done((bf16[256,1280]{1,0:T(8,128)(2,1)}, bf16[256,1280]{1,0:T(8,128)(2,1)S(1)}, u32[]{:S(2)}, u32[]{:S(2)}) %collective-permute-start.15) | collective-permute-done | bytes 655392 | tf_op jit(solution)/shard_map/ppermute | solution.py:41
  417.8 6.9 collective-permute-done.17
  425.7 11.4 collective-permute-done.18
  448.0 12.5 collective-permute-done.53
  512.0 20.2 %collective-permute-done.40 = bf16[256,2816]{0,1:T(8,128)(2,1)} collective-permute-done((bf16[256,2816]{0,1:T(8,128)(2,1)}, bf16[256,2816]{0,1:T(8,128)(2,1)}, u32[]{:S(2)}, u32[]{:S(2)}) %collective-permute-start.40) | collective-permute-done | bytes 1441824 | tf_op jit(solution)/shard_map/ppermute | solution.py:41
  553.6 9.5 collective-permute-done.42
  565.7 26.5 %collective-permute-done.26 = bf16[1,256,512]{2,1,0:T(8,128)(2,1)S(1)} collective-permute-done((bf16[1,256,512]{2,1,0:T(8,128)(2,1)S(1)}, bf16[1,256,512]{2,1,0:T(8,128)(2,1)S(1)}, u32[]{:S(2)}, u32[]{:S(2)}) %collective-permute-start.26) | collective-permute-done | bytes 262176 | tf_op jit(solution)/shard_map/ppermute | solution.py:41
  618.9 37.2 %collective-permute-done.28 = bf16[4,256,512]{2,1,0:T(8,128)(2,1)} collective-permute-done((bf16[4,256,512]{2,1,0:T(8,128)(2,1)}, bf16[4,256,512]{2,1,0:T(8,128)(2,1)}, u32[]{:S(2)}, u32[]{:S(2)}) %collective-permute-start.28) | collective-permute-done | bytes 1048608 | tf_op jit(solution)/shard_map/ppermute | solution.py:41
  663.7 23.2 %fusion.5 = (f32[4,8,256]{2,1,0:T(8,128)S(1)}, f32[4,2048,256,8]{2,1,3,0:T(8,128)}) fusion(pred[256,2048]{0,1:T(8,128)(4,1)S(1)} %fusion.59, bf16[2048,4,64,1]{0,2,3,1:T(8,128)(2,1)S(1)} %bitcast.521, bf16[256,4,8,64]{0,3,2,1:T(8,128)(2,1)S(1)} %bitcast.515), kind=kOutput, calls=%fused_computation.11 | convolution fusion | flops 2197807104 | bytes 69763072 | tf_op jit(solution)/shard_map/tkgd,skd->kgts/dot_general | solution.py:176
  687.0 21.7 %fusion.6 = f32[4,8,256]{2,1,0:T(8,128)S(1)} fusion(f32[4,2048,256,8]{2,1,3,0:T(8,128)} %get-tuple-element.282, f32[4,8,256]{2,1,0:T(8,128)S(1)} %get-tuple-element.281, pred[256,2048]{0,1:T(8,128)(4,1)S(1)} %fusion.59), kind=kLoop, calls=%fused_computation.12 | loop fusion | flops 67100672 | bytes 67698688 | tf_op jit(solution)/shard_map/reduce_sum | solution.py:180
  708.7 25.7 %fusion.61 = bf16[4,64,8,256]{3,1,2,0:T(8,128)(2,1)S(1)} fusion(bf16[2048,4,64,1]{0,2,3,1:T(8,128)(2,1)S(1)} %bitcast.546, f32[4,2048,256,8]{2,1,3,0:T(8,128)} %get-tuple-element.282, f32[4,8,256]{2,1,0:T(8,128)S(1)} %fusion.6, f32[4,8,256]{2,1,0:T(8,128)S(1)} %get-tuple-element.281, pred[256,2048]{0,1:T(8,128)(4,1)S(1)} %fusion.59), kind=kOutput, calls=%fused_computation.137 | convolution fusion | flops 2231894016 | bytes 69795840 | tf_op jit(solution)/shard_map/kgts,skd->tkgd/dot_general | solution.py:181
  759.2 10.3 collective-permute-done.37
  780.1 11.2 fusion.336
  829.9 13.2 fusion.15
  843.1 10.5 fusion.338
  879.7 12.7 fusion.23
  971.3 25.5 %fusion.39 = f32[2048,4,64]{0,2,1:T(8,128)} fusion(bf16[256,4,8,64]{0,3,2,1:T(8,128)(2,1)S(1)} %bitcast.540, f32[4,2048,256,8]{2,1,3,0:T(8,128)} %get-tuple-element.282, f32[4,8,256]{2,1,0:T(8,128)S(1)} %copy-done.65, pred[256,2048]{0,1:T(8,128)(4,1)S(1)} %copy-done.1), kind=kOutput, calls=%fused_computation.77 | convolution fusion | flops 2214592512 | bytes 70811648 | tf_op jit(solution)/shard_map/kgts,tkgd->skd/dot_general | solution.py:202
  996.7 46.5 %fusion = (f32[4,8,256]{2,1,0:T(8,128)S(1)}, f32[4,2048,256,8]{2,1,3,0:T(8,128)}) fusion(f32[4,2048,256,8]{2,1,3,0:T(8,128)} %get-tuple-element.282, f32[4,8,256]{2,1,0:T(8,128)S(1)} %copy-done.65, pred[256,2048]{0,1:T(8,128)(4,1)S(1)} %copy-done.1, bf16[2048,4,64,1]{0,2,3,1:T(8,128)(2,1)S(1)} %bitcast.547, bf16[256,4,8,64]{0,3,2,1:T(8,128)(2,1)S(1)} %bitcast.541), kind=kOutput, calls=%fused_computation.2 | convolution fusion | flops 2231361536 | bytes 136904704 | tf_op jit(solution)/shard_map/tkgd,skd->kgts/dot_general | solution.py:197
  1043.3 53.5 %fusion.2 = bf16[4,8,256,2048]{2,3,1,0:T(8,128)(2,1)} fusion(f32[4,2048,256,8]{2,1,3,0:T(8,128)} %get-tuple-element.284, f32[4,2048,256,8]{2,1,3,0:T(8,128)} %get-tuple-element.282, f32[4,8,256]{2,1,0:T(8,128)S(1)} %get-tuple-element.283, f32[4,8,256]{2,1,0:T(8,128)S(1)} %copy-done.65, pred[256,2048]{0,1:T(8,128)(4,1)S(1)} %copy-done.1), kind=kLoop, calls=%fused_computation.4 | loop fusion | flops 100663296 | bytes 168361984 | tf_op jit(solution)/shard_map/convert_element_type | solution.py:199
  1096.8 15.1 %convolution_multiply_fusion.5 = f32[4,64,8,256]{3,1,2,0:T(8,128)} fusion(bf16[2048,4,64,1]{0,2,3,1:T(8,128)(2,1)S(1)} %bitcast.522, bf16[4,8,256,2048]{2,3,1,0:T(8,128)(2,1)} %fusion.2), kind=kOutput, calls=%fused_computation.135 | convolution fusion | flops 2148007936 | bytes 36700160 | tf_op jit(solution)/shard_map/kgts,skd->tkgd/dot_general | solution.py:200
  1111.8 14.9 %fusion.47 = f32[2048,4,64]{0,2,1:T(8,128)S(1)} fusion(bf16[256,4,8,64]{0,3,2,1:T(8,128)(2,1)S(1)} %bitcast.516, bf16[4,8,256,2048]{2,3,1,0:T(8,128)(2,1)} %fusion.2), kind=kOutput, calls=%fused_computation.84 | convolution fusion | flops 2148007936 | bytes 36700160 | tf_op jit(solution)/shard_map/kgts,tkgd->skd/dot_general | solution.py:201
  1177.2 27.0 %collective-permute-done.74 = bf16[4,256,512]{2,1,0:T(8,128)(2,1)} collective-permute-done((bf16[4,256,512]{2,1,0:T(8,128)(2,1)}, bf16[4,256,512]{2,1,0:T(8,128)(2,1)}, u32[]{:S(2)}, u32[]{:S(2)}) %collective-permute-start.74) | collective-permute-done | bytes 1048608 | tf_op jit(solution)/shard_map/ppermute | solution.py:41
  1217.8 7.6 collective-permute-done.60
  1231.2 6.9 collective-permute-done.62
  1342.1 9.5 collective-permute-done.86
  1357.4 12.7 collective-permute-done.102
  (1212 shorter events, 784.4 us)
Async XLA Ops:
  6.4 250.4 %collective-permute-start.30 = (bf16[256,1024]{1,0:T(8,128)(2,1)}, bf16[256,1024]{1,0:T(8,128)(2,1)}, u32[]{:S(2)}, u32[]{:S(2)}) collective-permute-start(bf16[256,1024]{1,0:T(8,128)(2,1)} %get-tuple-element.76), channel_id=1, source_target_pairs={{0,2},{1,3},{2,0},{3,1},{4,6},{5,7},{6,4},{7,5},{8,10},{9,11},{10,... | collective-permute-start | bytes 1572872 | tf_op jit(solution)/shard_map/ppermute | solution.py:41
  9.4 245.5 %collective-permute-start.29 = (bf16[256,1024]{1,0:T(8,128)(2,1)}, bf16[256,1024]{1,0:T(8,128)(2,1)}, u32[]{:S(2)}, u32[]{:S(2)}) collective-permute-start(bf16[256,1024]{1,0:T(8,128)(2,1)} %get-tuple-element.76), channel_id=1, source_target_pairs={{0,1},{1,0},{2,3},{3,2},{4,5},{5,4},{6,7},{7,6},{8,9},{9,8},{10,11... | collective-permute-start | bytes 1572872 | tf_op jit(solution)/shard_map/ppermute | solution.py:41
  11.5 102.1 %collective-permute-start.7 = (f32[1,2,256]{2,1,0:T(2,128)}, f32[1,2,256]{2,1,0:T(2,128)}, u32[]{:S(2)}, u32[]{:S(2)}) collective-permute-start(f32[1,2,256]{2,1,0:T(2,128)} %maximum_bitcast_fusion.10), channel_id=1, source_target_pairs={{0,1},{1,0},{2,3},{3,2},{4,5},{5,4},{6,7},{7,6},{8,9},{9,8},{10,11... | collective-permute-start | bytes 6152 | tf_op jit(solution)/shard_map/ppermute | solution.py:41
  12.1 126.3 %collective-permute-start.45 = (f32[1,704,16]{1,2,0:T(8,128)S(1)}, f32[1,704,16]{1,2,0:T(8,128)}, u32[]{:S(2)}, u32[]{:S(2)}) collective-permute-start(f32[1,704,16]{1,2,0:T(8,128)S(1)} %bitcast.581), channel_id=1, source_target_pairs={{0,1},{1,0},{2,3},{3,2},{4,5},{5,4},{6,7},{7,6},{8,9},{9,8},{10,11... | collective-permute-start | bytes 135176 | tf_op jit(solution)/shard_map/ppermute | solution.py:41
  13.5 131.6 %collective-permute-start.10 = (f32[1,256,96]{1,2,0:T(8,128)S(1)}, f32[1,256,96]{1,2,0:T(8,128)}, u32[]{:S(2)}, u32[]{:S(2)}) collective-permute-start(f32[1,256,96]{1,2,0:T(8,128)S(1)} %bitcast.567), channel_id=1, source_target_pairs={{0,1},{1,0},{2,3},{3,2},{4,5},{5,4},{6,7},{7,6},{8,9},{9,8},{10,11... | collective-permute-start | bytes 294920 | tf_op jit(solution)/shard_map/ppermute | solution.py:41
  136.8 92.0 %collective-permute-start.95 = (f32[16,4480]{1,0:T(8,128)S(1)}, f32[16,4480]{1,0:T(8,128)}, u32[]{:S(2)}, u32[]{:S(2)}) collective-permute-start(f32[16,4480]{1,0:T(8,128)S(1)} %concatenate.311), channel_id=1, source_target_pairs={{0,1},{1,0},{2,3},{3,2},{4,5},{5,4},{6,7},{7,6},{8,9},{9,8},{10,11... | collective-permute-start | bytes 860168 | tf_op jit(solution)/shard_map/ppermute | solution.py:41
  254.9 78.9 %collective-permute-start.32 = (bf16[256,1024]{1,0:T(8,128)(2,1)}, bf16[256,1024]{1,0:T(8,128)(2,1)}, u32[]{:S(2)}, u32[]{:S(2)}) collective-permute-start(bf16[256,1024]{1,0:T(8,128)(2,1)} %get-tuple-element.76), channel_id=1, source_target_pairs={{0,4},{1,5},{2,6},{3,7},{4,0},{5,1},{6,2},{7,3},{8,12},{9,13},{10,... | collective-permute-start | bytes 1572872 | tf_op jit(solution)/shard_map/ppermute | solution.py:41
  256.8 110.1 %collective-permute-start.16 = (bf16[256,1280]{1,0:T(8,128)(2,1)}, bf16[256,1280]{1,0:T(8,128)(2,1)}, u32[]{:S(2)}, u32[]{:S(2)}) collective-permute-start(bf16[256,1280]{1,0:T(8,128)(2,1)} %get-tuple-element.74), channel_id=1, source_target_pairs={{0,4},{1,5},{2,6},{3,7},{4,0},{5,1},{6,2},{7,3},{8,12},{9,13},{10,... | collective-permute-start | bytes 1966088 | tf_op jit(solution)/shard_map/ppermute | solution.py:41
  263.7 71.5 %collective-permute-start.50 = (bf16[176,2048]{1,0:T(8,128)(2,1)}, bf16[176,2048]{1,0:T(8,128)(2,1)}, u32[]{:S(2)}, u32[]{:S(2)}) collective-permute-start(bf16[176,2048]{1,0:T(8,128)(2,1)} %get-tuple-element.66), channel_id=1, source_target_pairs={{0,2},{1,3},{2,0},{3,1},{4,6},{5,7},{6,4},{7,5},{8,10},{9,11},{10,... | collective-permute-start | bytes 2162696 | tf_op jit(solution)/shard_map/ppermute | solution.py:41
  265.5 58.4 %collective-permute-start.12 = (f32[4,256,96]{1,2,0:T(8,128)}, f32[4,256,96]{1,2,0:T(8,128)S(1)}, u32[]{:S(2)}, u32[]{:S(2)}) collective-permute-start(f32[4,256,96]{1,2,0:T(8,128)} %pad_maximum_fusion.13), channel_id=1, source_target_pairs={{0,4},{1,5},{2,6},{3,7},{4,0},{5,1},{6,2},{7,3},{8,12},{9,13},{10,... | collective-permute-start | bytes 1179656 | tf_op jit(solution)/shard_map/ppermute | solution.py:41
  269.0 59.6 %collective-permute-start.49 = (bf16[176,2048]{1,0:T(8,128)(2,1)}, bf16[176,2048]{1,0:T(8,128)(2,1)}, u32[]{:S(2)}, u32[]{:S(2)}) collective-permute-start(bf16[176,2048]{1,0:T(8,128)(2,1)} %get-tuple-element.66), channel_id=1, source_target_pairs={{0,1},{1,0},{2,3},{3,2},{4,5},{5,4},{6,7},{7,6},{8,9},{9,8},{10,11... | collective-permute-start | bytes 2162696 | tf_op jit(solution)/shard_map/ppermute | solution.py:41
  323.9 101.8 %collective-permute-start.52 = (bf16[176,2048]{1,0:T(8,128)(2,1)}, bf16[176,2048]{1,0:T(8,128)(2,1)}, u32[]{:S(2)}, u32[]{:S(2)}) collective-permute-start(bf16[176,2048]{1,0:T(8,128)(2,1)} %get-tuple-element.66), channel_id=1, source_target_pairs={{0,4},{1,5},{2,6},{3,7},{4,0},{5,1},{6,2},{7,3},{8,12},{9,13},{10,... | collective-permute-start | bytes 2162696 | tf_op jit(solution)/shard_map/ppermute | solution.py:41
  365.2 74.1 %collective-permute-start.39 = (bf16[256,2816]{0,1:T(8,128)(2,1)S(1)}, bf16[256,2816]{0,1:T(8,128)(2,1)}, u32[]{:S(2)}, u32[]{:S(2)}) collective-permute-start(bf16[256,2816]{0,1:T(8,128)(2,1)S(1)} %copy-done.62), channel_id=1, source_target_pairs={{0,2},{1,3},{2,0},{3,1},{4,6},{5,7},{6,4},{7,5},{8,10},{9,11},{10,... | collective-permute-start | bytes 4325384 | tf_op jit(solution)/shard_map/ppermute | solution.py:41
  366.1 72.0 %collective-permute-start.38 = (bf16[256,2816]{0,1:T(8,128)(2,1)S(1)}, bf16[256,2816]{0,1:T(8,128)(2,1)S(1)}, u32[]{:S(2)}, u32[]{:S(2)}) collective-permute-start(bf16[256,2816]{0,1:T(8,128)(2,1)S(1)} %copy-done.62), channel_id=1, source_target_pairs={{0,1},{1,0},{2,3},{3,2},{4,5},{5,4},{6,7},{7,6},{8,9},{9,8},{10,11... | collective-permute-start | bytes 4325384 | tf_op jit(solution)/shard_map/ppermute | solution.py:41
  368.9 55.8 %collective-permute-start.17 = (bf16[256,1280]{1,0:T(8,128)(2,1)}, bf16[256,1280]{1,0:T(8,128)(2,1)S(1)}, u32[]{:S(2)}, u32[]{:S(2)}) collective-permute-start(bf16[256,1280]{1,0:T(8,128)(2,1)} %collective-permute-done.16), channel_id=1, source_target_pairs={{0,1},{1,0},{2,3},{3,2},{4,5},{5,4},{6,7},{7,6},{8,9},{9,8},{10,11... | collective-permute-start | bytes 1966088 | tf_op jit(solution)/shard_map/ppermute | solution.py:41
  424.8 56.1 %collective-permute-start.41 = (bf16[256,2816]{0,1:T(8,128)(2,1)S(1)}, bf16[256,2816]{0,1:T(8,128)(2,1)}, u32[]{:S(2)}, u32[]{:S(2)}) collective-permute-start(bf16[256,2816]{0,1:T(8,128)(2,1)S(1)} %copy-done.62), channel_id=1, source_target_pairs={{0,4},{1,5},{2,6},{3,7},{4,0},{5,1},{6,2},{7,3},{8,12},{9,13},{10,... | collective-permute-start | bytes 4325384 | tf_op jit(solution)/shard_map/ppermute | solution.py:41
  480.9 51.3 %collective-permute-start.40 = (bf16[256,2816]{0,1:T(8,128)(2,1)}, bf16[256,2816]{0,1:T(8,128)(2,1)}, u32[]{:S(2)}, u32[]{:S(2)}) collective-permute-start(bf16[256,2816]{0,1:T(8,128)(2,1)} %collective-permute-done.39), channel_id=1, source_target_pairs={{0,1},{1,0},{2,3},{3,2},{4,5},{5,4},{6,7},{7,6},{8,9},{9,8},{10,11... | collective-permute-start | bytes 4325384 | tf_op jit(solution)/shard_map/ppermute | solution.py:41
  487.7 49.8 %collective-permute-start.20 = (bf16[2176,1280]{1,0:T(8,128)(2,1)}, bf16[2176,1280]{1,0:T(8,128)(2,1)}, u32[]{:S(2)}, u32[]{:S(2)}) collective-permute-start(bf16[2176,1280]{1,0:T(8,128)(2,1)} %constant_dynamic-update-slice_fusion.69), channel_id=1, source_target_pairs={{0,8},{8,0},{16,24},{24,16},{1,9},{9,1},{17,25},{25,17},{2,10},{10... | collective-permute-start | bytes 16711688 | tf_op jit(solution)/shard_map/ppermute | solution.py:41
  501.3 61.8 %collective-permute-start.42 = (bf16[256,2816]{0,1:T(8,128)(2,1)}, bf16[256,2816]{0,1:T(8,128)(2,1)}, u32[]{:S(2)}, u32[]{:S(2)}) collective-permute-start(bf16[256,2816]{0,1:T(8,128)(2,1)} %collective-permute-done.41), channel_id=1, source_target_pairs={{0,1},{1,0},{2,3},{3,2},{4,5},{5,4},{6,7},{7,6},{8,9},{9,8},{10,11... | collective-permute-start | bytes 4325384 | tf_op jit(solution)/shard_map/ppermute | solution.py:41
  503.3 235.3 %collective-permute-start.36 = (bf16[2176,1024]{1,0:T(8,128)(2,1)}, bf16[2176,1024]{1,0:T(8,128)(2,1)}, u32[]{:S(2)}, u32[]{:S(2)}) collective-permute-start(bf16[2176,1024]{1,0:T(8,128)(2,1)} %constant_dynamic-update-slice_fusion.61), channel_id=1, source_target_pairs={{0,8},{8,0},{16,24},{24,16},{1,9},{9,1},{17,25},{25,17},{2,10},{10... | collective-permute-start | bytes 13369352 | tf_op jit(solution)/shard_map/ppermute | solution.py:41
  532.2 214.0 %collective-permute-start.56 = (bf16[1536,2048]{1,0:T(8,128)(2,1)}, bf16[1536,2048]{1,0:T(8,128)(2,1)}, u32[]{:S(2)}, u32[]{:S(2)}) collective-permute-start(bf16[1536,2048]{1,0:T(8,128)(2,1)} %constant_dynamic-update-slice_fusion.45), channel_id=1, source_target_pairs={{0,8},{8,0},{16,24},{24,16},{1,9},{9,1},{17,25},{25,17},{2,10},{10... | collective-permute-start | bytes 18874376 | tf_op jit(solution)/shard_map/ppermute | solution.py:41
  532.2 64.4 %collective-permute-start.44 = (bf16[256,2816]{0,1:T(8,128)(2,1)}, bf16[256,2816]{0,1:T(8,128)(2,1)}, u32[]{:S(2)}, u32[]{:S(2)}) collective-permute-start(bf16[256,2816]{0,1:T(8,128)(2,1)} %collective-permute-done.43), channel_id=1, source_target_pairs={{0,1},{1,0},{2,3},{3,2},{4,5},{5,4},{6,7},{7,6},{8,9},{9,8},{10,11... | collective-permute-start | bytes 4325384 | tf_op jit(solution)/shard_map/ppermute | solution.py:41
  599.2 243.9 %collective-permute-start.48 = (bf16[2176,2816]{0,1:T(8,128)(2,1)}, bf16[2176,2816]{0,1:T(8,128)(2,1)}, u32[]{:S(2)}, u32[]{:S(2)}) collective-permute-start(bf16[2176,2816]{0,1:T(8,128)(2,1)} %constant_dynamic-update-slice_fusion.53), channel_id=1, source_target_pairs={{0,8},{8,0},{16,24},{24,16},{1,9},{9,1},{17,25},{25,17},{2,10},{10... | collective-permute-start | bytes 36765704 | tf_op jit(solution)/shard_map/ppermute | solution.py:41
  606.9 49.3 %collective-permute-start.28 = (bf16[4,256,512]{2,1,0:T(8,128)(2,1)}, bf16[4,256,512]{2,1,0:T(8,128)(2,1)}, u32[]{:S(2)}, u32[]{:S(2)}) collective-permute-start(bf16[4,256,512]{2,1,0:T(8,128)(2,1)} %pad_maximum_fusion.6), channel_id=1, source_target_pairs={{0,4},{1,5},{2,6},{3,7},{4,0},{5,1},{6,2},{7,3},{8,12},{9,13},{10,... | collective-permute-start | bytes 3145736 | tf_op jit(solution)/shard_map/ppermute | solution.py:41
  1129.1 116.7 %collective-permute-start.89 = (f32[1,2048]{1,0:T(1,128)S(1)}, f32[1,2048]{1,0:T(1,128)S(1)}, u32[]{:S(2)}, u32[]{:S(2)}) collective-permute-start(f32[1,2048]{1,0:T(1,128)S(1)} %bitcast.622), channel_id=1, source_target_pairs={{0,16},{8,24},{16,0},{24,8},{1,17},{9,25},{17,1},{25,9},{2,18},{10... | collective-permute-start | bytes 24584 | tf_op jit(solution)/shard_map/ppermute | solution.py:41
  1130.6 108.8 %collective-permute-start.64 = (bf16[256,256]{1,0:T(8,128)(2,1)S(1)}, bf16[256,256]{1,0:T(8,128)(2,1)}, u32[]{:S(2)}, u32[]{:S(2)}) collective-permute-start(bf16[256,256]{1,0:T(8,128)(2,1)S(1)} %get-tuple-element.151), channel_id=1, source_target_pairs={{0,7},{1,6},{2,5},{3,4},{4,3},{5,2},{6,1},{7,0},{8,15},{9,14},{10,... | collective-permute-start | bytes 393224 | tf_op jit(solution)/shard_map/ppermute | solution.py:41
  1132.8 82.7 %collective-permute-start.59 = (bf16[256,256]{1,0:T(8,128)(2,1)}, bf16[256,256]{1,0:T(8,128)(2,1)}, u32[]{:S(2)}, u32[]{:S(2)}) collective-permute-start(bf16[256,256]{1,0:T(8,128)(2,1)} %get-tuple-element.156), channel_id=1, source_target_pairs={{0,2},{1,3},{2,0},{3,1},{4,6},{5,7},{6,4},{7,5},{8,10},{9,11},{10,... | collective-permute-start | bytes 393224 | tf_op jit(solution)/shard_map/ppermute | solution.py:41
  1132.8 78.8 %collective-permute-start.58 = (bf16[256,256]{1,0:T(8,128)(2,1)}, bf16[256,256]{1,0:T(8,128)(2,1)}, u32[]{:S(2)}, u32[]{:S(2)}) collective-permute-start(bf16[256,256]{1,0:T(8,128)(2,1)} %get-tuple-element.157), channel_id=1, source_target_pairs={{0,1},{1,0},{2,3},{3,2},{4,5},{5,4},{6,7},{7,6},{8,9},{9,8},{10,11... | collective-permute-start | bytes 393224 | tf_op jit(solution)/shard_map/ppermute | solution.py:41
  1305.1 96.6 %collective-permute-start.83 = (bf16[256,256]{1,0:T(8,128)(2,1)S(1)}, bf16[256,256]{1,0:T(8,128)(2,1)}, u32[]{:S(2)}, u32[]{:S(2)}) collective-permute-start(bf16[256,256]{1,0:T(8,128)(2,1)S(1)} %get-tuple-element.133), channel_id=1, source_target_pairs={{0,7},{1,6},{2,5},{3,4},{4,3},{5,2},{6,1},{7,0},{8,15},{9,14},{10,... | collective-permute-start | bytes 393224 | tf_op jit(solution)/shard_map/ppermute | solution.py:41
  1307.7 90.4 %collective-permute-start.82 = (bf16[256,256]{1,0:T(8,128)(2,1)}, bf16[256,256]{1,0:T(8,128)(2,1)}, u32[]{:S(2)}, u32[]{:S(2)}) collective-permute-start(bf16[256,256]{1,0:T(8,128)(2,1)} %get-tuple-element.134), channel_id=1, source_target_pairs={{0,6},{1,7},{2,4},{3,5},{4,2},{5,3},{6,0},{7,1},{8,14},{9,15},{10,... | collective-permute-start | bytes 393224 | tf_op jit(solution)/shard_map/ppermute | solution.py:41
  1330.8 64.1 %collective-permute-start.81 = (bf16[256,256]{1,0:T(8,128)(2,1)}, bf16[256,256]{1,0:T(8,128)(2,1)S(1)}, u32[]{:S(2)}, u32[]{:S(2)}) collective-permute-start(bf16[256,256]{1,0:T(8,128)(2,1)} %get-tuple-element.135), channel_id=1, source_target_pairs={{0,5},{1,4},{2,7},{3,6},{4,1},{5,0},{6,3},{7,2},{8,13},{9,12},{10,... | collective-permute-start | bytes 393224 | tf_op jit(solution)/shard_map/ppermute | solution.py:41
  1337.6 54.1 %collective-permute-start.80 = (bf16[256,256]{1,0:T(8,128)(2,1)}, bf16[256,256]{1,0:T(8,128)(2,1)S(1)}, u32[]{:S(2)}, u32[]{:S(2)}) collective-permute-start(bf16[256,256]{1,0:T(8,128)(2,1)} %get-tuple-element.136), channel_id=1, source_target_pairs={{0,4},{1,5},{2,6},{3,7},{4,0},{5,1},{6,2},{7,3},{8,12},{9,13},{10,... | collective-permute-start | bytes 393224 | tf_op jit(solution)/shard_map/ppermute | solution.py:41
  (319 other events, 5728.5 us)

commit v2 on v1

v2 whole, which is shorter than its diff:
```python
import functools

import jax
import jax.numpy as jnp
from jax import lax
from jax.experimental import pallas as pl
from jax.experimental.pallas import tpu as pltpu
from jax.sharding import PartitionSpec as P

D = 2048
HEADS = 32
HD = 64
KVH = 4
FF = 5632
STEP = 10
RANK = 16
CHUNKS = 8
EXTRA = 128
COST = 1 << 10

EPS_NORM = 1e-05
ROPE_BASE = 10000.0
CLIP_MAX = 1.0
BETA_FIRST = 0.9
BETA_SECOND = 0.999
ADAM_EPS = 1e-08
WEIGHT_DECAY = 0.01
RATE_ADAPT = 0.02
RATE_OUTER = 0.05
RATE_MAGNITUDE = 0.4
PRECISE = lax.Precision.HIGHEST
MASKED = -1e30
NT = (((1,), (1,)), ((), ()))
GROUP = HEADS // KVH
FWD = 4
BWD = 4
BF = jnp.bfloat16
F32 = jnp.float32
WIDTHS = [D, KVH * HD, KVH * HD, D, FF, FF, D]
STARTS = [sum(WIDTHS[:number]) for number in range(7)]
OUTS = sum(WIDTHS)


def bits_of(count):
    return [1 << place for place in range(count.bit_length() - 1)]


def swap(array, axis, distance):
    count = lax.axis_size(axis)
    return lax.ppermute(array, axis, [(i, i ^ distance) for i in range(count)])


def mm(left, right):
    return jnp.dot(left, right, preferred_element_type=F32)


def mm_t(left, right):
    return lax.dot_general(left, right, (((1,), (1,)), ((), ())), preferred_element_type=F32)


def t_mm(left, right):
    return lax.dot_general(left, right, (((0,), (0,)), ((), ())), preferred_element_type=F32)


def two_parts(values):
    high = lax.reduce_precision(values, 8, 7)
    return high.astype(BF), (values - high).astype(BF)


def fold_parts(stacked, count):
    return stacked[:count] + stacked[count : 2 * count]


def adam(param, grad, first, second, rate, clip_factor):
    clipped = grad * clip_factor
    first_new = BETA_FIRST * first + (1.0 - BETA_FIRST) * clipped
    second_new = BETA_SECOND * second + (1.0 - BETA_SECOND) * clipped * clipped
    first_hat = first_new / (1.0 - BETA_FIRST**STEP)
    second_hat = second_new / (1.0 - BETA_SECOND**STEP)
    param_new = param - rate * (
        first_hat / (jnp.sqrt(second_hat) + ADAM_EPS) + WEIGHT_DECAY * param
    )
    return (param_new, first_new, second_new)


def squared_sum(values):
    return jnp.sum(values * values)


def all_sum(values, axes):
    for axis in axes:
        for bit in bits_of(lax.axis_size(axis)):
            values = values + swap(values, axis, bit)
    return values


def all_blocks(block, axis):
    stacked = block[None]
    index = lax.axis_index(axis)
    for bit in bits_of(lax.axis_size(axis)):
        upper = (index // bit) % 2 == 1
        received = swap(stacked, axis, bit)
        stacked = jnp.concatenate(
            [jnp.where(upper, received, stacked), jnp.where(upper, stacked, received)]
        )
    return stacked


def scatter_sum(blocks, axis, wire=F32, order=None):
    index = lax.axis_index(axis)
    bits = bits_of(lax.axis_size(axis))
    shape = blocks.shape[1:]
    left = list(reversed(bits))
    blocks = blocks.reshape((2,) * len(bits) + shape)
    for bit in order or bits:
        dim = left.index(bit)
        side = (index // bit) % 2
        keep = lax.dynamic_index_in_dim(blocks, side, dim, keepdims=False)
        send = lax.dynamic_index_in_dim(blocks, 1 - side, dim, keepdims=False)
        blocks = keep + swap(send.astype(wire), axis, bit).astype(blocks.dtype)
        left.remove(bit)
    return blocks


def after(value, *others):
    return lax.optimization_barrier((value,) + others)[0]


def gather_slots(shard, turned=False):
    slots = {0: shard}
    count = lax.axis_size("wide")
    for slot in sorted(range(1, count), key=lambda i: bin(i).count("1")):
        low = slot & -slot
        if turned and slot == count - 1:
            low = count // 4
        slots[slot] = swap(slots[slot ^ low], "wide", low)
    return slots


def near(slots):
    return [held for slot, held in slots.items() if bin(slot).count("1") == 1]


def put_rows(slots, extra):
    count = lax.axis_size("wide")
    index = lax.axis_index("wide")
    rows, cols = slots[0].shape
    whole = jnp.zeros((count * rows + extra.shape[0], cols), extra.dtype)
    whole = lax.dynamic_update_slice(whole, extra, (count * rows, 0))
    for slot, held in slots.items():
        whole = lax.dynamic_update_slice(whole, held, ((index ^ slot) * rows, 0))
    return whole


def rotate_half(values):
    half = HD // 2
    return jnp.concatenate([values[..., half:], values[..., :half]], axis=-1)


def turn(values, cosine, sine):
    shaped = values.reshape(values.shape[0], -1, HD)
    turned = shaped * cosine[:, None, :] + rotate_half(shaped) * sine[:, None, :]
    return turned.reshape(values.shape)


def pad_rows(rows, count):
    return jnp.concatenate([rows, jnp.zeros((count - rows.shape[0], rows.shape[1]), rows.dtype)])


def lanes_of(reduced):
    high, low = two_parts(reduced)
    return jnp.pad(
        jnp.concatenate([high, low], axis=1), ((0, 0), (0, EXTRA - 2 * reduced.shape[1]))
    )


def twice_low(rows):
    doubled = 2.0 * rows.astype(BF)
    return pad_rows(jnp.concatenate([doubled, doubled]), EXTRA)


def gram_of(left, right):
    return lax.dot_general(left, right, (((1,), (1,)), ((), ())), precision=PRECISE)


def turn_lanes(values, cosine, sine):
    lane = lax.broadcasted_iota(jnp.int32, values.shape, 1) % HD
    swapped = jnp.where(
        lane < HD // 2,
        pltpu.roll(values, 2 * HD - HD // 2, 1),
        pltpu.roll(values, HD // 2, 1),
    )
    return values * cosine + swapped * sine


def head_rows(pairs, low_side):
    rows = []
    for pair in pairs:
        lane = lax.broadcasted_iota(jnp.int32, pair.shape, 1)
        moved = pltpu.roll(pair, HD, 1)
        if low_side:
            rows.append(jnp.where(lane < HD, pair, 0.0))
            rows.append(jnp.where(lane < HD, moved, 0.0))
        else:
            rows.append(jnp.where(lane >= HD, moved, 0.0))
            rows.append(jnp.where(lane >= HD, pair, 0.0))
    return jnp.concatenate(rows, axis=0).astype(BF)


def pairs_of(columns, block):
    turned = jnp.concatenate([columns, columns], axis=0).T
    lane = lax.broadcasted_iota(jnp.int32, (block, 2 * HD), 1)
    out = []
    for pair in range(GROUP // 2):
        first = turned[2 * pair * block : (2 * pair + 1) * block]
        second = turned[(2 * pair + 1) * block : (2 * pair + 2) * block]
        out.append(jnp.where(lane < HD, first, second))
    return out


def forward_kernel(
    first_ref, z_ref, scale_ref, cos_ref, sin_ref, place_ref, start_ref, kv_ref, kvt_ref,
    query_ref, out_ref, log_ref, *, block, span, groups,
):
    rows = GROUP * block
    width = GROUP * HD

    def chunk_body(chunk, carry):
        at = pl.ds(pl.multiple_of(chunk * block, block), block)
        cosine = cos_ref[at, :]
        sine = sin_ref[at, :]
        query_rows = []
        for group in range(groups):
            pairs = []
            for pair in range(GROUP // 2):
                lanes = slice(group * width + pair * 2 * HD, group * width + (pair + 1) * 2 * HD)
                turned = turn_lanes(z_ref[at, lanes] * scale_ref[:, lanes], cosine, sine)
                low = turned.astype(BF)
                query_ref[at, lanes] = low
                pairs.append(low.astype(F32) * HD**-0.5)
            query_rows.append(head_rows(pairs, True))
        place = place_ref[chunk]
        start = start_ref[chunk]

        def key_body(step, state):
            key_block = chunk - step
            keys = pl.ds(pl.multiple_of(key_block * span, span), span)
            spot = key_block * span + lax.broadcasted_iota(jnp.int32, (span, rows), 0)
            allowed = (spot <= place) & (spot >= start)
            out = []
            all_scores = [
                lax.dot_general(
                    kv_ref[keys, group * 2 * HD : (group + 1) * 2 * HD], query_rows[group], NT, preferred_element_type=F32
                )
                for group in range(groups)
            ]
            for group in range(groups):
                peak, total, mixed = state[group]
                scores = jnp.where(allowed, all_scores[group], MASKED)
                peak_new = jnp.maximum(peak, jnp.max(scores, axis=0, keepdims=True))
                powers = jnp.exp(scores - peak_new)
                shrink = jnp.exp(peak - peak_new)
                total = total * shrink + jnp.sum(powers, axis=0, keepdims=True)
                mixed = mixed * shrink + jnp.dot(
                    kvt_ref[group, HD:, keys], powers.astype(BF), preferred_element_type=F32
                )
                out.append((peak_new, total, mixed))
            return tuple(out)

        start_state = tuple(
            (
                jnp.full((1, rows), MASKED, F32),
                jnp.zeros((1, rows), F32),
                jnp.zeros((HD, rows), F32),
            )
            for _ in range(groups)
        )
        state = lax.fori_loop(0, chunk + 1 - first_ref[chunk], key_body, start_state)
        for group in range(groups):
            peak, total, mixed = state[group]
            log_ref[group, chunk] = peak + jnp.log(total)
            for pair, value in enumerate(pairs_of(mixed / total, block)):
                low_lane = group * width + pair * 2 * HD
                out_ref[at, low_lane : low_lane + 2 * HD] = value.astype(BF)
        return carry

    lax.fori_loop(0, CHUNKS, chunk_body, 0)


def backward_kernel(
    first_ref, query_ref, cos_ref, sin_ref, place_ref, start_ref, kv_ref, kvt_ref, log_ref,
    out_ref, grad_ref, query_grad_ref, kv_grad_ref, sums, *, block, span, groups,
):
    rows = GROUP * block
    width = GROUP * HD
    sums[...] = jnp.zeros_like(sums)

    def chunk_body(chunk, carry):
        at = pl.ds(pl.multiple_of(chunk * block, block), block)
        tiles = []
        for group in range(groups):
            queries = []
            grads = []
            product_rows = []
            for pair in range(GROUP // 2):
                lanes = slice(group * width + pair * 2 * HD, group * width + (pair + 1) * 2 * HD)
                queries.append(query_ref[at, lanes].astype(F32) * HD**-0.5)
                grad = grad_ref[at, lanes].astype(F32)
                grads.append(grad)
                product = grad * out_ref[at, lanes].astype(F32)
                lane = lax.broadcasted_iota(jnp.int32, product.shape, 1)
                product_rows.append(jnp.where(lane < HD, product, 0.0))
                product_rows.append(jnp.where(lane >= HD, product, 0.0))
            inner = jnp.sum(jnp.concatenate(product_rows, axis=0).T, axis=0, keepdims=True)
            query_rows = head_rows(queries, True)
            grad_rows = head_rows(grads, False)
            tiles.append((query_rows, grad_rows, inner, log_ref[group, chunk]))
        place = place_ref[chunk]
        start = start_ref[chunk]

        def key_body(key_block, query_grads):
            keys = pl.ds(pl.multiple_of(key_block * span, span), span)
            spot = key_block * span + lax.broadcasted_iota(jnp.int32, (span, rows), 0)
            allowed = (spot <= place) & (spot >= start)
            out = []
            products = []
            for group in range(groups):
                query_rows, grad_rows, inner, log_total = tiles[group]
                kv = kv_ref[keys, group * 2 * HD : (group + 1) * 2 * HD]
                products.append(
                    (
                        lax.dot_general(kv, query_rows, NT, preferred_element_type=F32),
                        lax.dot_general(kv, grad_rows, NT, preferred_element_type=F32),
                    )
                )
            for group in range(groups):
                query_rows, grad_rows, inner, log_total = tiles[group]
                scores, grad_weights = products[group]
                weights = jnp.exp(jnp.where(allowed, scores - log_total, MASKED))
                grad_scores = (weights * (grad_weights - inner)).astype(BF)
                sums[group, keys, :] += jnp.dot(
                    grad_scores, query_rows, preferred_element_type=F32
                ) + jnp.dot(weights.astype(BF), grad_rows, preferred_element_type=F32)
                out.append(
                    query_grads[group]
                    + jnp.dot(kvt_ref[group, :HD, keys], grad_scores, preferred_element_type=F32)
                )
            return tuple(out)

        query_grads = lax.fori_loop(
            first_ref[chunk],
            chunk + 1,
            key_body,
            tuple(jnp.zeros((HD, rows), F32) for _ in range(groups)),
        )
        cosine = cos_ref[at, :]
        sine = sin_ref[at, :]
        for group in range(groups):
            for pair, value in enumerate(pairs_of(query_grads[group] * HD**-0.5, block)):
                low_lane = group * width + pair * 2 * HD
                query_grad_ref[at, low_lane : low_lane + 2 * HD] = turn_lanes(
                    value, cosine, -sine
                )
        return carry

    lax.fori_loop(0, CHUNKS, chunk_body, 0)
    for group in range(groups):
        kv_grad_ref[:, group * 2 * HD : (group + 1) * 2 * HD] = sums[group].astype(BF)


def attend(first_block, z, scale, cosine, sine, places, starts, kv, kvt):
    count = z.shape[0]
    block = count // CHUNKS
    length = kv.shape[0]
    span = length // CHUNKS
    rows = GROUP * block
    width = FWD * GROUP * HD
    grid_spec = pltpu.PrefetchScalarGridSpec(
        num_scalar_prefetch=1,
        grid=(KVH // FWD,),
        in_specs=[
            pl.BlockSpec((count, width), lambda g, s: (0, g)),
            pl.BlockSpec((1, width), lambda g, s: (0, g)),
            pl.BlockSpec((count, 2 * HD), lambda g, s: (0, 0)),
            pl.BlockSpec((count, 2 * HD), lambda g, s: (0, 0)),
            pl.BlockSpec((CHUNKS, 1, rows), lambda g, s: (0, 0, 0)),
            pl.BlockSpec((CHUNKS, 1, rows), lambda g, s: (0, 0, 0)),
            pl.BlockSpec((length, FWD * 2 * HD), lambda g, s: (0, g)),
            pl.BlockSpec((FWD, 2 * HD, length), lambda g, s: (g, 0, 0)),
        ],
        out_specs=[
            pl.BlockSpec((count, width), lambda g, s: (0, g)),
            pl.BlockSpec((count, width), lambda g, s: (0, g)),
            pl.BlockSpec((FWD, CHUNKS, 1, rows), lambda g, s: (g, 0, 0, 0)),
        ],
    )
    return pl.pallas_call(
        functools.partial(forward_kernel, block=block, span=span, groups=FWD),
        grid_spec=grid_spec,
        out_shape=[
            jax.ShapeDtypeStruct((count, HEADS * HD), BF),
            jax.ShapeDtypeStruct((count, HEADS * HD), BF),
            jax.ShapeDtypeStruct((KVH, CHUNKS, 1, rows), F32),
        ],
        compiler_params=pltpu.CompilerParams(vmem_limit_bytes=40 << 20),
        cost_estimate=pl.CostEstimate(flops=COST, bytes_accessed=COST, transcendentals=0),
    )(first_block, z, scale, cosine, sine, places, starts, kv, kvt)


def attend_back(
    first_block, queries, cosine, sine, places, starts, kv, kvt, log_total, attended, grads
):
    count = queries.shape[0]
    block = count // CHUNKS
    length = kv.shape[0]
    span = length // CHUNKS
    rows = GROUP * block
    width = BWD * GROUP * HD
    grid_spec = pltpu.PrefetchScalarGridSpec(
        num_scalar_prefetch=1,
        grid=(KVH // BWD,),
        in_specs=[
            pl.BlockSpec((count, width), lambda g, s: (0, g)),
            pl.BlockSpec((count, 2 * HD), lambda g, s: (0, 0)),
            pl.BlockSpec((count, 2 * HD), lambda g, s: (0, 0)),
            pl.BlockSpec((CHUNKS, 1, rows), lambda g, s: (0, 0, 0)),
            pl.BlockSpec((CHUNKS, 1, rows), lambda g, s: (0, 0, 0)),
            pl.BlockSpec((length, BWD * 2 * HD), lambda g, s: (0, g)),
            pl.BlockSpec((BWD, 2 * HD, length), lambda g, s: (g, 0, 0)),
            pl.BlockSpec((BWD, CHUNKS, 1, rows), lambda g, s: (g, 0, 0, 0)),
            pl.BlockSpec((count, width), lambda g, s: (0, g)),
            pl.BlockSpec((count, width), lambda g, s: (0, g)),
        ],
        out_specs=[
            pl.BlockSpec((count, width), lambda g, s: (0, g)),
            pl.BlockSpec((length, BWD * 2 * HD), lambda g, s: (0, g)),
        ],
        scratch_shapes=[pltpu.VMEM((BWD, length, 2 * HD), F32)],
    )
    return pl.pallas_call(
        functools.partial(backward_kernel, block=block, span=span, groups=BWD),
        grid_spec=grid_spec,
        out_shape=[
            jax.ShapeDtypeStruct((count, HEADS * HD), F32),
            jax.ShapeDtypeStruct((length, KVH * 2 * HD), BF),
        ],
        compiler_params=pltpu.CompilerParams(vmem_limit_bytes=40 << 20),
        cost_estimate=pl.CostEstimate(flops=COST, bytes_accessed=COST, transcendentals=0),
    )(first_block, queries, cosine, sine, places, starts, kv, kvt, log_total, attended, grads)


def place_of(place_ref, slot, rows):
    return pl.multiple_of((place_ref[0] ^ slot) * rows, rows)


def half_place(place_ref, half, tiles, pair_tiles):
    return (place_ref[1] ^ half) * pair_tiles + tiles


def set_rows(outer, offset):
    rank, cols = outer.shape
    parts = [outer]
    if offset:
        parts = [jnp.zeros((offset, cols), outer.dtype)] + parts
    if EXTRA - rank - offset:
        parts = parts + [jnp.zeros((EXTRA - rank - offset, cols), outer.dtype)]
    return jnp.concatenate(parts, axis=0)


def split_parts(values):
    high = values.astype(BF)
    return high, (values - high.astype(F32)).astype(BF)


def low_rank(reduced, outer, offset):
    high, low = split_parts(reduced)
    rows = set_rows(2.0 * outer.astype(BF).astype(F32), offset).astype(BF)
    return jnp.dot(high, rows, preferred_element_type=F32) + jnp.dot(
        low, rows, preferred_element_type=F32
    )


def slot_kernel(place_ref, inputs_ref, first_ref, outer_ref, *refs, offset):
    slots, out_ref, reduced_ref = refs[:-2], refs[-2], refs[-1]
    each = len(slots) // 2
    rows = slots[0].shape[0]

    @pl.when((pl.program_id(0) == 0) & (pl.program_id(1) == 0))
    def _():
        reduced_ref[...] = jnp.dot(inputs_ref[...], first_ref[...], preferred_element_type=F32)

    def total(chosen):
        result = low_rank(reduced_ref[...], outer_ref[...], offset)
        for slot, ref in enumerate(chosen):
            result = result + jnp.dot(
                inputs_ref[:, pl.ds(place_of(place_ref, slot, rows), rows)],
                ref[...],
                preferred_element_type=F32,
            )
        out_ref[...] = result

    for half in range(2):

        @pl.when(pl.program_id(0) == half)
        def _():
            total(slots[half * each : (half + 1) * each])


def slot_mm(place, inputs, first, outer, offset, slots, tile=256):
    rows = slots[0][0].shape[0]
    cols = outer.shape[1]
    tiles = cols // 2 // tile

    def held(half):
        def spot(h, n, s):
            return (0, jnp.where(h == half, n, (tiles - 1) * (1 - half)))

        return pl.BlockSpec((rows, tile), spot)

    return pl.pallas_call(
        functools.partial(slot_kernel, offset=offset),
        grid_spec=pltpu.PrefetchScalarGridSpec(
            num_scalar_prefetch=1,
            grid=(2, tiles),
            in_specs=[
                pl.BlockSpec(inputs.shape, lambda h, n, s: (0, 0)),
                pl.BlockSpec(first.shape, lambda h, n, s: (0, 0)),
                pl.BlockSpec(
                    (outer.shape[0], tile), lambda h, n, s: (0, half_place(s, h, n, tiles))
                ),
            ]
            + [held(half) for half in range(2) for _ in slots[half]],
            out_specs=[
                pl.BlockSpec(
                    (inputs.shape[0], tile), lambda h, n, s: (0, half_place(s, h, n, tiles))
                ),
                pl.BlockSpec((inputs.shape[0], EXTRA), lambda h, n, s: (0, 0)),
            ],
        ),
        out_shape=[
            jax.ShapeDtypeStruct((inputs.shape[0], cols), F32),
            jax.ShapeDtypeStruct((inputs.shape[0], EXTRA), F32),
        ],
        compiler_params=pltpu.CompilerParams(vmem_limit_bytes=40 << 20),
        cost_estimate=pl.CostEstimate(flops=COST, bytes_accessed=COST, transcendentals=0),
    )(place, inputs, first, outer, *slots[0], *slots[1])


def finish_kernel(*refs, count, sizes, offset, summed):
    raws = refs[: len(sizes)]
    narrow_ref, middle_ref, first_ref, inputs_ref, grad_ref, out_ref = refs[len(sizes) :]
    first = first_ref[...]
    narrow_high, narrow_low = split_parts(narrow_ref[...])
    total = lax.dot_general(narrow_high, first, NT, preferred_element_type=F32)
    total = total + lax.dot_general(narrow_low, first, NT, preferred_element_type=F32)
    weighted = []
    for ref, size in zip(raws, sizes):
        total = total + ref[:count, :]
        weighted.append(ref[count : count + size, :] + ref[count + size :, :])
    grad_ref[...] = total
    weighted = sum(weighted) if summed else jnp.concatenate(weighted, axis=0)
    middle_high, middle_low = split_parts(middle_ref[...])
    middle = lax.dot_general(middle_high, first, NT, preferred_element_type=F32)
    middle = middle + lax.dot_general(middle_low, first, NT, preferred_element_type=F32)
    under = (((0,), (0,)), ((), ()))
    inputs = inputs_ref[...]
    product = lax.dot_general(narrow_high, inputs, under, preferred_element_type=F32)
    product = product + lax.dot_general(narrow_low, inputs, under, preferred_element_type=F32)
    out_ref[...] = (
        product[offset : offset + weighted.shape[0]] + 2.0 * (weighted + 2.0 * middle)
    )


def finish_back(raws, sizes, narrow, middle, first, inputs, offset, summed=False, tile=512):
    count = inputs.shape[0]
    rank = middle.shape[0]
    tiled = lambda rows: pl.BlockSpec((rows, tile), lambda n: (0, n))
    return pl.pallas_call(
        functools.partial(
            finish_kernel, count=count, sizes=sizes, offset=offset, summed=summed
        ),
        grid=(D // tile,),
        in_specs=[tiled(raw.shape[0]) for raw in raws]
        + [
            pl.BlockSpec(narrow.shape, lambda n: (0, 0)),
            pl.BlockSpec(middle.shape, lambda n: (0, 0)),
            pl.BlockSpec((tile, EXTRA), lambda n: (n, 0)),
            tiled(count),
        ],
        out_specs=[tiled(count), tiled(rank)],
        out_shape=[
            jax.ShapeDtypeStruct((count, D), F32),
            jax.ShapeDtypeStruct((rank, D), F32),
        ],
        compiler_params=pltpu.CompilerParams(vmem_limit_bytes=40 << 20),
        cost_estimate=pl.CostEstimate(flops=COST, bytes_accessed=COST, transcendentals=0),
    )(*raws, narrow, middle, first, inputs)


def slot_back_kernel(place_ref, grad_ref, *refs):
    slots, out_ref, held, arrived = refs[:-3], refs[-3], refs[-2], refs[-1]
    each = len(slots) // 2
    rows, cols = held.shape[1:]
    copies = [
        pltpu.make_async_copy(ref.at[:, pl.ds(0, cols)], held.at[slot], arrived.at[slot])
        for slot, ref in enumerate(slots)
    ]
    for slot in range(each):
        copies[slot].start()
        copies[each + slot].start()
    grads = [
        grad_ref[:, pl.ds(pl.multiple_of((place_ref[1] ^ half) * cols, cols), cols)]
        for half in range(2)
    ]
    for slot in range(each):
        copies[slot].wait()
        copies[each + slot].wait()
        out_ref[:, pl.ds(place_of(place_ref, slot, rows), rows)] = lax.dot_general(
            grads[0], held[slot], NT, preferred_element_type=F32
        ) + lax.dot_general(grads[1], held[each + slot], NT, preferred_element_type=F32)


def slot_back(place, grads, slots):
    rows = slots[0][0].shape[0]
    count, cols = grads.shape
    many = 2 * len(slots[0])
    return pl.pallas_call(
        slot_back_kernel,
        grid_spec=pltpu.PrefetchScalarGridSpec(
            num_scalar_prefetch=1,
            grid=(1,),
            in_specs=[pl.BlockSpec((count, cols), lambda n, s: (0, 0))]
            + [pl.BlockSpec(memory_space=pl.ANY) for _ in range(many)],
            out_specs=pl.BlockSpec((count, D), lambda n, s: (0, 0)),
            scratch_shapes=[
                pltpu.VMEM((many, rows, cols // 2), BF),
                pltpu.SemaphoreType.DMA((many,)),
            ],
        ),
        out_shape=jax.ShapeDtypeStruct((count, D), F32),
        compiler_params=pltpu.CompilerParams(vmem_limit_bytes=40 << 20),
        cost_estimate=pl.CostEstimate(flops=COST, bytes_accessed=COST, transcendentals=0),
    )(place, grads, *slots[0], *slots[1])


def slot_back_wide(place, grads, slots):
    rows = slots[0].shape[0]
    out = jnp.zeros((grads.shape[0], len(slots) * rows), F32)
    for slot, held in enumerate(slots):
        out = lax.dynamic_update_slice(out, mm_t(grads, held), (0, (place[0] ^ slot) * rows))
    return out


def pad_to(rows, count):
    return jnp.concatenate([rows, jnp.zeros((count - rows.shape[0], rows.shape[1]), rows.dtype)])


def split_rows(weighted):
    high = weighted.astype(BF)
    return high, (weighted - high.astype(F32)).astype(BF)


def terms_of(grads_low, weighted, outer, reduced, offset):
    rank = outer.shape[0]
    rows = set_rows(outer, offset)
    narrow = 2.0 * lax.dot_general(grads_low, rows.astype(BF), NT, preferred_element_type=F32)
    middle = lax.dot_general(weighted, rows, NT, precision=PRECISE, preferred_element_type=F32)
    own = lax.broadcasted_iota(jnp.int32, middle.shape, 0) // RANK + offset // RANK
    middle = jnp.where(
        lax.broadcasted_iota(jnp.int32, middle.shape, 1) // RANK == own, middle, 0.0
    )
    under = (((0,), (0,)), ((), ()))
    high, low = split_parts(reduced)
    both = lax.dot_general(high, grads_low, under, preferred_element_type=F32)
    both = both + lax.dot_general(low, grads_low, under, preferred_element_type=F32)
    return narrow, middle, 2.0 * both[offset : offset + rank]


def terms_kernel(
    grad_ref, z_ref, scale_ref, slope_ref, outer_ref, reduced_ref,
    rows_ref, sum_ref, product_ref, narrow_ref, middle_ref, *, offset,
):
    count = grad_ref.shape[0]
    rank = outer_ref.shape[0]
    grads = grad_ref[...]
    sums = jnp.sum(grads * z_ref[...], axis=0, keepdims=True)
    sum_ref[...] = sums
    low = (grads * scale_ref[...]).astype(BF)
    weighted = (sums * slope_ref[...]) * outer_ref[...]
    high_part, low_part = split_rows(weighted)
    rows_ref[:count, :] = low
    rows_ref[count : count + rank, :] = high_part
    rows_ref[count + rank :, :] = low_part
    narrow, middle, product = terms_of(
        low, weighted, outer_ref[...], reduced_ref[...], offset
    )
    product_ref[...] = product

    @pl.when(pl.program_id(0) == 0)
    def _():
        narrow_ref[...] = narrow
        middle_ref[...] = middle

    @pl.when(pl.program_id(0) > 0)
    def _():
        narrow_ref[...] += narrow
        middle_ref[...] += middle


def grad_terms(grads, z, scale, slope, outer, offset, reduced, tile=512):
    count, cols = grads.shape
    rank = outer.shape[0]
    tiled = lambda rows: pl.BlockSpec((rows, tile), lambda n: (0, n))
    fixed = lambda rows, width: pl.BlockSpec((rows, width), lambda n: (0, 0))
    return pl.pallas_call(
        functools.partial(terms_kernel, offset=offset),
        grid=(cols // tile,),
        in_specs=[
            tiled(count), tiled(count), tiled(1), tiled(1), tiled(rank),
            fixed(count, reduced.shape[1]),
        ],
        out_specs=[
            tiled(count + 2 * rank), tiled(1), tiled(rank), fixed(count, EXTRA), fixed(rank, EXTRA),
        ],
        out_shape=[
            jax.ShapeDtypeStruct((count + 2 * rank, cols), BF),
            jax.ShapeDtypeStruct((1, cols), F32),
            jax.ShapeDtypeStruct((rank, cols), F32),
            jax.ShapeDtypeStruct((count, EXTRA), F32),
            jax.ShapeDtypeStruct((rank, EXTRA), F32),
        ],
        compiler_params=pltpu.CompilerParams(vmem_limit_bytes=40 << 20),
        cost_estimate=pl.CostEstimate(flops=COST, bytes_accessed=COST, transcendentals=0),
    )(grads, z, scale, slope, outer, reduced)


def mlp_kernel(
    place_ref, inputs_ref, main_ref, scale_ref, slope_ref, outer_ref,
    down_grad_ref, narrow_down_ref, first_ref, down_ref, *refs, offset,
):
    slots, kept = refs[:-7], refs[-7:]
    hidden_ref, rows_ref, sum_ref, product_ref, narrow_ref, middle_ref, reduced_ref = kept
    rows = slots[0].shape[0]
    half = hidden_ref.shape[1]
    count = hidden_ref.shape[0]

    @pl.when(pl.program_id(0) == 0)
    def _():
        reduced_ref[...] = jnp.dot(inputs_ref[...], main_ref[...], preferred_element_type=F32)

    gate_lanes = lax.broadcasted_iota(jnp.int32, (RANK, 2 * half), 1) < half
    outer = jnp.concatenate(
        [
            jnp.where(gate_lanes, outer_ref[...], 0.0),
            jnp.where(gate_lanes, 0.0, outer_ref[...]),
        ],
        axis=0,
    )
    z = low_rank(reduced_ref[...], outer, offset)
    for slot, ref in enumerate(slots):
        z = z + jnp.dot(
            inputs_ref[:, pl.ds(place_of(place_ref, slot, rows), rows)],
            ref[...],
            preferred_element_type=F32,
        )
    grad_hidden = lax.dot_general(
        down_grad_ref[...], down_ref[...], NT, preferred_element_type=F32
    ) + lax.dot_general(narrow_down_ref[...], first_ref[...], NT, preferred_element_type=F32)
    scale = scale_ref[...]
    gate_z, up_z = z[:, :half], z[:, half:]
    gate = gate_z * scale[:, :half]
    up = up_z * scale[:, half:]
    sigmoid = 1.0 / (1.0 + jnp.exp(-gate))
    silu = gate * sigmoid
    hidden_ref[...] = (silu * up).astype(BF)
    grad_up = grad_hidden * silu
    grad_gate = grad_hidden * up * (sigmoid * (1.0 + gate * (1.0 - sigmoid)))
    sums = jnp.concatenate(
        [
            jnp.sum(grad_gate * gate_z, axis=0, keepdims=True),
            jnp.sum(grad_up * up_z, axis=0, keepdims=True),
        ],
        axis=1,
    )
    sum_ref[...] = sums
    low = jnp.concatenate(
        [(grad_gate * scale[:, :half]).astype(BF), (grad_up * scale[:, half:]).astype(BF)], axis=1
    )
    rank = outer.shape[0]
    weighted = (sums * slope_ref[...]) * outer
    high_part, low_part = split_rows(weighted)
    rows_ref[:count, :] = low
    rows_ref[count : count + rank, :] = high_part
    rows_ref[count + rank :, :] = low_part
    narrow, middle, product = terms_of(low, weighted, outer, reduced_ref[...], offset)
    product_ref[:, :half] = product[: rank // 2, :half]
    product_ref[:, half:] = product[rank // 2 :, half:]

    @pl.when(pl.program_id(0) == 0)
    def _():
        narrow_ref[...] = narrow
        middle_ref[...] = middle

    @pl.when(pl.program_id(0) > 0)
    def _():
        narrow_ref[...] += narrow
        middle_ref[...] += middle


def mlp_block(
    place, inputs, first, offset, scale, slope, outer, down_grad, narrow_down, down, slots
):
    rows, cols = slots[0].shape
    count = inputs.shape[0]
    rank = 2 * RANK
    tile = 256
    fixed = lambda array: pl.BlockSpec(array.shape, lambda n, s: (0, 0))
    tiled = lambda rows: pl.BlockSpec((rows, tile), lambda n, s: (0, n))
    kept = lambda rows: pl.BlockSpec((rows, EXTRA), lambda n, s: (0, 0))
    return pl.pallas_call(
        functools.partial(mlp_kernel, offset=offset),
        grid_spec=pltpu.PrefetchScalarGridSpec(
            num_scalar_prefetch=1,
            grid=(cols // tile,),
            in_specs=[
                fixed(inputs), fixed(first), tiled(1), tiled(1), tiled(RANK), fixed(down_grad),
                fixed(narrow_down),
                pl.BlockSpec((tile // 2, 128), lambda n, s: (n, D // 128)),
                pl.BlockSpec((tile // 2, D), lambda n, s: (n, 0)),
            ]
            + [tiled(rows) for _ in slots],
            out_specs=[
                pl.BlockSpec((count, tile // 2), lambda n, s: (0, n)),
                tiled(count + 2 * rank),
                tiled(1),
                tiled(RANK),
                kept(count),
                kept(rank),
            ],
            scratch_shapes=[pltpu.VMEM((count, EXTRA), F32)],
        ),
        out_shape=[
            jax.ShapeDtypeStruct((count, cols // 2), BF),
            jax.ShapeDtypeStruct((count + 2 * rank, cols), BF),
            jax.ShapeDtypeStruct((1, cols), F32),
            jax.ShapeDtypeStruct((RANK, cols), F32),
            jax.ShapeDtypeStruct((count, EXTRA), F32),
            jax.ShapeDtypeStruct((rank, EXTRA), F32),
        ],
        compiler_params=pltpu.CompilerParams(vmem_limit_bytes=48 << 20),
        cost_estimate=pl.CostEstimate(flops=COST, bytes_accessed=COST, transcendentals=0),
    )(place, inputs, first, scale, slope, outer, down_grad, narrow_down, down, down, *slots)


def spread_kernel(quarter_ref, own_ref, other_ref, gate_ref, up_ref, hold, *, part):
    width = gate_ref.shape[1]
    blocks = width // (4 * part)
    for side, ref in enumerate((gate_ref, up_ref)):
        ref[...] = jnp.zeros_like(ref)
        for which, source in enumerate((own_ref, other_ref)):
            for tile in range(blocks * part // 128):
                hold[:, tile * 128 : (tile + 1) * 128] = source[
                    :, (2 * tile + side) * 128 : (2 * tile + side + 1) * 128
                ]
            for quarter in range(4):

                @pl.when((quarter_ref[0] ^ which) == quarter)
                def _():
                    for at in range(blocks):
                        low = (at * 4 + quarter) * part
                        ref[:, low : low + part] = hold[:, at * part : (at + 1) * part]


def spread_pair(quarter, own, other, part):
    rows, cols = own.shape
    return pl.pallas_call(
        functools.partial(spread_kernel, part=part),
        grid_spec=pltpu.PrefetchScalarGridSpec(
            num_scalar_prefetch=1,
            grid=(1,),
            in_specs=[pl.BlockSpec((rows, cols), lambda n, s: (0, 0))] * 2,
            out_specs=[pl.BlockSpec((rows, 2 * cols), lambda n, s: (0, 0))] * 2,
            scratch_shapes=[pltpu.VMEM((rows, cols // 2), F32)],
        ),
        out_shape=[jax.ShapeDtypeStruct((rows, 2 * cols), F32)] * 2,
        cost_estimate=pl.CostEstimate(flops=rows, bytes_accessed=1 << 20, transcendentals=0),
    )(quarter, own, other)


def column_sums(base, first_high, first_low, outer, offset):
    outer_high, outer_low = split_parts(set_rows(outer, offset))
    product = (
        jnp.dot(first_high, outer_high, preferred_element_type=F32)
        + jnp.dot(first_high, outer_low, preferred_element_type=F32)
        + jnp.dot(first_low, outer_high, preferred_element_type=F32)
    )
    merged = base.astype(F32) + 2.0 * product
    merged_high, merged_low = split_parts(merged)
    under = (((0,), (0,)), ((), ()))
    cross = (
        lax.dot_general(first_high, merged_high, under, preferred_element_type=F32)
        + lax.dot_general(first_high, merged_low, under, preferred_element_type=F32)
        + lax.dot_general(first_low, merged_high, under, preferred_element_type=F32)
    )
    return jnp.sum(merged * merged, axis=0, keepdims=True), cross[offset : offset + RANK]


def widened(first):
    return jnp.concatenate(
        [first, jnp.zeros((first.shape[0], EXTRA - first.shape[1]), first.dtype)], axis=1
    )


def early_kernel(
    place_ref, query_ref, key_ref, value_ref, main_ref, outer_ref,
    query_out, kv_out, square_ref, cross_ref,
):
    half = query_out.shape[1]
    kv_cols = key_ref.shape[1]
    high, low = split_parts(widened(main_ref[...]))
    kv_out[:, kv_cols:] = high
    for core in range(2):

        @pl.when(place_ref[1] == core)
        def _():
            query_out[...] = query_ref[:, core * half : (core + 1) * half]
            kv = (key_ref, value_ref)[core][...]
            kv_out[:, :kv_cols] = kv
            start = 2 * half + core * kv_cols
            square, cross = column_sums(
                kv, high, low, outer_ref[:, start : start + kv_cols], (1 + core) * RANK
            )
            square_ref[:, :kv_cols] = square
            cross_ref[:, :kv_cols] = cross
            for tile in range(half // 256):
                at = core * half + tile * 256
                square, cross = column_sums(
                    query_ref[:, at : at + 256], high, low, outer_ref[:, at : at + 256], 0
                )
                to = kv_cols + tile * 256
                square_ref[:, to : to + 256] = square
                cross_ref[:, to : to + 256] = cross


def early_work(place, query, key, value, main, outer):
    rows, cols = query.shape
    kv_cols = key.shape[1]
    fixed = lambda array: pl.BlockSpec(array.shape, lambda n, s: (0, 0))
    shapes = [
        jax.ShapeDtypeStruct((rows, cols // 2), BF),
        jax.ShapeDtypeStruct((rows, kv_cols + EXTRA), BF),
        jax.ShapeDtypeStruct((1, kv_cols + cols // 2), F32),
        jax.ShapeDtypeStruct((RANK, kv_cols + cols // 2), F32),
    ]
    return pl.pallas_call(
        early_kernel,
        grid_spec=pltpu.PrefetchScalarGridSpec(
            num_scalar_prefetch=1,
            grid=(1,),
            in_specs=[fixed(query), fixed(key), fixed(value), fixed(main)]
            + [pl.BlockSpec((RANK, cols + 2 * kv_cols), lambda n, s: (0, 0))],
            out_specs=[fixed(shape) for shape in shapes],
        ),
        out_shape=shapes,
        compiler_params=pltpu.CompilerParams(vmem_limit_bytes=32 << 20),
        cost_estimate=pl.CostEstimate(flops=COST, bytes_accessed=COST, transcendentals=0),
    )(place, query, key, value, main, outer)


def later_kernel(
    place_ref, out_w_ref, gate_ref, up_ref, down_w_ref, main_ref, first_ref, outer_ref, mags_ref,
    out_out, mlp_out, down_out, square_ref, cross_ref, picked_ref, hold, *, part,
):
    half = out_out.shape[1]
    width = gate_ref.shape[1]
    blocks = width // (4 * part)
    cols = blocks * part
    starts = [STARTS[n] for n in range(7)]
    high, low = split_parts(widened(main_ref[...]))
    down_first = widened(first_ref[...])
    down_high, down_low = split_parts(down_first)
    rows = gate_ref.shape[0]
    lanes = mags_ref.shape[0]
    for quarter in range(4):

        @pl.when(place_ref[2] == quarter)
        def _():
            for side, ref in enumerate((gate_ref, up_ref)):
                for at in range(blocks):
                    start = (at * 4 + quarter) * part
                    hold[side, :rows, at * part : (at + 1) * part] = ref[
                        :, start : start + part
                    ].astype(F32)
                    begin = starts[4 + side] + start
                    hold[side, rows : rows + RANK, at * part : (at + 1) * part] = outer_ref[
                        :, begin : begin + part
                    ]
                    hold[side, rows + RANK :, at * part : (at + 1) * part] = mags_ref[
                        :, begin : begin + part
                    ]
    for tile in range(cols // 128):
        for side in range(2):
            to = slice((2 * tile + side) * 128, (2 * tile + side + 1) * 128)
            taken = hold[side, :, tile * 128 : (tile + 1) * 128]
            base = taken[:rows].astype(BF)
            mlp_out[:, to] = base
            outer = taken[rows : rows + RANK]
            picked_ref[:RANK, to] = outer
            picked_ref[RANK:, to] = taken[rows + RANK :]
            square, cross = column_sums(base, high, low, outer, (4 + side) * RANK)
            square_ref[:, half + to.start : half + to.stop] = square
            cross_ref[:, half + to.start : half + to.stop] = cross
    down_at = pl.ds(pl.multiple_of(place_ref[2] * part, 16 if part % 16 == 0 else 8), part)
    down_out[:, : 2 * half] = down_w_ref[down_at, :]
    factor = first_ref[down_at, :]
    factor = jnp.concatenate([factor, factor], axis=1)
    down_out[:, 2 * half :] = widened(factor).astype(BF)
    for core in range(2):

        @pl.when(place_ref[1] == core)
        def _():
            out_out[...] = out_w_ref[:, core * half : (core + 1) * half]
            for tile in range(half // 256):
                at = core * half + tile * 256
                square, cross = column_sums(
                    out_w_ref[:, at : at + 256],
                    high,
                    low,
                    outer_ref[:, starts[3] + at : starts[3] + at + 256],
                    3 * RANK,
                )
                to = slice(tile * 256, (tile + 1) * 256)
                square_ref[:, to] = square
                cross_ref[:, to] = cross
                square, cross = column_sums(
                    down_w_ref[:, at : at + 256],
                    down_high,
                    down_low,
                    outer_ref[:, starts[6] + at : starts[6] + at + 256],
                    0,
                )
                begin = half + 2 * cols + tile * 256
                square_ref[:, begin : begin + 256] = square
                cross_ref[:, begin : begin + 256] = cross


def later_work(place, out_w, gate, up, down_w, main, first, outer, mags, part):
    rows, cols = out_w.shape
    half = cols // 2
    mlp = 2 * (gate.shape[1] // 4)
    total = 2 * half + mlp
    fixed = lambda array: pl.BlockSpec(array.shape, lambda n, s: (0, 0))
    inputs = [out_w, gate, up, down_w, main, first, outer, mags]
    shapes = [
        jax.ShapeDtypeStruct((rows, half), BF),
        jax.ShapeDtypeStruct((rows, mlp), BF),
        jax.ShapeDtypeStruct((part, cols + EXTRA), BF),
        jax.ShapeDtypeStruct((1, total), F32),
        jax.ShapeDtypeStruct((RANK, total), F32),
        jax.ShapeDtypeStruct((RANK + 8, mlp), F32),
    ]
    return pl.pallas_call(
        functools.partial(later_kernel, part=part),
        grid_spec=pltpu.PrefetchScalarGridSpec(
            num_scalar_prefetch=1,
            grid=(1,),
            in_specs=[fixed(array) for array in inputs],
            out_specs=[fixed(shape) for shape in shapes],
            scratch_shapes=[pltpu.VMEM((2, rows + RANK + 8, mlp // 2), F32)],
        ),
        out_shape=shapes,
        compiler_params=pltpu.CompilerParams(vmem_limit_bytes=48 << 20),
        cost_estimate=pl.CostEstimate(flops=COST, bytes_accessed=COST, transcendentals=0),
    )(place, *inputs)


def shards(
    tokens,
    cotangent,
    gain_attn,
    gain_ffn,
    w_query,
    w_key,
    w_value,
    w_output,
    w_gate,
    w_up,
    w_down,
    adapt_main,
    adapt_down,
    adapt_outer,
    magnitudes,
    main_first,
    main_second,
    down_first,
    down_second,
    outer_first,
    outer_second,
    mag_first,
    mag_second,
    segments,
):
    wide_count = lax.axis_size("wide")
    tok_count = lax.axis_size("tok")
    wide = lax.axis_index("wide")
    tok = lax.axis_index("tok")
    core = tok % 2
    place = jnp.stack([wide, core, tok % 4]).astype(jnp.int32)
    quarter = (tok % 4).astype(jnp.int32)[None]
    length, share = tokens.shape
    hidden_share = w_down.shape[0]
    part = hidden_share // 4
    block = length // (wide_count * CHUNKS)
    count = CHUNKS * block
    block_cols = wide_count * part
    half = D // 2
    kv_cols = KVH * HD

    def partner(array):
        return swap(array, "tok", 2)

    def other_core(array):
        return swap(array, "tok", 1)

    def to_tokens(features):
        pieces = features.reshape(CHUNKS, wide_count, block, share)
        whole = jnp.zeros((count, D), features.dtype)
        for slot in range(wide_count):
            piece = lax.dynamic_index_in_dim(pieces, wide ^ slot, 1, keepdims=False)
            piece = piece.reshape(count, share)
            if slot:
                piece = swap(piece, "wide", slot)
            whole = lax.dynamic_update_slice(whole, piece, (0, (wide ^ slot) * share))
        return whole

    across = wide_count // 4
    deep, side = wide // across, wide % across

    def to_tokens_staged(features):
        pieces = features.reshape(CHUNKS, 4, across, block, share)
        rows = jnp.zeros((4, CHUNKS, block, across * share), features.dtype)
        for slot in range(across):
            piece = lax.dynamic_index_in_dim(pieces, side ^ slot, 2, keepdims=False)
            piece = jnp.swapaxes(piece, 0, 1)
            if slot:
                piece = swap(piece, "wide", slot)
            rows = lax.dynamic_update_slice(rows, piece, (0, 0, 0, (side ^ slot) * share))
        whole = jnp.zeros((count, D), features.dtype)
        for slot in range(4):
            piece = lax.dynamic_index_in_dim(rows, deep ^ slot, 0, keepdims=False)
            piece = piece.reshape(count, across * share)
            if slot:
                piece = swap(piece, "wide", slot * across)
            whole = lax.dynamic_update_slice(whole, piece, (0, (deep ^ slot) * across * share))
        return whole

    def from_tokens(rows):
        cols = across * share
        held = jnp.zeros((CHUNKS, 4, block, cols), rows.dtype)
        for slot in range(4):
            piece = lax.dynamic_slice(rows, (0, (deep ^ slot) * cols), (count, cols))
            if slot:
                piece = swap(piece, "wide", slot * across)
            piece = piece.reshape(CHUNKS, 1, block, cols)
            held = lax.dynamic_update_slice(held, piece, (0, deep ^ slot, 0, 0))
        whole = jnp.zeros((CHUNKS, 4, across, block, share), rows.dtype)
        for slot in range(across):
            piece = lax.dynamic_slice_in_dim(held, (side ^ slot) * share, share, 3)
            if slot:
                piece = swap(piece, "wide", slot)
            whole = lax.dynamic_update_slice(whole, piece[:, :, None], (0, 0, side ^ slot, 0, 0))
        return whole.reshape(length, share)

    def own_half(array, axis=-1):
        size = array.shape[axis] // 2
        return lax.dynamic_slice_in_dim(array, core * size, size, axis)

    def in_order(blocks):
        return jnp.where(
            core == 0, jnp.concatenate(blocks, axis=-1), jnp.concatenate(blocks[::-1], axis=-1)
        )

    def by_core(zero, one, flip=0):
        return jnp.where(core == flip, zero, one)

    def sides(array, n):
        return array[..., STARTS[n] : STARTS[n] + WIDTHS[n]]

    ends = [0, kv_cols, kv_cols + half, kv_cols + 2 * half, kv_cols + 2 * half + 2 * block_cols]
    ends.append(ends[-1] + half)

    def cut(array, n):
        return array[..., ends[n] : ends[n + 1]]

    KV, QUERY, OUT, MLP, DOWN = range(5)

    residual = to_tokens(tokens).astype(F32)
    gains = all_blocks(jnp.stack([gain_attn, gain_ffn]), "wide")
    gains = jnp.swapaxes(gains, 0, 1).reshape(2, D)

    query_shard, kv_shard, squares, soon_cross = early_work(
        place, w_query, w_key, w_value, adapt_main, adapt_outer
    )
    kv_slots = [gather_slots(kv_shard)]
    query_slots = [gather_slots(after(query_shard, *near(kv_slots[0])))]
    mags = magnitudes[None]

    def column_terms(squares, pieces):
        norms = jnp.sqrt(all_sum(squares, ["wide"]))
        rows = jnp.concatenate([piece[0] for piece in pieces], axis=1)
        rows = jnp.concatenate([rows, norms])
        out = []
        for held in (rows, other_core(rows)):
            mags_row, norm = held[:1], held[1:2]
            scale, slope = mags_row / norm, -mags_row / (norm * norm * norm)
            start = 0
            split = []
            for piece in pieces:
                stop = start + piece[0].shape[1]
                split.append((scale[:, start:stop], slope[:, start:stop], norm[:, start:stop]))
                start = stop
            out.append(split)
        return out

    soon = column_terms(
        squares, [(by_core(sides(mags, 1), sides(mags, 2)),), (own_half(sides(mags, 0)),)]
    )
    later_output, *_ = lax.optimization_barrier(
        (w_output, residual, *near(kv_slots[0]))
    )
    out_shard, mlp_shard, down_shard, squares, rest_cross, picked = later_work(
        place, later_output, w_gate, w_up, w_down, adapt_main, adapt_down, adapt_outer,
        jnp.broadcast_to(mags, (8, OUTS)), part,
    )
    rest = column_terms(
        squares,
        [(own_half(sides(mags, 3)),), (picked[RANK : RANK + 1],), (own_half(sides(mags, 6)),)],
    )
    mlp_outer = [picked[:RANK]]
    mlp_outer.append(other_core(mlp_outer[0]))
    columns = [soon[k] + rest[k] for k in range(2)]
    scale_by, slope_by, norms_by = (
        [[columns[k][n][i] for n in range(5)] for k in range(2)] for i in range(3)
    )

    def natural_of(parts, n):
        return in_order([p[n] for p in parts])

    scales, slopes, norms = (
        [natural_of(parts, n) if n != MLP else None for n in range(5)]
        for parts in (scale_by, slope_by, norms_by)
    )
    outers = [sides(adapt_outer, n) for n in range(7)]
    outer_kv = jnp.concatenate(
        [jnp.pad(outers[1], ((0, 0), (0, kv_cols))), jnp.pad(outers[2], ((0, 0), (kv_cols, 0)))]
    )

    kv_slots.append({s: other_core(held) for s, held in kv_slots[0].items()})
    query_slots.append({s: other_core(held) for s, held in query_slots[0].items()})
    low_main = put_rows(
        {s: held[:, kv_cols:] for s, held in kv_slots[0].items()}, jnp.zeros((0, EXTRA), BF)
    )

    def main_cols(n, many=1):
        return low_main[:, n * RANK : (n + many) * RANK]

    def norm_rows(values, gain_row):
        inverse = lax.rsqrt(jnp.mean(values * values, axis=1, keepdims=True) + EPS_NORM)
        return (values * inverse * gain_row[None, :]).astype(BF), inverse

    def norm_rows_back(values, gain_row, inverse, grad_normed):
        inner = jnp.sum(values * gain_row[None, :] * grad_normed, axis=1, keepdims=True)
        return (
            grad_normed * gain_row[None, :] * inverse
            - values * (inverse * inverse * inverse * inner / D)
        )

    def ordered(slots):
        return [slots[s] for s in range(wide_count)]

    own_places = (
        jnp.arange(CHUNKS, dtype=jnp.int32)[:, None] * (wide_count * block)
        + wide * block
        + jnp.arange(block, dtype=jnp.int32)[None, :]
    ).reshape(count)
    segment_row = segments[0]
    own_segment = lax.dynamic_index_in_dim(
        segment_row.reshape(CHUNKS, wide_count, block), wide, 1, keepdims=False
    ).reshape(count)
    own_starts = jnp.sum(
        (segment_row[None, :] < own_segment[:, None]).astype(jnp.int32), axis=1
    )
    frequency = ROPE_BASE ** (-2.0 * jnp.arange(HD // 2, dtype=F32) / HD)
    angles = (own_places - own_starts).astype(F32)[:, None] * frequency[None, :]
    cosine = jnp.tile(jnp.cos(angles), (1, 4))
    sine = jnp.tile(jnp.concatenate([-jnp.sin(angles), jnp.sin(angles)], axis=1), (1, 2))
    place_rows = jnp.tile(own_places.reshape(CHUNKS, 1, block), (1, 1, GROUP))
    start_rows = jnp.tile(own_starts.reshape(CHUNKS, 1, block), (1, 1, GROUP))
    first_block = own_starts.reshape(CHUNKS, block)[:, 0] // (wide_count * block)

    normed_one, inverse_one = norm_rows(residual, gains[0])
    kv_z, reduced_one = slot_mm(
        place, normed_one, low_main, outer_kv, RANK, [ordered(kv_slots[k]) for k in range(2)]
    )
    kv_scaled = kv_z * scales[KV]
    keys = turn(kv_scaled[:, :kv_cols], cosine[:, :HD], sine[:, :HD])
    kv = jnp.concatenate(
        [keys.reshape(count, KVH, HD), kv_scaled[:, kv_cols:].reshape(count, KVH, HD)], axis=2
    ).astype(BF)
    token_slots = gather_slots(kv.reshape(CHUNKS, 1, block, KVH * 2 * HD))
    kv = jnp.zeros((CHUNKS, wide_count, block, KVH * 2 * HD), BF)
    for slot, held in token_slots.items():
        kv = lax.dynamic_update_slice(kv, held, (0, wide ^ slot, 0, 0))
    kv = kv.reshape(length, KVH * 2 * HD)
    kvt = kv.T.reshape(KVH, 2 * HD, length)
    query_z, _ = slot_mm(
        place, normed_one, low_main, outers[0], 0, [ordered(query_slots[k]) for k in range(2)]
    )
    queries, attended, log_total = attend(
        first_block, query_z, scales[QUERY], cosine, sine, place_rows, start_rows, kv, kvt
    )

    out_slots = [gather_slots(after(out_shard, *near(query_slots[0])), True)]
    out_slots.append({s: other_core(held) for s, held in out_slots[0].items()})
    upstream = to_tokens_staged(after(cotangent, *near(out_slots[0]), *near(token_slots))).astype(F32)
    down_slots = gather_slots(after(down_shard, *near(out_slots[0]), *token_slots.values()))
    down_weights = [put_rows(down_slots, jnp.zeros((0, D + EXTRA), BF))]
    down_weights.append(other_core(down_weights[0]))
    mlp_slots = [gather_slots(after(mlp_shard, *near(down_slots)), True)]
    mlp_slots.append({s: other_core(held) for s, held in mlp_slots[0].items()})

    output_z, reduced_out = slot_mm(
        place, attended, low_main, outers[3], 3 * RANK, [ordered(out_slots[k]) for k in range(2)]
    )
    hidden_one = residual + output_z * scales[OUT]

    normed_own, inverse_two = norm_rows(hidden_one, gains[1])
    normed_two = jnp.concatenate([normed_own, partner(normed_own)])
    down_low = (upstream * scales[DOWN]).astype(BF)
    down_low = jnp.concatenate([down_low, partner(down_low)])
    narrow_down = 2.0 * mm_t(down_low, outers[6].astype(BF))
    narrow_down_lanes = lanes_of(narrow_down)
    blocks = [
        mlp_block(
            place,
            normed_two,
            low_main,
            4 * RANK,
            scale_by[k][MLP],
            slope_by[k][MLP],
            mlp_outer[k],
            down_low,
            narrow_down_lanes,
            down_weights[k],
            ordered(mlp_slots[k]),
        )
        for k in range(2)
    ]
    through = mm(blocks[0][0], down_weights[0]) + mm(blocks[1][0], down_weights[1])
    reduced_down = through[:, D : D + RANK]
    down_sum = through[:, :D] + mm(
        lanes_of(reduced_down), twice_low(outers[6])
    )

    def first_term(product, weight_term, middle, first_cols):
        both = jnp.concatenate(two_parts(middle))
        return product + 2.0 * (weight_term + 2.0 * fold_parts(mm_t(both, first_cols), RANK))

    backs = [slot_back_wide(place, blocks[k][1], ordered(mlp_slots[k])) for k in range(2)]
    pairs = 2 * RANK
    grad_normed, first_pairs = finish_back(
        backs, [pairs, pairs], blocks[0][4] + blocks[1][4], blocks[0][5] + blocks[1][5], low_main,
        normed_two, 4 * RANK, True,
    )
    swapped = partner(grad_normed[count:].astype(BF))
    grad_normed = grad_normed[:count] + swapped.astype(F32)
    grad_mid = upstream + norm_rows_back(hidden_one, gains[1], inverse_two, grad_normed)
    down_far = partner(after(down_sum[count:].astype(BF), swapped))
    down_z = down_sum[:count] + down_far.astype(F32)
    layer_out = from_tokens((hidden_one + down_z * scales[DOWN]).astype(BF))

    def first_grads(rows, inputs, narrow, middle, factors, many):
        size = many * RANK
        parts = jnp.concatenate(two_parts(narrow), axis=1)
        product = fold_parts(t_mm(parts, inputs), size)
        same = jnp.arange(size)[:, None] // RANK == jnp.arange(size)[None, :] // RANK
        middle = jnp.where(same, middle[:, :size], 0.0)
        term = fold_parts(mm_t(jnp.concatenate(two_parts(middle)), factors), size)
        return product + 2.0 * (fold_parts(rows, size) + 2.0 * term)

    def twice(cols):
        return jnp.concatenate([cols, cols], axis=1)

    out_rows, scale_out, outer_out, narrow_out, middle_out = grad_terms(
        grad_mid, output_z, scales[OUT], slopes[OUT], outers[3], 3 * RANK, reduced_out
    )
    back_out = slot_back(place, out_rows, [ordered(out_slots[k]) for k in range(2)])
    grad_mixed, first_out = finish_back(
        [back_out], [RANK], narrow_out, middle_out, low_main, attended, 3 * RANK
    )
    grad_mixed = grad_mixed.astype(BF)

    query_grad, kv_grad = attend_back(
        first_block, queries, cosine, sine, place_rows, start_rows, kv, kvt, log_total, attended,
        grad_mixed,
    )
    kv_grad = kv_grad.reshape(CHUNKS, wide_count, block, KVH * 2 * HD)
    kv_grad = after(jnp.swapaxes(kv_grad, 0, 1).astype(F32), layer_out)
    bits = bits_of(wide_count)
    kv_half = KVH * HD
    kv_grad = jnp.concatenate(
        [
            scatter_sum(kv_grad[..., :kv_half], "wide", BF),
            scatter_sum(kv_grad[..., kv_half:], "wide", BF, [bits[-2], *bits[:-2], bits[-1]]),
        ],
        axis=-1,
    )
    kv_grad = kv_grad.reshape(count, KVH, 2 * HD)
    key_grad = turn(kv_grad[:, :, :HD].reshape(count, -1), cosine[:, :HD], -sine[:, :HD])
    value_grad = kv_grad[:, :, HD:].reshape(count, -1)

    query_rows_low, scale_query, outer_query, narrow_query, middle_query = grad_terms(
        query_grad, query_z, scales[QUERY], slopes[QUERY], outers[0], 0, reduced_one
    )
    back_query = slot_back(place, query_rows_low, [ordered(query_slots[k]) for k in range(2)])
    kv_rows_low, scale_kv, outer_kv_grad, narrow_kv, middle_kv = grad_terms(
        jnp.concatenate([key_grad, value_grad], axis=1), kv_z, scales[KV], slopes[KV], outer_kv,
        RANK, reduced_one,
    )
    back_kv = slot_back(place, kv_rows_low, [ordered(kv_slots[k]) for k in range(2)])
    grad_normed, first_one = finish_back(
        [back_query, back_kv],
        [RANK, pairs],
        narrow_query + narrow_kv,
        jnp.concatenate([middle_query, middle_kv]),
        low_main,
        normed_one,
        0,
    )
    grad_tokens = from_tokens(
        (grad_mid + norm_rows_back(residual, gains[0], inverse_one, grad_normed)).astype(BF)
    )

    scale_down = jnp.sum(upstream * down_z, axis=0, keepdims=True)
    pair_down = scale_down + partner(scale_down)
    weighted = (pair_down * slopes[DOWN]) * outers[6]
    middle_down = gram_of(weighted, outers[6])
    weighted_parts = jnp.pad(jnp.concatenate(two_parts(weighted)), ((0, 0), (0, EXTRA)))
    first_down = [
        first_grads(
            mm_t(weighted_parts, down_weights[k]), blocks[k][0], narrow_down, middle_down,
            down_weights[k][:, D : D + RANK], 1,
        )
        for k in range(2)
    ]
    outer_down = 2.0 * fold_parts(
        t_mm(jnp.concatenate(two_parts(reduced_down), axis=1), down_low), RANK
    )
    of_keys = (jnp.arange(2 * kv_cols) < kv_cols)[None, :]
    outer_kv_grad = jnp.where(of_keys, outer_kv_grad[:RANK], outer_kv_grad[RANK:])
    crosses = [soon_cross, rest_cross]
    cross_own = all_sum(after(jnp.concatenate(crosses, axis=1), down_z), ["wide"])
    cross_by = [cross_own, other_core(cross_own)]

    def second_grads(product, sums, slope, norm, cross):
        return jnp.concatenate([product + 2.0 * (sums * slope) * cross, sums / norm])

    plain = {
        n: second_grads(
            product, sums, slopes[n], norms[n], in_order([cut(c, n) for c in cross_by])
        )
        for n, product, sums in (
            (KV, outer_kv_grad, scale_kv),
            (QUERY, outer_query, scale_query),
            (OUT, outer_out, scale_out),
            (DOWN, outer_down, scale_down),
        )
    }
    eights = [
        jnp.pad(
            second_grads(
                blocks[k][3], blocks[k][2], slope_by[k][MLP], norms_by[k][MLP], cut(cross_by[k], MLP)
            ),
            ((0, 7), (0, 0)),
        )
        for k in range(2)
    ]
    gate_grads, up_grads = spread_pair(quarter, *eights, part)
    outer_cols = jnp.concatenate(
        [
            plain[QUERY],
            plain[KV],
            plain[OUT],
            gate_grads[: RANK + 1],
            up_grads[: RANK + 1],
            plain[DOWN],
        ],
        axis=1,
    )
    main_rows = jnp.concatenate([first_one, first_out, first_pairs])
    down_rows = jnp.zeros((RANK, wide_count, 4, part), F32)
    for k in range(2):
        down_rows = lax.dynamic_update_slice(
            down_rows,
            first_down[k].reshape(RANK, wide_count, 1, part),
            (0, 0, quarter[0] ^ k, 0),
        )
    down_rows = down_rows.reshape(RANK, FF)

    main_width = 6 * RANK // tok_count
    down_width = RANK // tok_count
    outer_share = OUTS // (tok_count * wide_count)

    def to_owner(rows, tok_rows, wide_cols):
        shaped = rows.reshape(tok_count, tok_rows, wide_count, wide_cols)
        summed = scatter_sum(shaped, "tok")
        return scatter_sum(jnp.swapaxes(summed, 0, 1), "wide")

    main_part = to_owner(main_rows, main_width, share).T
    down_part = to_owner(down_rows, down_width, hidden_share).T
    outer_blocks = jnp.moveaxis(
        outer_cols.reshape(RANK + 1, tok_count, wide_count, outer_share), 0, 2
    )
    outer_sum = scatter_sum(scatter_sum(outer_blocks, "tok"), "wide")
    outer_part = outer_sum[:RANK]
    block_start = (tok * wide_count + wide) * outer_share
    mag_part = outer_sum[RANK]

    local_squares = (
        squared_sum(main_part)
        + squared_sum(down_part)
        + squared_sum(outer_part)
        + squared_sum(mag_part)
    )
    grad_total = all_sum(jnp.full((8, 128), local_squares), ["tok", "wide"])[0, 0]
    grad_norm = jnp.sqrt(grad_total)
    clip_factor = CLIP_MAX / jnp.maximum(grad_norm, CLIP_MAX)
    main_param = lax.dynamic_slice_in_dim(adapt_main, tok * main_width, main_width, 1)
    down_param = lax.dynamic_slice_in_dim(adapt_down, tok * down_width, down_width, 1)
    outer_param = lax.dynamic_slice_in_dim(adapt_outer, block_start, outer_share, 1)
    mag_param = lax.dynamic_slice_in_dim(magnitudes, block_start, outer_share, 0)
    main_new, main_first_new, main_second_new = adam(
        main_param, main_part, main_first, main_second, RATE_ADAPT, clip_factor
    )
    down_new, down_first_new, down_second_new = adam(
        down_param, down_part, down_first, down_second, RATE_ADAPT, clip_factor
    )
    outer_new, outer_first_new, outer_second_new = adam(
        outer_param, outer_part, outer_first, outer_second, RATE_OUTER, clip_factor
    )
    mag_new, mag_first_new, mag_second_new = adam(
        mag_param, mag_part, mag_first, mag_second, RATE_MAGNITUDE, clip_factor
    )
    mag_clipped = mag_part * clip_factor
    return (
        layer_out,
        grad_tokens,
        grad_norm,
        main_new,
        main_first_new,
        main_second_new,
        down_new,
        down_first_new,
        down_second_new,
        outer_new,
        outer_first_new,
        outer_second_new,
        mag_new,
        mag_clipped,
        mag_second_new,
    )


def solution(mesh):
    return jax.shard_map(
        shards,
        mesh=mesh,
        in_specs=(
            P("tok", "wide"),
            P("tok", "wide"),
            P("wide"),
            P("wide"),
            P("wide", None),
            P("wide", None),
            P("wide", None),
            P("wide", None),
            P("wide", None),
            P("wide", None),
            P("wide", None),
            P("wide", None),
            P("wide", None),
            P(),
            P(),
            P("wide", "tok"),
            P("wide", "tok"),
            P("wide", "tok"),
            P("wide", "tok"),
            P(None, ("tok", "wide")),
            P(None, ("tok", "wide")),
            P(("tok", "wide")),
            P(("tok", "wide")),
            P("tok", None),
        ),
        out_specs=(
            P("tok", "wide"),
            P("tok", "wide"),
            P(),
            P("wide", "tok"),
            P("wide", "tok"),
            P("wide", "tok"),
            P("wide", "tok"),
            P("wide", "tok"),
            P("wide", "tok"),
            P(None, ("tok", "wide")),
            P(None, ("tok", "wide")),
            P(None, ("tok", "wide")),
            P(("tok", "wide")),
            P(("tok", "wide")),
            P(("tok", "wide")),
        ),
        check_vma=False,
    )
```

time: 1430 us -> 972 us (0.68)
  matrix products: 351 us -> 64.8 us
  Pallas kernels: 0 us -> 170 us
  local copies, waits for them, and re-layouts: 306 us -> 144 us
  waiting for transfers between devices: 463 us -> 333 us
  other arithmetic: 185 us -> 79.2 us
  starting transfers between devices: 100 us -> 157 us
    dot_general x37 -> x1, matrix products: 196 us -> 1.22 us  [gram_of(): lax.dot_general(left, right, (((1,), (1,)), ((), ())), precision=PRECISE)]
    pallas_call x0 -> x19, Pallas kernels: none -> 170 us  [the longest x2 53.8 us: mlp_block(): pl.pallas_call(functools.partial(mlp_kernel, offset=offset), grid_spec=pl...]
    ppermute x110 -> x141, waiting for transfers between devices: 463 us -> 333 us  [swap(): return lax.ppermute(array, axis, [(i, i ^ distance) for i in range(count)])]
    dynamic_update_slice x60 -> x44, local copies, waits for them, and re-layouts: 103 us -> 23.5 us  [the longest x16 9.34 us: put_rows(): whole = lax.dynamic_update_slice(whole, held, ((index ^ slot) * rows, 0))]
    convert_element_type x8 -> x3, other arithmetic: 64.9 us -> 3.99 us  [the longest x1 2.58 us: shards(): kv_grad = after(jnp.swapaxes(kv_grad, 0, 1).astype(F32), layer_out)]
    ppermute x110 -> x141, starting transfers between devices: 100 us -> 157 us  [swap(): return lax.ppermute(array, axis, [(i, i ^ distance) for i in range(count)])]
    dot_general x13 -> x3, matrix products: 56.8 us -> 18 us  [mm(): return jnp.dot(left, right, preferred_element_type=F32)]
    dot_general x15 -> x21, matrix products: 80.4 us -> 42.4 us  [mm_t(): lax.dot_general(left, right, (((1,), (1,)), ((), ())), preferred_element_...]
  transfers between devices with their start and end apart: 110 -> 141, of which waited for: 62 -> 59; matrix products, arithmetic and copies ran while one was open for 39% -> 20% of each run, Pallas kernels for 0% -> 13%
where the time goes in v2:
time: 972 us; the launch traced here: 960 us
  waiting for transfers between devices  333 us (34%)
  Pallas kernels  170 us (17%)
  starting transfers between devices  157 us (16%)
  local copies, waits for them, and re-layouts  144 us (15%)
  other arithmetic  79.2 us (8%)
  matrix products  64.8 us (7%)
  between operations  10.7 us (1%)
    ppermute x141, waiting for transfers between devices, swap(): return lax.ppermute(array, axis, [(i, i ^ distance) for i in range(count)])  333 us
    ppermute x141, starting transfers between devices, swap(): return lax.ppermute(array, axis, [(i, i ^ distance) for i in range(count)])  157 us
    pallas_call x2, Pallas kernels, mlp_block(): pl.pallas_call(functools.partial(mlp_kernel, offset=offset), grid_spec=pl...  53.8 us
    unnamed x618, local copies, waits for them, and re-layouts  53.7 us
    dot_general x21, matrix products, mm_t(): lax.dot_general(left, right, (((1,), (1,)), ((), ())), preferred_element_...  42.4 us
    pallas_call x1, Pallas kernels, attend_back(): pl.pallas_call(functools.partial(backward_kernel, block=block, span=span,...  23.3 us
    pallas_call x3, Pallas kernels, slot_mm(): pl.pallas_call(functools.partial(slot_kernel, offset=offset), grid_spec=p...  20.3 us
    pallas_call x3, Pallas kernels, slot_back(): pl.pallas_call(slot_back_kernel, grid_spec=pltpu.PrefetchScalarGridSpec(n...  19.6 us
  transfers between devices with their start and end apart: 141, of which 59 were waited for; matrix products, arithmetic and copies ran while one was open for 20% of the time, Pallas kernels for 13%

profile of v2, /device:TPU:0, one launch (start us, length us, event | category | flops | bytes accessed | tf_op | source)
XLA Modules:
  0.0 959.6 jit_solution(5946853154624055840)
XLA Ops:
  67.1 6.4 collective-permute-start.5
  92.0 13.8 %shard_map.347 = (bf16[256,1024]{1,0:T(8,128)(2,1)}, bf16[256,2816]{1,0:T(8,128)(2,1)}, bf16[176,2176]{1,0:T(8,128)(2,1)S(1)}, f32[1,4864]{1,0:T(1,128)S(1)}, f3...) custom-call(s32[3]{0:T(128)S(1)} %copy-done.172, bf16[256,2048]{1,0:T(8,128)(2,1)S(1)} %copy-done.121, ...), custom_call_target="tpu_custom_call" | custom-call | flops 1024 | bytes 1024 | tf_op jit(solution)/shard_map/pallas_call | solution.py:1062
  124.3 5.4 collective-permute-done.13.refs_3_
  139.6 5.5 collective-permute-done.16.refs_7_
  160.2 5.8 collective-permute-done.44
  170.5 9.0 collective-permute-done.46
  188.6 10.9 %collective-permute-done.54.refs_4_ = bf16[256,1024]{1,0:T(8,128)(2,1)S(1)} collective-permute-done((bf16[256,1024]{1,0:T(8,128)(2,1)}, bf16[256,1024]{1,0:T(8,128)(2,1)S(1)}, u32[]{:S(2)}, u32[]{:S(2)}) %collective-permute-start.54) | collective-permute-done | bytes 524320 | tf_op jit(solution)/shard_map/ppermute | solution.py:50
  219.4 15.2 %collective-permute-done.47 = bf16[8,1,32,512]{3,2,0,1:T(8,128)(2,1)S(1)} collective-permute-done((bf16[8,1,32,512]{3,2,0,1:T(8,128)(2,1)S(1)}, bf16[8,1,32,512]{3,2,0,1:T(8,128)(2,1)S(1)}, u32[]{:S(2)}, u32[]{:S(2)}) %collective-permute-start.47) | collective-permute-done | bytes 262176 | tf_op jit(solution)/shard_map/ppermute | solution.py:50
  240.2 5.6 collective-permute-done.50
  259.9 9.5 collective-permute-done.72
  273.4 34.4 %collective-permute-done.73 = bf16[256,512]{1,0:T(8,128)(2,1)S(1)} collective-permute-done((bf16[256,512]{1,0:T(8,128)(2,1)S(1)}, bf16[256,512]{1,0:T(8,128)(2,1)S(1)}, u32[]{:S(2)}, u32[]{:S(2)}) %collective-permute-start.73) | collective-permute-done | bytes 262176 | tf_op jit(solution)/shard_map/ppermute | solution.py:50
  315.1 10.0 %collective-permute-done.76 = bf16[176,2176]{1,0:T(8,128)(2,1)S(1)} collective-permute-done((bf16[176,2176]{1,0:T(8,128)(2,1)S(1)}, bf16[176,2176]{1,0:T(8,128)(2,1)S(1)}, u32[]{:S(2)}, u32[]{:S(2)}) %collective-permute-start.76) | collective-permute-done | bytes 765984 | tf_op jit(solution)/shard_map/ppermute | solution.py:50
  336.4 19.0 %collective-permute-done.81 = bf16[176,2176]{1,0:T(8,128)(2,1)S(1)} collective-permute-done((bf16[176,2176]{1,0:T(8,128)(2,1)S(1)}, bf16[176,2176]{1,0:T(8,128)(2,1)S(1)}, u32[]{:S(2)}, u32[]{:S(2)}) %collective-permute-start.81) | collective-permute-done | bytes 765984 | tf_op jit(solution)/shard_map/ppermute | solution.py:50
  361.6 25.7 %collective-permute-done.57.refs_7_ = bf16[256,1024]{1,0:T(8,128)(2,1)S(1)} collective-permute-done((bf16[256,1024]{1,0:T(8,128)(2,1)S(1)}, bf16[256,1024]{1,0:T(8,128)(2,1)S(1)}, u32[]{:S(2)}, u32[]{:S(2)}) %collective-permute-start.57) | collective-permute-done | bytes 524320 | tf_op jit(solution)/shard_map/ppermute | solution.py:50
  387.8 11.6 %collective-permute-done.86.refs_4_ = bf16[256,2816]{1,0:T(8,128)(2,1)} collective-permute-done((bf16[256,2816]{1,0:T(8,128)(2,1)}, bf16[256,2816]{1,0:T(8,128)(2,1)}, u32[]{:S(2)}, u32[]{:S(2)}) %collective-permute-start.86) | collective-permute-done | bytes 1441824 | tf_op jit(solution)/shard_map/ppermute | solution.py:50
  423.8 9.0 shard_map.344
  432.9 19.1 %shard_map.346 = (bf16[256,2048]{1,0:T(8,128)(2,1)S(1)}, bf16[256,2048]{1,0:T(8,128)(2,1)S(1)}, f32[4,8,1,256]{3,2,1,0:T(1,128)S(1)}) custom-call(s32[8]{0:T(128)S(1)} %copy-done.190, f32[256,2048]{1,0:T(8,128)S(1)} %get-tuple-element.82.z_ref, f32[1,2048]{1,0:T(1,128)S(1)} %broadcast_select_fusion.7.scale_ref, f32[256,128]{1,0:T(8,128)S(1)} %copy.367.cos_ref, ...), custom_call_target="tpu_custom_call" | custom-call | flops 1024 | bytes 1024 | tf_op jit(solution)/shard_map/pallas_call | solution.py:397
  452.2 7.8 shard_map.348
  476.9 15.0 %collective-permute-done.70 = bf16[256,2048]{1,0:T(8,128)(2,1)} collective-permute-done((bf16[256,2048]{1,0:T(8,128)(2,1)}, bf16[256,2048]{1,0:T(8,128)(2,1)}, u32[]{:S(2)}, u32[]{:S(2)}) %collective-permute-start.70) | collective-permute-done | bytes 1048608 | tf_op jit(solution)/shard_map/ppermute | solution.py:50
  497.7 30.2 %collective-permute-done.89.refs_7_ = bf16[256,2816]{1,0:T(8,128)(2,1)} collective-permute-done((bf16[256,2816]{1,0:T(8,128)(2,1)}, bf16[256,2816]{1,0:T(8,128)(2,1)}, u32[]{:S(2)}, u32[]{:S(2)}) %collective-permute-start.89) | collective-permute-done | bytes 1441824 | tf_op jit(solution)/shard_map/ppermute | solution.py:50
  527.9 26.7 %shard_map.349 = (bf16[512,1408]{1,0:T(8,128)(2,1)S(1)}, bf16[576,2816]{1,0:T(8,128)(2,1)}, f32[1,2816]{1,0:T(1,128)S(1)}, f32[16,2816]{1,0:T(8,128)S(1)}, f32[5...) custom-call(s32[3]{0:T(128)S(1)} %copy-done.174, bf16[512,2048]{1,0:T(8,128)(2,1)} %pad_maximum_fusion.inputs_ref.refs_5_, ...), custom_call_target="tpu_custom_call" | custom-call | flops 1024 | bytes 1024 | tf_op jit(solution)/shard_map/pallas_call | solution.py:820
  581.8 27.1 %shard_map.350 = (bf16[512,1408]{1,0:T(8,128)(2,1)S(1)}, bf16[576,2816]{1,0:T(8,128)(2,1)}, f32[1,2816]{1,0:T(1,128)S(1)}, f32[16,2816]{1,0:T(8,128)S(1)}, f32[5...) custom-call(s32[3]{0:T(128)S(1)} %copy-done.174, bf16[512,2048]{1,0:T(8,128)(2,1)} %pad_maximum_fusion.inputs_ref.refs_5_, ...), custom_call_target="tpu_custom_call" | custom-call | flops 1024 | bytes 1024 | tf_op jit(solution)/shard_map/pallas_call | solution.py:820
  626.0 5.2 shard_map.351
  633.0 6.5 fusion.136
  639.6 8.3 convolution_add_fusion
  666.1 18.9 %collective-permute-done.101 = bf16[256,2048]{1,0:T(8,128)(2,1)S(1)} collective-permute-done((bf16[256,2048]{1,0:T(8,128)(2,1)S(1)}, bf16[256,2048]{1,0:T(8,128)(2,1)S(1)}, u32[]{:S(2)}, u32[]{:S(2)}) %collective-permute-start.101) | collective-permute-done | bytes 1048608 | tf_op jit(solution)/shard_map/ppermute | solution.py:50
  696.5 8.1 shard_map.353.refs_0_
  708.5 23.3 %shard_map.355 = (f32[256,2048]{1,0:T(8,128)S(1)}, bf16[2048,512]{1,0:T(8,128)(2,1)S(1)}) custom-call(s32[8]{0:T(128)S(1)} %copy-done.191, bf16[256,2048]{1,0:T(8,128)(2,1)S(1)} %copy-done.124, f32[256,128]{1,0:T(8,128)S(1)} %copy.367.cos_ref, f32[256,128]{1,0:T(8,128)S(1)} %copy-done.108, s32[8,1,256]{2,1,0:T(1,128)S(1)} %copy-done.168, ...), custom_call_target="tpu_custom_call" | custom-call | flops 1024 | bytes 1024 | tf_op jit(solution)/shard_map/pallas_call | solution.py:440
  739.7 7.8 shard_map.357.refs_0_
  805.2 13.1 %collective-permute-done.129 = f32[16,6144]{1,0:T(8,128)S(1)} collective-permute-done((f32[16,6144]{1,0:T(8,128)S(1)}, f32[16,6144]{1,0:T(8,128)S(1)}, u32[]{:S(2)}, u32[]{:S(2)}) %collective-permute-start.129) | collective-permute-done | bytes 393248 | tf_op jit(solution)/shard_map/ppermute | solution.py:50
  822.7 6.2 collective-permute-done.110
  934.8 8.1 collective-permute-done.138
  (1231 shorter events, 520.6 us)
Async XLA Ops:
  9.6 76.3 %collective-permute-start.10 = (bf16[256,384]{1,0:T(8,128)(2,1)S(1)}, bf16[256,384]{1,0:T(8,128)(2,1)S(1)}, u32[]{:S(2)}, u32[]{:S(2)}) collective-permute-start(bf16[256,384]{1,0:T(8,128)(2,1)S(1)} %get-tuple-element.79.refs_0_), channel_id=1, source_target_pairs={{0,1},{1,0},{2,3},{3,2},{4,5},{5,4},{6,7},{7,6},{8,9},{9,8},{10,11... | collective-permute-start | bytes 589832 | tf_op jit(solution)/shard_map/ppermute | solution.py:50
  12.5 73.4 %collective-permute-start.11 = (bf16[256,384]{1,0:T(8,128)(2,1)S(1)}, bf16[256,384]{1,0:T(8,128)(2,1)}, u32[]{:S(2)}, u32[]{:S(2)}) collective-permute-start(bf16[256,384]{1,0:T(8,128)(2,1)S(1)} %get-tuple-element.79.refs_0_), channel_id=1, source_target_pairs={{0,2},{1,3},{2,0},{3,1},{4,6},{5,7},{6,4},{7,5},{8,10},{9,11},{10,... | collective-permute-start | bytes 589832 | tf_op jit(solution)/shard_map/ppermute | solution.py:50
  14.1 71.9 %collective-permute-start.12 = (bf16[256,384]{1,0:T(8,128)(2,1)S(1)}, bf16[256,384]{1,0:T(8,128)(2,1)}, u32[]{:S(2)}, u32[]{:S(2)}) collective-permute-start(bf16[256,384]{1,0:T(8,128)(2,1)S(1)} %get-tuple-element.79.refs_0_), channel_id=1, source_target_pairs={{0,4},{1,5},{2,6},{3,7},{4,0},{5,1},{6,2},{7,3},{8,12},{9,13},{10,... | collective-permute-start | bytes 589832 | tf_op jit(solution)/shard_map/ppermute | solution.py:50
  77.9 53.3 %collective-permute-start.36 = (bf16[256,384]{1,0:T(8,128)(2,1)S(1)}, bf16[256,384]{1,0:T(8,128)(2,1)S(1)}, u32[]{:S(2)}, u32[]{:S(2)}) collective-permute-start(bf16[256,384]{1,0:T(8,128)(2,1)S(1)} %get-tuple-element.79.refs_0_), channel_id=1, source_target_pairs={{0,8},{8,0},{16,24},{24,16},{1,9},{9,1},{17,25},{25,17},{2,10},{10... | collective-permute-start | bytes 589832 | tf_op jit(solution)/shard_map/ppermute | solution.py:50
  86.0 59.1 %collective-permute-start.17 = (bf16[256,1024]{1,0:T(8,128)(2,1)S(1)}, bf16[256,1024]{1,0:T(8,128)(2,1)S(1)}, u32[]{:S(2)}, u32[]{:S(2)}) collective-permute-start(bf16[256,1024]{1,0:T(8,128)(2,1)S(1)} %get-tuple-element.81.refs_0_), channel_id=1, source_target_pairs={{0,1},{1,0},{2,3},{3,2},{4,5},{5,4},{6,7},{7,6},{8,9},{9,8},{10,11... | collective-permute-start | bytes 1572872 | tf_op jit(solution)/shard_map/ppermute | solution.py:50
  88.0 57.6 %collective-permute-start.18 = (bf16[256,1024]{1,0:T(8,128)(2,1)S(1)}, bf16[256,1024]{1,0:T(8,128)(2,1)}, u32[]{:S(2)}, u32[]{:S(2)}) collective-permute-start(bf16[256,1024]{1,0:T(8,128)(2,1)S(1)} %get-tuple-element.81.refs_0_), channel_id=1, source_target_pairs={{0,2},{1,3},{2,0},{3,1},{4,6},{5,7},{6,4},{7,5},{8,10},{9,11},{10,... | collective-permute-start | bytes 1572872 | tf_op jit(solution)/shard_map/ppermute | solution.py:50
  90.1 55.6 %collective-permute-start.20 = (bf16[256,1024]{1,0:T(8,128)(2,1)S(1)}, bf16[256,1024]{1,0:T(8,128)(2,1)}, u32[]{:S(2)}, u32[]{:S(2)}) collective-permute-start(bf16[256,1024]{1,0:T(8,128)(2,1)S(1)} %get-tuple-element.81.refs_0_), channel_id=1, source_target_pairs={{0,4},{1,5},{2,6},{3,7},{4,0},{5,1},{6,2},{7,3},{8,12},{9,13},{10,... | collective-permute-start | bytes 1572872 | tf_op jit(solution)/shard_map/ppermute | solution.py:50
  208.3 37.7 %collective-permute-start.23 = (bf16[256,1024]{1,0:T(8,128)(2,1)S(1)}, bf16[256,1024]{1,0:T(8,128)(2,1)S(1)}, u32[]{:S(2)}, u32[]{:S(2)}) collective-permute-start(bf16[256,1024]{1,0:T(8,128)(2,1)S(1)} %collective-permute-done.22.refs_6_), channel_id=1, source_target_pairs={{0,1},{1,0},{2,3},{3,2},{4,5},{5,4},{6,7},{7,6},{8,9},{9,8},{10,11... | collective-permute-start | bytes 1572872 | tf_op jit(solution)/shard_map/ppermute | solution.py:50
  251.2 61.9 %collective-permute-start.55 = (bf16[256,1024]{1,0:T(8,128)(2,1)S(1)}, bf16[256,1024]{1,0:T(8,128)(2,1)S(1)}, u32[]{:S(2)}, u32[]{:S(2)}) collective-permute-start(bf16[256,1024]{1,0:T(8,128)(2,1)S(1)} %collective-permute-done.54.refs_4_), channel_id=1, source_target_pairs={{0,1},{1,0},{2,3},{3,2},{4,5},{5,4},{6,7},{7,6},{8,9},{9,8},{10,11... | collective-permute-start | bytes 1572872 | tf_op jit(solution)/shard_map/ppermute | solution.py:50
  252.8 60.4 %collective-permute-start.56 = (bf16[256,1024]{1,0:T(8,128)(2,1)S(1)}, bf16[256,1024]{1,0:T(8,128)(2,1)S(1)}, u32[]{:S(2)}, u32[]{:S(2)}) collective-permute-start(bf16[256,1024]{1,0:T(8,128)(2,1)S(1)} %collective-permute-done.54.refs_4_), channel_id=1, source_target_pairs={{0,2},{1,3},{2,0},{3,1},{4,6},{5,7},{6,4},{7,5},{8,10},{9,11},{10,... | collective-permute-start | bytes 1572872 | tf_op jit(solution)/shard_map/ppermute | solution.py:50
  253.7 60.1 %collective-permute-start.78 = (bf16[176,2176]{1,0:T(8,128)(2,1)S(1)}, bf16[176,2176]{1,0:T(8,128)(2,1)S(1)}, u32[]{:S(2)}, u32[]{:S(2)}) collective-permute-start(bf16[176,2176]{1,0:T(8,128)(2,1)S(1)} %copy-done.142), channel_id=1, source_target_pairs={{0,4},{1,5},{2,6},{3,7},{4,0},{5,1},{6,2},{7,3},{8,12},{9,13},{10,... | collective-permute-start | bytes 2297864 | tf_op jit(solution)/shard_map/ppermute | solution.py:50
  256.0 51.8 %collective-permute-start.73 = (bf16[256,512]{1,0:T(8,128)(2,1)S(1)}, bf16[256,512]{1,0:T(8,128)(2,1)S(1)}, u32[]{:S(2)}, u32[]{:S(2)}) collective-permute-start(bf16[256,512]{1,0:T(8,128)(2,1)S(1)} %bitcast.344), channel_id=1, source_target_pairs={{0,4},{1,5},{2,6},{3,7},{4,0},{5,1},{6,2},{7,3},{8,12},{9,13},{10,... | collective-permute-start | bytes 786440 | tf_op jit(solution)/shard_map/ppermute | solution.py:50
  269.4 39.7 %collective-permute-start.74 = (bf16[256,512]{1,0:T(8,128)(2,1)S(1)}, bf16[256,512]{1,0:T(8,128)(2,1)S(1)}, u32[]{:S(2)}, u32[]{:S(2)}) collective-permute-start(bf16[256,512]{1,0:T(8,128)(2,1)S(1)} %bitcast.343), channel_id=1, source_target_pairs={{0,6},{1,7},{2,4},{3,5},{4,2},{5,3},{6,0},{7,1},{8,14},{9,15},{10,... | collective-permute-start | bytes 786440 | tf_op jit(solution)/shard_map/ppermute | solution.py:50
  313.9 41.5 %collective-permute-start.81 = (bf16[176,2176]{1,0:T(8,128)(2,1)S(1)}, bf16[176,2176]{1,0:T(8,128)(2,1)S(1)}, u32[]{:S(2)}, u32[]{:S(2)}) collective-permute-start(bf16[176,2176]{1,0:T(8,128)(2,1)S(1)} %collective-permute-done.78), channel_id=1, source_target_pairs={{0,2},{1,3},{2,0},{3,1},{4,6},{5,7},{6,4},{7,5},{8,10},{9,11},{10,... | collective-permute-start | bytes 2297864 | tf_op jit(solution)/shard_map/ppermute | solution.py:50
  333.3 66.1 %collective-permute-start.86 = (bf16[256,2816]{1,0:T(8,128)(2,1)}, bf16[256,2816]{1,0:T(8,128)(2,1)}, u32[]{:S(2)}, u32[]{:S(2)}) collective-permute-start(bf16[256,2816]{1,0:T(8,128)(2,1)} %get-tuple-element.96.refs_0_), channel_id=1, source_target_pairs={{0,4},{1,5},{2,6},{3,7},{4,0},{5,1},{6,2},{7,3},{8,12},{9,13},{10,... | collective-permute-start | bytes 4325384 | tf_op jit(solution)/shard_map/ppermute | solution.py:50
  355.4 44.1 %collective-permute-start.82 = (bf16[176,2176]{1,0:T(8,128)(2,1)S(1)}, bf16[176,2176]{1,0:T(8,128)(2,1)S(1)}, u32[]{:S(2)}, u32[]{:S(2)}) collective-permute-start(bf16[176,2176]{1,0:T(8,128)(2,1)S(1)} %collective-permute-done.81), channel_id=1, source_target_pairs={{0,1},{1,0},{2,3},{3,2},{4,5},{5,4},{6,7},{7,6},{8,9},{9,8},{10,11... | collective-permute-start | bytes 2297864 | tf_op jit(solution)/shard_map/ppermute | solution.py:50
  361.3 40.9 %collective-permute-start.63 = (bf16[256,1024]{1,0:T(8,128)(2,1)S(1)}, bf16[256,1024]{1,0:T(8,128)(2,1)S(1)}, u32[]{:S(2)}, u32[]{:S(2)}) collective-permute-start(bf16[256,1024]{1,0:T(8,128)(2,1)S(1)} %collective-permute-done.55.refs_5_), channel_id=1, source_target_pairs={{0,8},{8,0},{16,24},{24,16},{1,9},{9,1},{17,25},{25,17},{2,10},{10... | collective-permute-start | bytes 1572872 | tf_op jit(solution)/shard_map/ppermute | solution.py:50
  399.5 63.2 %collective-permute-start.84 = (bf16[256,2816]{1,0:T(8,128)(2,1)}, bf16[256,2816]{1,0:T(8,128)(2,1)}, u32[]{:S(2)}, u32[]{:S(2)}) collective-permute-start(bf16[256,2816]{1,0:T(8,128)(2,1)} %get-tuple-element.96.refs_0_), channel_id=1, source_target_pairs={{0,2},{1,3},{2,0},{3,1},{4,6},{5,7},{6,4},{7,5},{8,10},{9,11},{10,... | collective-permute-start | bytes 4325384 | tf_op jit(solution)/shard_map/ppermute | solution.py:50
  399.5 63.3 %collective-permute-start.87 = (bf16[256,2816]{1,0:T(8,128)(2,1)}, bf16[256,2816]{1,0:T(8,128)(2,1)}, u32[]{:S(2)}, u32[]{:S(2)}) collective-permute-start(bf16[256,2816]{1,0:T(8,128)(2,1)} %collective-permute-done.86.refs_4_), channel_id=1, source_target_pairs={{0,1},{1,0},{2,3},{3,2},{4,5},{5,4},{6,7},{7,6},{8,9},{9,8},{10,11... | collective-permute-start | bytes 4325384 | tf_op jit(solution)/shard_map/ppermute | solution.py:50
  402.2 60.4 %collective-permute-start.75 = (bf16[256,2048]{1,0:T(8,128)(2,1)}, bf16[256,2048]{1,0:T(8,128)(2,1)}, u32[]{:S(2)}, u32[]{:S(2)}) collective-permute-start(bf16[256,2048]{1,0:T(8,128)(2,1)} %fusion.8), channel_id=1, source_target_pairs={{0,16},{8,24},{16,0},{24,8},{1,17},{9,25},{17,1},{25,9},{2,18},{10... | collective-permute-start | bytes 3145736 | tf_op jit(solution)/shard_map/ppermute | solution.py:50
  403.9 62.1 %collective-permute-start.83 = (bf16[256,2816]{1,0:T(8,128)(2,1)}, bf16[256,2816]{1,0:T(8,128)(2,1)}, u32[]{:S(2)}, u32[]{:S(2)}) collective-permute-start(bf16[256,2816]{1,0:T(8,128)(2,1)} %get-tuple-element.96.refs_0_), channel_id=1, source_target_pairs={{0,1},{1,0},{2,3},{3,2},{4,5},{5,4},{6,7},{7,6},{8,9},{9,8},{10,11... | collective-permute-start | bytes 4325384 | tf_op jit(solution)/shard_map/ppermute | solution.py:50
  405.8 176.0 %collective-permute-start.91 = (bf16[1408,2176]{1,0:T(8,128)(2,1)}, bf16[1408,2176]{1,0:T(8,128)(2,1)}, u32[]{:S(2)}, u32[]{:S(2)}) collective-permute-start(bf16[1408,2176]{1,0:T(8,128)(2,1)} %constant_dynamic-update-slice_fusion.8.first_ref.down_ref), channel_id=1, source_target_pairs={{0,8},{8,0},{16,24},{24,16},{1,9},{9,1},{17,25},{25,17},{2,10},{10... | collective-permute-start | bytes 18382856 | tf_op jit(solution)/shard_map/ppermute | solution.py:50
  462.6 35.1 %collective-permute-start.88 = (bf16[256,2816]{1,0:T(8,128)(2,1)}, bf16[256,2816]{1,0:T(8,128)(2,1)}, u32[]{:S(2)}, u32[]{:S(2)}) collective-permute-start(bf16[256,2816]{1,0:T(8,128)(2,1)} %collective-permute-done.86.refs_4_), channel_id=1, source_target_pairs={{0,2},{1,3},{2,0},{3,1},{4,6},{5,7},{6,4},{7,5},{8,10},{9,11},{10,... | collective-permute-start | bytes 4325384 | tf_op jit(solution)/shard_map/ppermute | solution.py:50
  462.8 65.1 %collective-permute-start.89 = (bf16[256,2816]{1,0:T(8,128)(2,1)}, bf16[256,2816]{1,0:T(8,128)(2,1)}, u32[]{:S(2)}, u32[]{:S(2)}) collective-permute-start(bf16[256,2816]{1,0:T(8,128)(2,1)} %collective-permute-done.87.refs_5_), channel_id=1, source_target_pairs={{0,2},{1,3},{2,0},{3,1},{4,6},{5,7},{6,4},{7,5},{8,10},{9,11},{10,... | collective-permute-start | bytes 4325384 | tf_op jit(solution)/shard_map/ppermute | solution.py:50
  491.9 62.7 %collective-permute-start.90 = (f32[16,2816]{1,0:T(8,128)}, f32[16,2816]{1,0:T(8,128)S(1)}, u32[]{:S(2)}, u32[]{:S(2)}) collective-permute-start(f32[16,2816]{1,0:T(8,128)} %slice.379.outer_ref), channel_id=1, source_target_pairs={{0,8},{8,0},{16,24},{24,16},{1,9},{9,1},{17,25},{25,17},{2,10},{10... | collective-permute-start | bytes 540680 | tf_op jit(solution)/shard_map/ppermute | solution.py:50
  497.0 69.7 %collective-permute-start.92 = (bf16[256,2816]{1,0:T(8,128)(2,1)}, bf16[256,2816]{1,0:T(8,128)(2,1)S(1)}, u32[]{:S(2)}, u32[]{:S(2)}) collective-permute-start(bf16[256,2816]{1,0:T(8,128)(2,1)} %get-tuple-element.96.refs_0_), channel_id=1, source_target_pairs={{0,8},{8,0},{16,24},{24,16},{1,9},{9,1},{17,25},{25,17},{2,10},{10... | collective-permute-start | bytes 4325384 | tf_op jit(solution)/shard_map/ppermute | solution.py:50
  497.7 69.7 %collective-permute-start.94 = (bf16[256,2816]{1,0:T(8,128)(2,1)}, bf16[256,2816]{1,0:T(8,128)(2,1)}, u32[]{:S(2)}, u32[]{:S(2)}) collective-permute-start(bf16[256,2816]{1,0:T(8,128)(2,1)} %collective-permute-done.84.refs_2_), channel_id=1, source_target_pairs={{0,8},{8,0},{16,24},{24,16},{1,9},{9,1},{17,25},{25,17},{2,10},{10... | collective-permute-start | bytes 4325384 | tf_op jit(solution)/shard_map/ppermute | solution.py:50
  527.9 38.9 %collective-permute-start.93 = (bf16[256,2816]{1,0:T(8,128)(2,1)}, bf16[256,2816]{1,0:T(8,128)(2,1)S(1)}, u32[]{:S(2)}, u32[]{:S(2)}) collective-permute-start(bf16[256,2816]{1,0:T(8,128)(2,1)} %collective-permute-done.83.refs_1_), channel_id=1, source_target_pairs={{0,8},{8,0},{16,24},{24,16},{1,9},{9,1},{17,25},{25,17},{2,10},{10... | collective-permute-start | bytes 4325384 | tf_op jit(solution)/shard_map/ppermute | solution.py:50
  689.1 87.8 %collective-permute-start.102 = (bf16[256,512]{1,0:T(8,128)(2,1)}, bf16[256,512]{1,0:T(8,128)(2,1)}, u32[]{:S(2)}, u32[]{:S(2)}) collective-permute-start(bf16[256,512]{1,0:T(8,128)(2,1)} %get-tuple-element.184), channel_id=1, source_target_pairs={{0,2},{1,3},{2,0},{3,1},{4,6},{5,7},{6,4},{7,5},{8,10},{9,11},{10,... | collective-permute-start | bytes 786440 | tf_op jit(solution)/shard_map/ppermute | solution.py:50
  689.2 89.4 %collective-permute-start.103 = (bf16[256,512]{1,0:T(8,128)(2,1)}, bf16[256,512]{1,0:T(8,128)(2,1)}, u32[]{:S(2)}, u32[]{:S(2)}) collective-permute-start(bf16[256,512]{1,0:T(8,128)(2,1)} %get-tuple-element.183), channel_id=1, source_target_pairs={{0,4},{1,5},{2,6},{3,7},{4,0},{5,1},{6,2},{7,3},{8,12},{9,13},{10,... | collective-permute-start | bytes 786440 | tf_op jit(solution)/shard_map/ppermute | solution.py:50
  689.2 93.9 %collective-permute-start.104 = (bf16[256,512]{1,0:T(8,128)(2,1)}, bf16[256,512]{1,0:T(8,128)(2,1)}, u32[]{:S(2)}, u32[]{:S(2)}) collective-permute-start(bf16[256,512]{1,0:T(8,128)(2,1)} %get-tuple-element.182), channel_id=1, source_target_pairs={{0,6},{1,7},{2,4},{3,5},{4,2},{5,3},{6,0},{7,1},{8,14},{9,15},{10,... | collective-permute-start | bytes 786440 | tf_op jit(solution)/shard_map/ppermute | solution.py:50
  735.7 53.7 %collective-permute-start.127 = (f32[16,6144]{1,0:T(8,128)}, f32[16,6144]{1,0:T(8,128)}, u32[]{:S(2)}, u32[]{:S(2)}) collective-permute-start(f32[16,6144]{1,0:T(8,128)} %pad_maximum_fusion.5), channel_id=1, source_target_pairs={{0,1},{1,0},{2,3},{3,2},{4,5},{5,4},{6,7},{7,6},{8,9},{9,8},{10,11... | collective-permute-start | bytes 1179656 | tf_op jit(solution)/shard_map/ppermute | solution.py:50
  (414 other events, 5462.8 us)

commit v3 on v2

--- a/solution.py
+++ b/solution.py
@@ -126,19 +126,26 @@
     return lax.optimization_barrier((value,) + others)[0]
 
 
-def gather_slots(shard, turned=False):
+def gather_slots(shard, turned=False, gate=None):
     slots = {0: shard}
     count = lax.axis_size("wide")
     for slot in sorted(range(1, count), key=lambda i: bin(i).count("1")):
         low = slot & -slot
         if turned and slot == count - 1:
             low = count // 4
-        slots[slot] = swap(slots[slot ^ low], "wide", low)
+        held = slots[slot ^ low]
+        if gate is not None and slot != low:
+            held = after(held, gate)
+        slots[slot] = swap(held, "wide", low)
     return slots
 
 
 def near(slots):
     return [held for slot, held in slots.items() if bin(slot).count("1") == 1]
+
+
+def far(slots, steps):
+    return [held for slot, held in slots.items() if bin(slot).count("1") == steps]
 
 
 def put_rows(slots, extra):
@@ -403,7 +410,7 @@
             jax.ShapeDtypeStruct((KVH, CHUNKS, 1, rows), F32),
         ],
         compiler_params=pltpu.CompilerParams(vmem_limit_bytes=40 << 20),
-        cost_estimate=pl.CostEstimate(flops=COST, bytes_accessed=COST, transcendentals=0),
+        cost_estimate=pl.CostEstimate(flops=40 << 30, bytes_accessed=64 << 20, transcendentals=0),
     )(first_block, z, scale, cosine, sine, places, starts, kv, kvt)
 
 
@@ -445,7 +452,7 @@
             jax.ShapeDtypeStruct((length, KVH * 2 * HD), BF),
         ],
         compiler_params=pltpu.CompilerParams(vmem_limit_bytes=40 << 20),
-        cost_estimate=pl.CostEstimate(flops=COST, bytes_accessed=COST, transcendentals=0),
+        cost_estimate=pl.CostEstimate(flops=40 << 30, bytes_accessed=64 << 20, transcendentals=0),
     )(first_block, queries, cosine, sine, places, starts, kv, kvt, log_total, attended, grads)
 
 
@@ -506,14 +513,14 @@
             total(slots[half * each : (half + 1) * each])
 
 
-def slot_mm(place, inputs, first, outer, offset, slots, tile=256):
+def slot_mm(place, inputs, first, outer, offset, slots, skip=0, tile=256):
     rows = slots[0][0].shape[0]
     cols = outer.shape[1]
     tiles = cols // 2 // tile
 
     def held(half):
         def spot(h, n, s):
-            return (0, jnp.where(h == half, n, (tiles - 1) * (1 - half)))
+            return (0, skip // tile + jnp.where(h == half, n, (tiles - 1) * (1 - half)))
 
         return pl.BlockSpec((rows, tile), spot)
 
@@ -597,12 +604,12 @@
     )(*raws, narrow, middle, first, inputs)
 
 
-def slot_back_kernel(place_ref, grad_ref, *refs):
+def slot_back_kernel(place_ref, grad_ref, *refs, skip):
     slots, out_ref, held, arrived = refs[:-3], refs[-3], refs[-2], refs[-1]
     each = len(slots) // 2
     rows, cols = held.shape[1:]
     copies = [
-        pltpu.make_async_copy(ref.at[:, pl.ds(0, cols)], held.at[slot], arrived.at[slot])
+        pltpu.make_async_copy(ref.at[:, pl.ds(skip, cols)], held.at[slot], arrived.at[slot])
         for slot, ref in enumerate(slots)
     ]
     for slot in range(each):
@@ -620,12 +627,12 @@
         ) + lax.dot_general(grads[1], held[each + slot], NT, preferred_element_type=F32)
 
 
-def slot_back(place, grads, slots):
+def slot_back(place, grads, slots, skip=0):
     rows = slots[0][0].shape[0]
     count, cols = grads.shape
     many = 2 * len(slots[0])
     return pl.pallas_call(
-        slot_back_kernel,
+        functools.partial(slot_back_kernel, skip=skip),
         grid_spec=pltpu.PrefetchScalarGridSpec(
             num_scalar_prefetch=1,
             grid=(1,),
@@ -641,14 +648,6 @@
         compiler_params=pltpu.CompilerParams(vmem_limit_bytes=40 << 20),
         cost_estimate=pl.CostEstimate(flops=COST, bytes_accessed=COST, transcendentals=0),
     )(place, grads, *slots[0], *slots[1])
-
-
-def slot_back_wide(place, grads, slots):
-    rows = slots[0].shape[0]
-    out = jnp.zeros((grads.shape[0], len(slots) * rows), F32)
-    for slot, held in enumerate(slots):
-        out = lax.dynamic_update_slice(out, mm_t(grads, held), (0, (place[0] ^ slot) * rows))
-    return out
 
 
 def pad_to(rows, count):
@@ -734,20 +733,39 @@
     )(grads, z, scale, slope, outer, reduced)
 
 
+def pack_kernel(inputs_ref, first_ref, out_ref, turned_ref, *, offset, rank):
+    reduced = jnp.dot(inputs_ref[...], first_ref[...], preferred_element_type=F32)
+    high, low = split_parts(reduced)
+    pick = lambda part: part.astype(F32)[:, offset : offset + rank]
+    count = inputs_ref.shape[0]
+    packed = jnp.concatenate(
+        [pick(high), pick(low), jnp.zeros((count, EXTRA - 2 * rank), F32)], axis=1
+    )
+    out_ref[...] = packed.astype(BF)
+    turned_ref[...] = packed.T.astype(BF)
+
+
+def pack_reduced(inputs, first, offset, rank):
+    count = inputs.shape[0]
+    return pl.pallas_call(
+        functools.partial(pack_kernel, offset=offset, rank=rank),
+        out_shape=[
+            jax.ShapeDtypeStruct((count, EXTRA), BF),
+            jax.ShapeDtypeStruct((EXTRA, count), BF),
+        ],
+        cost_estimate=pl.CostEstimate(flops=COST, bytes_accessed=COST, transcendentals=0),
+    )(inputs, first)
+
+
 def mlp_kernel(
-    place_ref, inputs_ref, main_ref, scale_ref, slope_ref, outer_ref,
+    place_ref, inputs_ref, packed_ref, turned_ref, scale_ref, slope_ref, outer_ref,
     down_grad_ref, narrow_down_ref, first_ref, down_ref, *refs, offset,
 ):
-    slots, kept = refs[:-7], refs[-7:]
-    hidden_ref, rows_ref, sum_ref, product_ref, narrow_ref, middle_ref, reduced_ref = kept
+    slots, kept = refs[:-8], refs[-8:]
+    hidden_ref, rows_ref, sum_ref, product_ref, narrow_ref, middle_ref, z_ref, back_ref = kept
     rows = slots[0].shape[0]
     half = hidden_ref.shape[1]
     count = hidden_ref.shape[0]
-
-    @pl.when(pl.program_id(0) == 0)
-    def _():
-        reduced_ref[...] = jnp.dot(inputs_ref[...], main_ref[...], preferred_element_type=F32)
-
     gate_lanes = lax.broadcasted_iota(jnp.int32, (RANK, 2 * half), 1) < half
     outer = jnp.concatenate(
         [
@@ -756,43 +774,65 @@
         ],
         axis=0,
     )
-    z = low_rank(reduced_ref[...], outer, offset)
+    rank = outer.shape[0]
+    doubled = 2.0 * outer.astype(BF).astype(F32)
+    pad = jnp.zeros((EXTRA - 2 * rank, 2 * half), F32)
+    z = jnp.dot(
+        packed_ref[...],
+        jnp.concatenate([doubled, doubled, pad], axis=0).astype(BF),
+        preferred_element_type=F32,
+    )
     for slot, ref in enumerate(slots):
         z = z + jnp.dot(
             inputs_ref[:, pl.ds(place_of(place_ref, slot, rows), rows)],
             ref[...],
             preferred_element_type=F32,
         )
-    grad_hidden = lax.dot_general(
+    z_ref[...] = z
+    back_ref[...] = lax.dot_general(
         down_grad_ref[...], down_ref[...], NT, preferred_element_type=F32
     ) + lax.dot_general(narrow_down_ref[...], first_ref[...], NT, preferred_element_type=F32)
     scale = scale_ref[...]
-    gate_z, up_z = z[:, :half], z[:, half:]
-    gate = gate_z * scale[:, :half]
-    up = up_z * scale[:, half:]
-    sigmoid = 1.0 / (1.0 + jnp.exp(-gate))
-    silu = gate * sigmoid
-    hidden_ref[...] = (silu * up).astype(BF)
-    grad_up = grad_hidden * silu
-    grad_gate = grad_hidden * up * (sigmoid * (1.0 + gate * (1.0 - sigmoid)))
+    step = 64
+    gate_sums = jnp.zeros((8, half), F32)
+    up_sums = jnp.zeros((8, half), F32)
+
+    def eighth(values):
+        return jnp.sum(values.reshape(step // 8, 8, half), axis=0)
+
+    for begin in range(0, count, step):
+        at = slice(begin, begin + step)
+        gate_z, up_z = z_ref[at, :half], z_ref[at, half:]
+        grad_hidden = back_ref[at, :]
+        gate = gate_z * scale[:, :half]
+        up = up_z * scale[:, half:]
+        sigmoid = 0.5 * jnp.tanh(0.5 * gate) + 0.5
+        silu = gate * sigmoid
+        hidden_ref[at, :] = (silu * up).astype(BF)
+        grad_up = grad_hidden * silu
+        grad_gate = grad_hidden * up * (sigmoid + silu * (1.0 - sigmoid))
+        gate_sums = gate_sums + eighth(grad_gate * gate_z)
+        up_sums = up_sums + eighth(grad_up * up_z)
+        rows_ref[at, :half] = (grad_gate * scale[:, :half]).astype(BF)
+        rows_ref[at, half:] = (grad_up * scale[:, half:]).astype(BF)
     sums = jnp.concatenate(
         [
-            jnp.sum(grad_gate * gate_z, axis=0, keepdims=True),
-            jnp.sum(grad_up * up_z, axis=0, keepdims=True),
+            jnp.sum(gate_sums, axis=0, keepdims=True),
+            jnp.sum(up_sums, axis=0, keepdims=True),
         ],
         axis=1,
     )
     sum_ref[...] = sums
-    low = jnp.concatenate(
-        [(grad_gate * scale[:, :half]).astype(BF), (grad_up * scale[:, half:]).astype(BF)], axis=1
-    )
-    rank = outer.shape[0]
+    low = rows_ref[:count, :]
     weighted = (sums * slope_ref[...]) * outer
     high_part, low_part = split_rows(weighted)
-    rows_ref[:count, :] = low
     rows_ref[count : count + rank, :] = high_part
     rows_ref[count + rank :, :] = low_part
-    narrow, middle, product = terms_of(low, weighted, outer, reduced_ref[...], offset)
+    placed = set_rows(outer, offset)
+    narrow = 2.0 * lax.dot_general(low, placed.astype(BF), NT, preferred_element_type=F32)
+    middle = lax.dot_general(weighted, placed, NT, precision=PRECISE, preferred_element_type=F32)
+    both = jnp.dot(turned_ref[...], low, preferred_element_type=F32)
+    product = 2.0 * (both[:rank] + both[rank : 2 * rank])
     product_ref[:, :half] = product[: rank // 2, :half]
     product_ref[:, half:] = product[rank // 2 :, half:]
 
@@ -808,14 +848,16 @@
 
 
 def mlp_block(
-    place, inputs, first, offset, scale, slope, outer, down_grad, narrow_down, down, slots
+    place, inputs, packs, offset, scale, slope, outer, down_grad, narrow_down, down, slots, start
 ):
     rows, cols = slots[0].shape
     count = inputs.shape[0]
     rank = 2 * RANK
     tile = 256
+    skip = start // tile
     fixed = lambda array: pl.BlockSpec(array.shape, lambda n, s: (0, 0))
     tiled = lambda rows: pl.BlockSpec((rows, tile), lambda n, s: (0, n))
+    late = lambda rows: pl.BlockSpec((rows, tile), lambda n, s: (0, n + skip))
     kept = lambda rows: pl.BlockSpec((rows, EXTRA), lambda n, s: (0, 0))
     return pl.pallas_call(
         functools.partial(mlp_kernel, offset=offset),
@@ -823,10 +865,10 @@
             num_scalar_prefetch=1,
             grid=(cols // tile,),
             in_specs=[
-                fixed(inputs), fixed(first), tiled(1), tiled(1), tiled(RANK), fixed(down_grad),
-                fixed(narrow_down),
-                pl.BlockSpec((tile // 2, 128), lambda n, s: (n, D // 128)),
-                pl.BlockSpec((tile // 2, D), lambda n, s: (n, 0)),
+                fixed(inputs), fixed(packs[0]), fixed(packs[1]), late(1), late(1), late(RANK),
+                fixed(down_grad), fixed(narrow_down),
+                pl.BlockSpec((tile // 2, 128), lambda n, s: (n + skip, D // 128)),
+                pl.BlockSpec((tile // 2, D), lambda n, s: (n + skip, 0)),
             ]
             + [tiled(rows) for _ in slots],
             out_specs=[
@@ -837,7 +879,10 @@
                 kept(count),
                 kept(rank),
             ],
-            scratch_shapes=[pltpu.VMEM((count, EXTRA), F32)],
+            scratch_shapes=[
+                pltpu.VMEM((count, tile), F32),
+                pltpu.VMEM((count, tile // 2), F32),
+            ],
         ),
         out_shape=[
             jax.ShapeDtypeStruct((count, cols // 2), BF),
@@ -849,42 +894,263 @@
         ],
         compiler_params=pltpu.CompilerParams(vmem_limit_bytes=48 << 20),
         cost_estimate=pl.CostEstimate(flops=COST, bytes_accessed=COST, transcendentals=0),
-    )(place, inputs, first, scale, slope, outer, down_grad, narrow_down, down, down, *slots)
-
-
-def spread_kernel(quarter_ref, own_ref, other_ref, gate_ref, up_ref, hold, *, part):
-    width = gate_ref.shape[1]
-    blocks = width // (4 * part)
-    for side, ref in enumerate((gate_ref, up_ref)):
-        ref[...] = jnp.zeros_like(ref)
-        for which, source in enumerate((own_ref, other_ref)):
-            for tile in range(blocks * part // 128):
-                hold[:, tile * 128 : (tile + 1) * 128] = source[
-                    :, (2 * tile + side) * 128 : (2 * tile + side + 1) * 128
-                ]
-            for quarter in range(4):
-
-                @pl.when((quarter_ref[0] ^ which) == quarter)
-                def _():
-                    for at in range(blocks):
-                        low = (at * 4 + quarter) * part
-                        ref[:, low : low + part] = hold[:, at * part : (at + 1) * part]
-
-
-def spread_pair(quarter, own, other, part):
-    rows, cols = own.shape
+    )(place, inputs, *packs, scale, slope, outer, down_grad, narrow_down, down, down, *slots)
+
+
+def down_kernel(*refs, bounds):
+    hiddens, (weights_ref, first_ref, outer_ref) = refs[:-6], refs[-6:-3]
+    keep_ref, send_ref, reduced_ref = refs[-3:]
+
+    @pl.when(pl.program_id(0) == 0)
+    def _():
+        reduced_ref[...] = jnp.zeros_like(reduced_ref)
+        for (start, stop), ref in zip(bounds, hiddens):
+            reduced_ref[...] += jnp.dot(
+                ref[...], first_ref[start:stop, :], preferred_element_type=F32
+            )
+
+    lane = lax.broadcasted_iota(jnp.int32, reduced_ref.shape, 1)
+    total = low_rank(jnp.where(lane < RANK, reduced_ref[...], 0.0), outer_ref[...], 0)
+    for (start, stop), ref in zip(bounds, hiddens):
+        total = total + jnp.dot(
+            ref[...], weights_ref[start:stop, :], preferred_element_type=F32
+        )
+    count = keep_ref.shape[0]
+    keep_ref[...] = total[:count]
+    send_ref[...] = total[count:].astype(BF)
+
+
+def down_forward(hiddens, bounds, down, outer, tile=256):
+    count = hiddens[0].shape[0]
+    rows = down.shape[0]
     return pl.pallas_call(
-        functools.partial(spread_kernel, part=part),
+        functools.partial(down_kernel, bounds=bounds),
+        grid=(D // tile,),
+        in_specs=[pl.BlockSpec(hidden.shape, lambda n: (0, 0)) for hidden in hiddens]
+        + [
+            pl.BlockSpec((rows, tile), lambda n: (0, n)),
+            pl.BlockSpec((rows, EXTRA), lambda n: (0, D // EXTRA)),
+            pl.BlockSpec((RANK, tile), lambda n: (0, n)),
+        ],
+        out_specs=[
+            pl.BlockSpec((count // 2, tile), lambda n: (0, n)),
+            pl.BlockSpec((count // 2, tile), lambda n: (0, n)),
+            pl.BlockSpec((count, EXTRA), lambda n: (0, 0)),
+        ],
+        out_shape=[
+            jax.ShapeDtypeStruct((count // 2, D), F32),
+            jax.ShapeDtypeStruct((count // 2, D), BF),
+            jax.ShapeDtypeStruct((count, EXTRA), F32),
+        ],
+        compiler_params=pltpu.CompilerParams(vmem_limit_bytes=40 << 20),
+        cost_estimate=pl.CostEstimate(flops=COST, bytes_accessed=COST, transcendentals=0),
+    )(*hiddens, down, down, outer)
+
+
+def kv_form_kernel(z_ref, scale_ref, cos_ref, sin_ref, out_ref):
+    lane = lax.broadcasted_iota(jnp.int32, cos_ref.shape, 1)
+    half = z_ref.shape[1] // 2
+    for pair in range(half // 128):
+        at = slice(pair * 128, (pair + 1) * 128)
+        to = slice(half + pair * 128, half + (pair + 1) * 128)
+        keys = turn_lanes(z_ref[:, at] * scale_ref[:, at], cos_ref[...], sin_ref[...])
+        values = z_ref[:, to] * scale_ref[:, to]
+        first = jnp.where(lane < HD, keys, pltpu.roll(values, HD, 1))
+        second = jnp.where(lane < HD, pltpu.roll(keys, HD, 1), values)
+        out_ref[:, 2 * pair * 128 : (2 * pair + 1) * 128] = first.astype(BF)
+        out_ref[:, (2 * pair + 1) * 128 : (2 * pair + 2) * 128] = second.astype(BF)
+
+
+def kv_form(z, scale, cosine, sine):
+    return pl.pallas_call(
+        kv_form_kernel,
+        out_shape=jax.ShapeDtypeStruct(z.shape, BF),
+        cost_estimate=pl.CostEstimate(flops=COST, bytes_accessed=COST, transcendentals=0),
+    )(z, scale, cosine, sine)
+
+
+def kv_back_kernel(sum_ref, cos_ref, sin_ref, out_ref):
+    lane = lax.broadcasted_iota(jnp.int32, cos_ref.shape, 1)
+    half = sum_ref.shape[1] // 2
+    for pair in range(half // 128):
+        first = sum_ref[:, 2 * pair * 128 : (2 * pair + 1) * 128].astype(F32)
+        second = sum_ref[:, (2 * pair + 1) * 128 : (2 * pair + 2) * 128].astype(F32)
+        keys = jnp.where(lane < HD, first, pltpu.roll(second, HD, 1))
+        values = jnp.where(lane < HD, pltpu.roll(first, HD, 1), second)
+        out_ref[:, pair * 128 : (pair + 1) * 128] = turn_lanes(keys, cos_ref[...], -sin_ref[...])
+        out_ref[:, half + pair * 128 : half + (pair + 1) * 128] = values
+
+
+def kv_back(sums, cosine, sine):
+    return pl.pallas_call(
+        kv_back_kernel,
+        out_shape=jax.ShapeDtypeStruct(sums.shape, F32),
+        cost_estimate=pl.CostEstimate(flops=COST, bytes_accessed=COST, transcendentals=0),
+    )(sums, cosine, sine)
+
+
+def pack_all_kernel(
+    query_ref, kv_ref, out_ref_, mlp_ref, down_ref, one_ref, first_out_ref, pairs_ref, down_first_ref,
+    place_ref, packed_ref, wide_rows, hold, down_rows, *, toks, part, layout,
+):
+    tall, low, lanes, share, hidden_share, outer_share = layout
+    many = wide_rows.shape[0]
+    wides = packed_ref.shape[0] // toks
+    for n, ref in ((0, query_ref), (1, kv_ref), (3, out_ref_), (6, down_ref)):
+        wide_rows[: RANK + 1, STARTS[n] : STARTS[n] + ref.shape[1]] = ref[...]
+    blocks = FF // (4 * part)
+    down_rows[...] = jnp.zeros_like(down_rows)
+    for side in range(2):
+        start = STARTS[4 + side]
+        wide_rows[:, start : start + FF] = jnp.zeros((many, FF), F32)
+        for tile in range(blocks * part // 128):
+            hold[: RANK + 1, tile * 128 : (tile + 1) * 128] = mlp_ref[
+                :, (2 * tile + side) * 128 : (2 * tile + side + 1) * 128
+            ]
+        for quarter in range(4):
+
+            @pl.when(place_ref[2] == quarter)
+            def _():
+                for at in range(blocks):
+                    to = start + (at * 4 + quarter) * part
+                    wide_rows[: RANK + 1, to : to + part] = hold[
+                        : RANK + 1, at * part : (at + 1) * part
+                    ]
+    for quarter in range(4):
+
+        @pl.when(place_ref[2] == quarter)
+        def _():
+            for at in range(blocks):
+                to = (at * 4 + quarter) * part
+                down_rows[:, to : to + part] = down_first_ref[:, at * part : (at + 1) * part]
+
+    packed_ref[...] = jnp.zeros_like(packed_ref)
+    sources = [(0, one_ref), (3 * RANK, first_out_ref), (4 * RANK, pairs_ref)]
+
+    def main_piece(start, rows, cols):
+        parts = []
+        while rows:
+            base, ref = [pair for pair in sources if pair[0] <= start][-1]
+            here = min(rows, base + ref.shape[0] - start)
+            parts.append(ref[start - base : start - base + here, cols])
+            start, rows = start + here, rows - here
+        return parts[0] if len(parts) == 1 else jnp.concatenate(parts, axis=0)
+
+    fit = lanes // share
+    for tok in range(toks):
+        for wide in range(wides):
+            at = tok * wides + wide
+            cols = slice(wide * share, (wide + 1) * share)
+            for piece in range(fit):
+                packed_ref[at, :tall, piece * share : (piece + 1) * share] = main_piece(
+                    (tok * fit + piece) * tall, tall, cols
+                )
+            packed_ref[at, tall : tall + low, :hidden_share] = down_rows[
+                tok * low : (tok + 1) * low, wide * hidden_share : (wide + 1) * hidden_share
+            ]
+            packed_ref[at, tall + low : tall + low + RANK + 1, :outer_share] = wide_rows[
+                : RANK + 1, at * outer_share : (at + 1) * outer_share
+            ]
+
+
+def pack_all(place, pieces, toks, part, layout):
+    tall, low, lanes, share, hidden_share, outer_share = layout
+    owners = OUTS // outer_share
+    rows = -(-(tall + low + RANK + 1) // 8) * 8
+    fixed = lambda array: pl.BlockSpec(array.shape, lambda *n: (0,) * array.ndim)
+    shape = jax.ShapeDtypeStruct((owners, rows, lanes), F32)
+    return pl.pallas_call(
+        functools.partial(pack_all_kernel, toks=toks, part=part, layout=layout),
+        grid=(1,),
+        in_specs=[fixed(piece) for piece in pieces]
+        + [pl.BlockSpec(memory_space=pltpu.SMEM)],
+        out_specs=fixed(shape),
+        out_shape=shape,
+        scratch_shapes=[
+            pltpu.VMEM((RANK + 8, OUTS), F32),
+            pltpu.VMEM((RANK + 8, FF // 4), F32),
+            pltpu.VMEM((RANK, FF), F32),
+        ],
+        compiler_params=pltpu.CompilerParams(vmem_limit_bytes=40 << 20),
+        cost_estimate=pl.CostEstimate(flops=COST, bytes_accessed=COST, transcendentals=0),
+    )(*pieces, place)
+
+
+def mlp_back_kernel(
+    place_ref, one_ref, two_ref, narrow_ref, middle_ref, first_ref, inputs_ref, *refs, offset, rank
+):
+    slots, (keep_ref, send_ref, out_ref, held_one, held_two, arrived) = refs[:-6], refs[-6:]
+    each = len(slots) // 2
+    rows = held_one.shape[1]
+    count = inputs_ref.shape[0]
+    copies = []
+    for half, held in enumerate((held_one, held_two)):
+        copies.append(
+            [
+                pltpu.make_async_copy(slots[half * each + i], held.at[i], arrived.at[half * each + i])
+                for i in range(each)
+            ]
+        )
+    for i in range(each):
+        copies[0][i].start()
+        copies[1][i].start()
+    narrow_high, narrow_low = split_parts(narrow_ref[...])
+    turned_high = narrow_high.astype(F32).T.astype(BF)
+    turned_low = narrow_low.astype(F32).T.astype(BF)
+    middle_high, middle_low = split_parts(middle_ref[...])
+    for i in range(each):
+        copies[0][i].wait()
+        copies[1][i].wait()
+        at = pl.ds(place_of(place_ref, i, rows), rows)
+        first = first_ref[at, :]
+        total = lax.dot_general(one_ref[...], held_one[i], NT, preferred_element_type=F32)
+        total = total + lax.dot_general(two_ref[...], held_two[i], NT, preferred_element_type=F32)
+        grad = (
+            total[:count]
+            + lax.dot_general(narrow_high, first, NT, preferred_element_type=F32)
+            + lax.dot_general(narrow_low, first, NT, preferred_element_type=F32)
+        )
+        keep_ref[:, at] = grad[: count // 2]
+        send_ref[:, at] = grad[count // 2 :].astype(BF)
+        weighted = total[count : count + rank] + total[count + rank :]
+        middle = lax.dot_general(middle_high, first, NT, preferred_element_type=F32)
+        middle = middle + lax.dot_general(middle_low, first, NT, preferred_element_type=F32)
+        inputs = inputs_ref[:, at]
+        product = jnp.dot(turned_high, inputs, preferred_element_type=F32)
+        product = product + jnp.dot(turned_low, inputs, preferred_element_type=F32)
+        out_ref[:, at] = product[offset : offset + rank] + 2.0 * (weighted + 2.0 * middle)
+
+
+def mlp_back(place, grads, narrow, middle, first, inputs, slots, offset):
+    count = inputs.shape[0]
+    rank = middle.shape[0]
+    rows = slots[0][0].shape[0]
+    many = len(slots[0])
+    operands = [*grads, narrow, middle, first, inputs]
+    fixed = lambda array: pl.BlockSpec(array.shape, lambda n, s: (0, 0))
+    shapes = [
+        jax.ShapeDtypeStruct((count // 2, D), F32),
+        jax.ShapeDtypeStruct((count // 2, D), BF),
+        jax.ShapeDtypeStruct((rank, D), F32),
+    ]
+    return pl.pallas_call(
+        functools.partial(mlp_back_kernel, offset=offset, rank=rank),
         grid_spec=pltpu.PrefetchScalarGridSpec(
             num_scalar_prefetch=1,
             grid=(1,),
-            in_specs=[pl.BlockSpec((rows, cols), lambda n, s: (0, 0))] * 2,
-            out_specs=[pl.BlockSpec((rows, 2 * cols), lambda n, s: (0, 0))] * 2,
-            scratch_shapes=[pltpu.VMEM((rows, cols // 2), F32)],
+            in_specs=[fixed(array) for array in operands]
+            + [pl.BlockSpec(memory_space=pl.ANY) for _ in range(2 * many)],
+            out_specs=[fixed(shape) for shape in shapes],
+            scratch_shapes=[
+                pltpu.VMEM((many, rows, grads[0].shape[1]), BF),
+                pltpu.VMEM((many, rows, grads[1].shape[1]), BF),
+                pltpu.SemaphoreType.DMA((2 * many,)),
+            ],
         ),
-        out_shape=[jax.ShapeDtypeStruct((rows, 2 * cols), F32)] * 2,
-        cost_estimate=pl.CostEstimate(flops=rows, bytes_accessed=1 << 20, transcendentals=0),
-    )(quarter, own, other)
+        out_shape=shapes,
+        compiler_params=pltpu.CompilerParams(vmem_limit_bytes=60 << 20),
+        cost_estimate=pl.CostEstimate(flops=COST, bytes_accessed=COST, transcendentals=0),
+    )(place, *operands, *slots[0], *slots[1])
 
 
 def column_sums(base, first_high, first_low, outer, offset):
@@ -912,20 +1178,19 @@
 
 
 def early_kernel(
-    place_ref, query_ref, key_ref, value_ref, main_ref, outer_ref,
-    query_out, kv_out, square_ref, cross_ref,
+    place_ref, query_ref, key_ref, value_ref, main_ref, outer_ref, shard_out, square_ref, cross_ref,
 ):
-    half = query_out.shape[1]
+    half = query_ref.shape[1] // 2
     kv_cols = key_ref.shape[1]
     high, low = split_parts(widened(main_ref[...]))
-    kv_out[:, kv_cols:] = high
+    shard_out[:, half + kv_cols :] = high
     for core in range(2):
 
         @pl.when(place_ref[1] == core)
         def _():
-            query_out[...] = query_ref[:, core * half : (core + 1) * half]
+            shard_out[:, :half] = query_ref[:, core * half : (core + 1) * half]
             kv = (key_ref, value_ref)[core][...]
-            kv_out[:, :kv_cols] = kv
+            shard_out[:, half : half + kv_cols] = kv
             start = 2 * half + core * kv_cols
             square, cross = column_sums(
                 kv, high, low, outer_ref[:, start : start + kv_cols], (1 + core) * RANK
@@ -947,8 +1212,7 @@
     kv_cols = key.shape[1]
     fixed = lambda array: pl.BlockSpec(array.shape, lambda n, s: (0, 0))
     shapes = [
-        jax.ShapeDtypeStruct((rows, cols // 2), BF),
-        jax.ShapeDtypeStruct((rows, kv_cols + EXTRA), BF),
+        jax.ShapeDtypeStruct((rows, cols // 2 + kv_cols + EXTRA), BF),
         jax.ShapeDtypeStruct((1, kv_cols + cols // 2), F32),
         jax.ShapeDtypeStruct((RANK, kv_cols + cols // 2), F32),
     ]
@@ -1122,21 +1386,10 @@
     def other_core(array):
         return swap(array, "tok", 1)
 
-    def to_tokens(features):
-        pieces = features.reshape(CHUNKS, wide_count, block, share)
-        whole = jnp.zeros((count, D), features.dtype)
-        for slot in range(wide_count):
-            piece = lax.dynamic_index_in_dim(pieces, wide ^ slot, 1, keepdims=False)
-            piece = piece.reshape(count, share)
-            if slot:
-                piece = swap(piece, "wide", slot)
-            whole = lax.dynamic_update_slice(whole, piece, (0, (wide ^ slot) * share))
-        return whole
-
     across = wide_count // 4
     deep, side = wide // across, wide % across
 
-    def to_tokens_staged(features):
+    def to_tokens(features, gate=()):
         pieces = features.reshape(CHUNKS, 4, across, block, share)
         rows = jnp.zeros((4, CHUNKS, block, across * share), features.dtype)
         for slot in range(across):
@@ -1151,6 +1404,8 @@
             piece = piece.reshape(count, across * share)
             if slot:
                 piece = swap(piece, "wide", slot * across)
+            if gate:
+                piece = after(piece, *gate)
             whole = lax.dynamic_update_slice(whole, piece, (0, (deep ^ slot) * across * share))
         return whole
 
@@ -1195,15 +1450,15 @@
     KV, QUERY, OUT, MLP, DOWN = range(5)
 
     residual = to_tokens(tokens).astype(F32)
-    gains = all_blocks(jnp.stack([gain_attn, gain_ffn]), "wide")
-    gains = jnp.swapaxes(gains, 0, 1).reshape(2, D)
-
-    query_shard, kv_shard, squares, soon_cross = early_work(
-        place, w_query, w_key, w_value, adapt_main, adapt_outer
-    )
-    kv_slots = [gather_slots(kv_shard)]
-    query_slots = [gather_slots(after(query_shard, *near(kv_slots[0])))]
-    mags = magnitudes[None]
+    gain_parts = jnp.stack([gain_attn, gain_ffn], axis=1)
+    split = [lax.reduce_precision(gain_parts, 8, 7)]
+    split.append(lax.reduce_precision(gain_parts - split[0], 8, 7))
+    split.append(gain_parts - split[0] - split[1])
+    qkv_shard, squares, soon_cross = early_work(
+        place, w_query, w_key, w_value, jnp.concatenate([adapt_main, *split], axis=1), adapt_outer
+    )
+    qkv_slots = [gather_slots(qkv_shard)]
+    mags = after(magnitudes, residual)[None]
 
     def column_terms(squares, pieces):
         norms = jnp.sqrt(all_sum(squares, ["wide"]))
@@ -1225,41 +1480,26 @@
     soon = column_terms(
         squares, [(by_core(sides(mags, 1), sides(mags, 2)),), (own_half(sides(mags, 0)),)]
     )
-    later_output, *_ = lax.optimization_barrier(
-        (w_output, residual, *near(kv_slots[0]))
-    )
-    out_shard, mlp_shard, down_shard, squares, rest_cross, picked = later_work(
-        place, later_output, w_gate, w_up, w_down, adapt_main, adapt_down, adapt_outer,
-        jnp.broadcast_to(mags, (8, OUTS)), part,
-    )
-    rest = column_terms(
-        squares,
-        [(own_half(sides(mags, 3)),), (picked[RANK : RANK + 1],), (own_half(sides(mags, 6)),)],
-    )
-    mlp_outer = [picked[:RANK]]
-    mlp_outer.append(other_core(mlp_outer[0]))
-    columns = [soon[k] + rest[k] for k in range(2)]
-    scale_by, slope_by, norms_by = (
-        [[columns[k][n][i] for n in range(5)] for k in range(2)] for i in range(3)
-    )
+    scale_by, slope_by, norms_by = ([list(soon[k][n][i] for n in range(2)) for k in range(2)] for i in range(3))
 
     def natural_of(parts, n):
         return in_order([p[n] for p in parts])
 
     scales, slopes, norms = (
-        [natural_of(parts, n) if n != MLP else None for n in range(5)]
-        for parts in (scale_by, slope_by, norms_by)
+        [natural_of(parts, n) for n in range(2)] for parts in (scale_by, slope_by, norms_by)
     )
     outers = [sides(adapt_outer, n) for n in range(7)]
     outer_kv = jnp.concatenate(
         [jnp.pad(outers[1], ((0, 0), (0, kv_cols))), jnp.pad(outers[2], ((0, 0), (kv_cols, 0)))]
     )
 
-    kv_slots.append({s: other_core(held) for s, held in kv_slots[0].items()})
-    query_slots.append({s: other_core(held) for s, held in query_slots[0].items()})
+    qkv_slots.append({s: other_core(held) for s, held in qkv_slots[0].items()})
     low_main = put_rows(
-        {s: held[:, kv_cols:] for s, held in kv_slots[0].items()}, jnp.zeros((0, EXTRA), BF)
-    )
+        {s: held[:, half + kv_cols :] for s, held in qkv_slots[0].items()},
+        jnp.zeros((0, EXTRA), BF),
+    )
+    gains = low_main[:, 6 * RANK : 6 * RANK + 6].astype(F32).T
+    gains = (gains[4:6] + gains[2:4]) + gains[:2]
 
     def main_cols(n, many=1):
         return low_main[:, n * RANK : (n + many) * RANK]
@@ -1283,7 +1523,7 @@
         + wide * block
         + jnp.arange(block, dtype=jnp.int32)[None, :]
     ).reshape(count)
-    segment_row = segments[0]
+    segment_row = after(segments, residual)[0]
     own_segment = lax.dynamic_index_in_dim(
         segment_row.reshape(CHUNKS, wide_count, block), wide, 1, keepdims=False
     ).reshape(count)
@@ -1298,86 +1538,119 @@
     start_rows = jnp.tile(own_starts.reshape(CHUNKS, 1, block), (1, 1, GROUP))
     first_block = own_starts.reshape(CHUNKS, block)[:, 0] // (wide_count * block)
 
-    normed_one, inverse_one = norm_rows(residual, gains[0])
+    ready = residual
+    normed_one, inverse_one = norm_rows(ready, gains[0])
     kv_z, reduced_one = slot_mm(
-        place, normed_one, low_main, outer_kv, RANK, [ordered(kv_slots[k]) for k in range(2)]
-    )
-    kv_scaled = kv_z * scales[KV]
-    keys = turn(kv_scaled[:, :kv_cols], cosine[:, :HD], sine[:, :HD])
-    kv = jnp.concatenate(
-        [keys.reshape(count, KVH, HD), kv_scaled[:, kv_cols:].reshape(count, KVH, HD)], axis=2
-    ).astype(BF)
+        place, normed_one, low_main, outer_kv, RANK, [ordered(qkv_slots[k]) for k in range(2)], half
+    )
+    kv = kv_form(kv_z, scales[KV], cosine, sine)
     token_slots = gather_slots(kv.reshape(CHUNKS, 1, block, KVH * 2 * HD))
+
+    out_shard, mlp_shard, down_shard, squares, rest_cross, picked = later_work(
+        place, after(w_output, *near(qkv_slots[0])), w_gate, w_up, w_down, adapt_main, adapt_down, adapt_outer,
+        jnp.broadcast_to(mags, (8, OUTS)), part,
+    )
     kv = jnp.zeros((CHUNKS, wide_count, block, KVH * 2 * HD), BF)
     for slot, held in token_slots.items():
         kv = lax.dynamic_update_slice(kv, held, (0, wide ^ slot, 0, 0))
     kv = kv.reshape(length, KVH * 2 * HD)
     kvt = kv.T.reshape(KVH, 2 * HD, length)
     query_z, _ = slot_mm(
-        place, normed_one, low_main, outers[0], 0, [ordered(query_slots[k]) for k in range(2)]
+        place, normed_one, low_main, outers[0], 0, [ordered(qkv_slots[k]) for k in range(2)]
     )
     queries, attended, log_total = attend(
         first_block, query_z, scales[QUERY], cosine, sine, place_rows, start_rows, kv, kvt
     )
 
-    out_slots = [gather_slots(after(out_shard, *near(query_slots[0])), True)]
+    rest = column_terms(
+        after(squares, attended),
+        [(own_half(sides(mags, 3)),), (picked[RANK : RANK + 1],), (own_half(sides(mags, 6)),)],
+    )
+    mlp_outer = [picked[:RANK]]
+    for found, index in ((scale_by, 0), (slope_by, 1), (norms_by, 2)):
+        for k in range(2):
+            found[k].extend(rest[k][n][index] for n in range(3))
+    for found, parts in ((scales, scale_by), (slopes, slope_by), (norms, norms_by)):
+        found.extend(natural_of(parts, n) if n != MLP else None for n in range(2, 5))
+
+    down_slots = gather_slots(after(down_shard, *near(qkv_slots[0])))
+    out_slots = [gather_slots(after(out_shard, *near(down_slots)), True)]
     out_slots.append({s: other_core(held) for s, held in out_slots[0].items()})
-    upstream = to_tokens_staged(after(cotangent, *near(out_slots[0]), *near(token_slots))).astype(F32)
-    down_slots = gather_slots(after(down_shard, *near(out_slots[0]), *token_slots.values()))
-    down_weights = [put_rows(down_slots, jnp.zeros((0, D + EXTRA), BF))]
-    down_weights.append(other_core(down_weights[0]))
-    mlp_slots = [gather_slots(after(mlp_shard, *near(down_slots)), True)]
-    mlp_slots.append({s: other_core(held) for s, held in mlp_slots[0].items()})
-
+    down_weights = put_rows(down_slots, jnp.zeros((0, D + EXTRA), BF))
+    tiles = 2 * block_cols // 256
+    cuts = [0, (tiles + 1) // 2 * 256, 2 * block_cols]
+    spans = [slice(cuts[i], cuts[i + 1]) for i in range(2)]
+    mlp_slots = []
+    before = near(out_slots[0])
+    for i, span in enumerate(spans):
+        mlp_slots.append(gather_slots(after(mlp_shard[:, span], *before), i == 0))
+        before = near(mlp_slots[-1])
+
+    upstream = to_tokens(
+        after(cotangent, kv, *near(out_slots[0])), far(mlp_slots[0], 2)
+    ).astype(F32)
     output_z, reduced_out = slot_mm(
         place, attended, low_main, outers[3], 3 * RANK, [ordered(out_slots[k]) for k in range(2)]
     )
     hidden_one = residual + output_z * scales[OUT]
 
     normed_own, inverse_two = norm_rows(hidden_one, gains[1])
-    normed_two = jnp.concatenate([normed_own, partner(normed_own)])
+    def of_four(rows):
+        pair = jnp.concatenate([rows, partner(rows)])
+        return jnp.concatenate([pair, other_core(pair)])
+
+    def to_owner_of_four(keep, sent, *behind):
+        pair = keep + other_core(after(sent, *behind) if behind else sent).astype(F32)
+        swapped = partner(pair[count:].astype(BF))
+        return pair[:count] + swapped.astype(F32), swapped
+
+    normed_two = of_four(normed_own)
     down_low = (upstream * scales[DOWN]).astype(BF)
-    down_low = jnp.concatenate([down_low, partner(down_low)])
+    down_low = of_four(down_low)
     narrow_down = 2.0 * mm_t(down_low, outers[6].astype(BF))
     narrow_down_lanes = lanes_of(narrow_down)
+    crosses = after(jnp.concatenate([soon_cross, rest_cross], axis=1), normed_own)
+    for bit in bits_of(wide_count):
+        crosses = crosses + swap(crosses.astype(BF), "wide", bit).astype(F32)
+    cross_by = [crosses, other_core(crosses)]
+    normed_two = after(normed_two, *cross_by)
+    packs = pack_reduced(normed_two, low_main, 4 * RANK, 2 * RANK)
     blocks = [
         mlp_block(
             place,
             normed_two,
-            low_main,
+            packs,
             4 * RANK,
-            scale_by[k][MLP],
-            slope_by[k][MLP],
-            mlp_outer[k],
+            scale_by[0][MLP],
+            slope_by[0][MLP],
+            mlp_outer[0],
             down_low,
             narrow_down_lanes,
-            down_weights[k],
-            ordered(mlp_slots[k]),
+            down_weights,
+            ordered(mlp_slots[i]),
+            span.start,
         )
-        for k in range(2)
+        for i, span in enumerate(spans)
     ]
-    through = mm(blocks[0][0], down_weights[0]) + mm(blocks[1][0], down_weights[1])
-    reduced_down = through[:, D : D + RANK]
-    down_sum = through[:, :D] + mm(
-        lanes_of(reduced_down), twice_low(outers[6])
-    )
-
-    def first_term(product, weight_term, middle, first_cols):
-        both = jnp.concatenate(two_parts(middle))
-        return product + 2.0 * (weight_term + 2.0 * fold_parts(mm_t(both, first_cols), RANK))
-
-    backs = [slot_back_wide(place, blocks[k][1], ordered(mlp_slots[k])) for k in range(2)]
+    bounds = [(span.start // 2, span.stop // 2) for span in spans]
+    down_keep, down_sent, reduced_down = down_forward([b[0] for b in blocks], bounds, down_weights, outers[6])
+    reduced_down = reduced_down[:, :RANK]
+
     pairs = 2 * RANK
-    grad_normed, first_pairs = finish_back(
-        backs, [pairs, pairs], blocks[0][4] + blocks[1][4], blocks[0][5] + blocks[1][5], low_main,
-        normed_two, 4 * RANK, True,
-    )
-    swapped = partner(grad_normed[count:].astype(BF))
-    grad_normed = grad_normed[:count] + swapped.astype(F32)
+    keep, sent, first_pairs = mlp_back(
+        place,
+        [b[1] for b in blocks],
+        sum(b[4] for b in blocks),
+        sum(b[5] for b in blocks),
+        low_main,
+        normed_two,
+        [ordered(slots) for slots in mlp_slots],
+        4 * RANK,
+    )
+    grad_normed, swapped = to_owner_of_four(keep, sent)
     grad_mid = upstream + norm_rows_back(hidden_one, gains[1], inverse_two, grad_normed)
-    down_far = partner(after(down_sum[count:].astype(BF), swapped))
-    down_z = down_sum[:count] + down_far.astype(F32)
-    layer_out = from_tokens((hidden_one + down_z * scales[DOWN]).astype(BF))
+    down_z, _ = to_owner_of_four(down_keep, down_sent, swapped)
+    layer_rows = (hidden_one + down_z * scales[DOWN]).astype(BF)
 
     def first_grads(rows, inputs, narrow, middle, factors, many):
         size = many * RANK
@@ -1405,29 +1678,20 @@
         grad_mixed,
     )
     kv_grad = kv_grad.reshape(CHUNKS, wide_count, block, KVH * 2 * HD)
-    kv_grad = after(jnp.swapaxes(kv_grad, 0, 1).astype(F32), layer_out)
-    bits = bits_of(wide_count)
-    kv_half = KVH * HD
-    kv_grad = jnp.concatenate(
-        [
-            scatter_sum(kv_grad[..., :kv_half], "wide", BF),
-            scatter_sum(kv_grad[..., kv_half:], "wide", BF, [bits[-2], *bits[:-2], bits[-1]]),
-        ],
-        axis=-1,
-    )
-    kv_grad = kv_grad.reshape(count, KVH, 2 * HD)
-    key_grad = turn(kv_grad[:, :, :HD].reshape(count, -1), cosine[:, :HD], -sine[:, :HD])
-    value_grad = kv_grad[:, :, HD:].reshape(count, -1)
+    kv_grad = jnp.swapaxes(kv_grad, 0, 1).astype(F32)
+    kv_grad = scatter_sum(kv_grad, "wide", BF)
+    kv_grad = kv_back(kv_grad.reshape(count, KVH * 2 * HD), cosine, sine)
+    layer_out = from_tokens(after(layer_rows, kv_grad))
 
     query_rows_low, scale_query, outer_query, narrow_query, middle_query = grad_terms(
         query_grad, query_z, scales[QUERY], slopes[QUERY], outers[0], 0, reduced_one
     )
-    back_query = slot_back(place, query_rows_low, [ordered(query_slots[k]) for k in range(2)])
+    back_query = slot_back(place, query_rows_low, [ordered(qkv_slots[k]) for k in range(2)])
     kv_rows_low, scale_kv, outer_kv_grad, narrow_kv, middle_kv = grad_terms(
-        jnp.concatenate([key_grad, value_grad], axis=1), kv_z, scales[KV], slopes[KV], outer_kv,
+        kv_grad, kv_z, scales[KV], slopes[KV], outer_kv,
         RANK, reduced_one,
     )
-    back_kv = slot_back(place, kv_rows_low, [ordered(kv_slots[k]) for k in range(2)])
+    back_kv = slot_back(place, kv_rows_low, [ordered(qkv_slots[k]) for k in range(2)], half)
     grad_normed, first_one = finish_back(
         [back_query, back_kv],
         [RANK, pairs],
@@ -1443,25 +1707,23 @@
 
     scale_down = jnp.sum(upstream * down_z, axis=0, keepdims=True)
     pair_down = scale_down + partner(scale_down)
+    pair_down = pair_down + other_core(pair_down)
     weighted = (pair_down * slopes[DOWN]) * outers[6]
     middle_down = gram_of(weighted, outers[6])
     weighted_parts = jnp.pad(jnp.concatenate(two_parts(weighted)), ((0, 0), (0, EXTRA)))
-    first_down = [
-        first_grads(
-            mm_t(weighted_parts, down_weights[k]), blocks[k][0], narrow_down, middle_down,
-            down_weights[k][:, D : D + RANK], 1,
-        )
-        for k in range(2)
-    ]
+    first_down = first_grads(
+        mm_t(weighted_parts, down_weights),
+        jnp.concatenate([b[0] for b in blocks], axis=1),
+        narrow_down,
+        middle_down,
+        down_weights[:, D : D + RANK],
+        1,
+    )
     outer_down = 2.0 * fold_parts(
         t_mm(jnp.concatenate(two_parts(reduced_down), axis=1), down_low), RANK
     )
     of_keys = (jnp.arange(2 * kv_cols) < kv_cols)[None, :]
     outer_kv_grad = jnp.where(of_keys, outer_kv_grad[:RANK], outer_kv_grad[RANK:])
-    crosses = [soon_cross, rest_cross]
-    cross_own = all_sum(after(jnp.concatenate(crosses, axis=1), down_z), ["wide"])
-    cross_by = [cross_own, other_core(cross_own)]
-
     def second_grads(product, sums, slope, norm, cross):
         return jnp.concatenate([product + 2.0 * (sums * slope) * cross, sums / norm])
 
@@ -1476,52 +1738,36 @@
             (DOWN, outer_down, scale_down),
         )
     }
-    eights = [
-        jnp.pad(
-            second_grads(
-                blocks[k][3], blocks[k][2], slope_by[k][MLP], norms_by[k][MLP], cut(cross_by[k], MLP)
-            ),
-            ((0, 7), (0, 0)),
-        )
-        for k in range(2)
-    ]
-    gate_grads, up_grads = spread_pair(quarter, *eights, part)
-    outer_cols = jnp.concatenate(
-        [
-            plain[QUERY],
-            plain[KV],
-            plain[OUT],
-            gate_grads[: RANK + 1],
-            up_grads[: RANK + 1],
-            plain[DOWN],
-        ],
-        axis=1,
-    )
-    main_rows = jnp.concatenate([first_one, first_out, first_pairs])
-    down_rows = jnp.zeros((RANK, wide_count, 4, part), F32)
-    for k in range(2):
-        down_rows = lax.dynamic_update_slice(
-            down_rows,
-            first_down[k].reshape(RANK, wide_count, 1, part),
-            (0, 0, quarter[0] ^ k, 0),
-        )
-    down_rows = down_rows.reshape(RANK, FF)
-
+    mlp_grads = second_grads(
+        jnp.concatenate([b[3] for b in blocks], axis=1),
+        jnp.concatenate([b[2] for b in blocks], axis=1),
+        slope_by[0][MLP],
+        norms_by[0][MLP],
+        cut(cross_by[0], MLP),
+    )
     main_width = 6 * RANK // tok_count
     down_width = RANK // tok_count
     outer_share = OUTS // (tok_count * wide_count)
 
-    def to_owner(rows, tok_rows, wide_cols):
-        shaped = rows.reshape(tok_count, tok_rows, wide_count, wide_cols)
-        summed = scatter_sum(shaped, "tok")
-        return scatter_sum(jnp.swapaxes(summed, 0, 1), "wide")
-
-    main_part = to_owner(main_rows, main_width, share).T
-    down_part = to_owner(down_rows, down_width, hidden_share).T
-    outer_blocks = jnp.moveaxis(
-        outer_cols.reshape(RANK + 1, tok_count, wide_count, outer_share), 0, 2
-    )
-    outer_sum = scatter_sum(scatter_sum(outer_blocks, "tok"), "wide")
+    lanes = 768
+    fit = lanes // share
+    tall = main_width // fit
+    packed = pack_all(
+        place,
+        [
+            plain[QUERY], plain[KV], plain[OUT], mlp_grads, plain[DOWN], first_one, first_out,
+            first_pairs, first_down,
+        ],
+        tok_count,
+        part,
+        (tall, down_width, lanes, share, hidden_share, outer_share),
+    )
+    packed = packed.reshape((tok_count, wide_count) + packed.shape[1:])
+    packed = scatter_sum(scatter_sum(packed, "tok"), "wide")
+    main_part = jnp.swapaxes(packed[:tall].reshape(tall, fit, share), 0, 1)
+    main_part = main_part.reshape(main_width, share).T
+    down_part = packed[tall : tall + down_width, :hidden_share].T
+    outer_sum = packed[tall + down_width : tall + down_width + RANK + 1, :outer_share]
     outer_part = outer_sum[:RANK]
     block_start = (tok * wide_count + wide) * outer_share
     mag_part = outer_sum[RANK]

time: 972 us -> 892 us (0.918)
  Pallas kernels: 170 us -> 228 us
  matrix products: 64.8 us -> 10 us
  starting transfers between devices: 157 us -> 115 us
  local copies, waits for them, and re-layouts: 144 us -> 119 us
  other arithmetic: 79.2 us -> 58.9 us
    pallas_call x4 -> x9, Pallas kernels: 22.6 us -> 86.4 us  [the longest x1 40.8 us: mlp_back(): pl.pallas_call(functools.partial(mlp_back_kernel, offset=offset, rank=ran...]
    ppermute x141 -> x109, starting transfers between devices: 157 us -> 115 us  [swap(): return lax.ppermute(array, axis, [(i, i ^ distance) for i in range(count)])]
    dot_general x21 -> x3, matrix products: 42.4 us -> 5.99 us  [mm_t(): lax.dot_general(left, right, (((1,), (1,)), ((), ())), preferred_element_...]
    dot_general x3 -> x0, matrix products: 18 us -> none  [mm(): return jnp.dot(left, right, preferred_element_type=F32)]
    dynamic_update_slice x16 -> x12, local copies, waits for them, and re-layouts: 11.3 us -> 1.18 us  [the longest x4 0.97 us: to_tokens(): lax.dynamic_update_slice(rows, piece, (0, 0, 0, (side ^ slot) * share))]
    ppermute x141 -> x109, waiting for transfers between devices: 333 us -> 338 us  [swap(): return lax.ppermute(array, axis, [(i, i ^ distance) for i in range(count)])]
    unnamed x618 -> x529, local copies, waits for them, and re-layouts: 53.7 us -> 49.2 us
  transfers between devices with their start and end apart: 141 -> 109, of which waited for: 59 -> 44; matrix products, arithmetic and copies ran while one was open for 20% -> 13% of each run, Pallas kernels for 13% -> 17%
where the time goes in v3:
time: 892 us; the launch traced here: 878 us
  waiting for transfers between devices  338 us (38%)
  Pallas kernels  228 us (26%)
  local copies, waits for them, and re-layouts  119 us (13%)
  starting transfers between devices  115 us (13%)
  other arithmetic  58.9 us (7%)
  matrix products  10 us (1%)
  between operations  9.4 us (1%)
    ppermute x109, waiting for transfers between devices, swap(): return lax.ppermute(array, axis, [(i, i ^ distance) for i in range(count)])  338 us
    ppermute x109, starting transfers between devices, swap(): return lax.ppermute(array, axis, [(i, i ^ distance) for i in range(count)])  115 us
    unnamed x529, local copies, waits for them, and re-layouts  49.2 us
    pallas_call x2, Pallas kernels, mlp_block(): pl.pallas_call(functools.partial(mlp_kernel, offset=offset), grid_spec=pl...  48.5 us
    pallas_call x1, Pallas kernels, mlp_back(): pl.pallas_call(functools.partial(mlp_back_kernel, offset=offset, rank=ran...  40.8 us
    pallas_call x1, Pallas kernels, attend_back(): pl.pallas_call(functools.partial(backward_kernel, block=block, span=span,...  24.9 us
    pallas_call x3, Pallas kernels, slot_back(): pl.pallas_call(functools.partial(slot_back_kernel, skip=skip), grid_spec=...  21.4 us
    pallas_call x3, Pallas kernels, slot_mm(): pl.pallas_call(functools.partial(slot_kernel, offset=offset), grid_spec=p...  21 us
  transfers between devices with their start and end apart: 109, of which 44 were waited for; matrix products, arithmetic and copies ran while one was open for 13% of the time, Pallas kernels for 17%

profile of v3, /device:TPU:0, one launch (start us, length us, event | category | flops | bytes accessed | tf_op | source)
XLA Modules:
  0.0 878.2 jit_solution(1010714053631459927)
XLA Ops:
  25.8 18.1 %collective-permute-done.19 = f32[1,1280]{1,0:T(1,128)S(1)} collective-permute-done((f32[1,1280]{1,0:T(1,128)S(1)}, f32[1,1280]{1,0:T(1,128)S(1)}, u32[]{:S(2)}, u32[]{:S(2)}) %collective-permute-start.19) | collective-permute-done | bytes 5152 | tf_op jit(solution)/shard_map/ppermute | solution.py:50
  61.4 10.7 %collective-permute-done.2 = bf16[256,512]{1,0:T(8,128)(2,1)S(1)} collective-permute-done((bf16[256,512]{1,0:T(8,128)(2,1)S(1)}, bf16[256,512]{1,0:T(8,128)(2,1)S(1)}, u32[]{:S(2)}, u32[]{:S(2)}) %collective-permute-start.2) | collective-permute-done | bytes 262176 | tf_op jit(solution)/shard_map/ppermute | solution.py:50
  75.1 13.8 %shard_map.348 = (bf16[256,1024]{1,0:T(8,128)(2,1)S(1)}, bf16[256,2816]{1,0:T(8,128)(2,1)}, bf16[176,2176]{1,0:T(8,128)(2,1)}, f32[1,4864]{1,0:T(1,128)S(1)}, f3...) custom-call(s32[3]{0:T(128)S(1)} %pad_add_fusion.place_ref, bf16[256,2048]{1,0:T(8,128)(2,1)S(1)} %copy-done.118, ...), custom_call_target="tpu_custom_call" | custom-call | flops 1024 | bytes 1024 | tf_op jit(solution)/shard_map/pallas_call | solution.py:1326
  114.0 28.6 %collective-permute-done.31 = bf16[176,2176]{1,0:T(8,128)(2,1)} collective-permute-done((bf16[176,2176]{1,0:T(8,128)(2,1)}, bf16[176,2176]{1,0:T(8,128)(2,1)}, u32[]{:S(2)}, u32[]{:S(2)}) %collective-permute-start.31) | collective-permute-done | bytes 765984 | tf_op jit(solution)/shard_map/ppermute | solution.py:50
  166.2 9.0 %collective-permute-done.34.refs_2_ = bf16[256,1024]{1,0:T(8,128)(2,1)} collective-permute-done((bf16[256,1024]{1,0:T(8,128)(2,1)S(1)}, bf16[256,1024]{1,0:T(8,128)(2,1)}, u32[]{:S(2)}, u32[]{:S(2)}) %collective-permute-start.34) | collective-permute-done | bytes 524320 | tf_op jit(solution)/shard_map/ppermute | solution.py:50
  178.6 6.9 collective-permute-done.24
  196.6 9.2 %shard_map.344 = (f32[256,2048]{1,0:T(8,128)}, f32[256,128]{1,0:T(8,128)}) custom-call(s32[3]{0:T(128)S(1)} %pad_add_fusion.place_ref, bf16[256,2048]{1,0:T(8,128)(2,1)S(1)} %fusion.6.inputs_ref.refs_5_, bf16[2048,128]{1,0:T(8,128)(2,1)S(1)} %slice_dynamic-update-slice_fusion.first_ref.refs_3_.refs_4_, f32[16,2048]{1,0:T(8,128)S(1)} %copy-done.107, ...), custom_call_target="tpu_custom_call" | custom-call | flops 1024 | bytes 1024 | tf_op jit(solution)/shard_map/pallas_call | solution.py:527
  207.4 10.3 %collective-permute-done.26 = bf16[8,1,32,512]{3,2,1,0:T(8,128)(2,1)S(1)} collective-permute-done((bf16[8,1,32,512]{3,2,1,0:T(8,128)(2,1)S(1)}, bf16[8,1,32,512]{3,2,1,0:T(8,128)(2,1)S(1)}, u32[]{:S(2)}, u32[]{:S(2)}) %collective-permute-start.26) | collective-permute-done | bytes 262176 | tf_op jit(solution)/shard_map/ppermute | solution.py:50
  237.6 20.7 %shard_map.347 = (bf16[256,2048]{1,0:T(8,128)(2,1)S(1)}, bf16[256,2048]{1,0:T(8,128)(2,1)S(1)}, f32[4,8,1,256]{3,2,1,0:T(1,128)S(1)}) custom-call(s32[8]{0:T(128)S(1)} %and_select_fusion.1.first_ref, f32[256,2048]{1,0:T(8,128)S(1)} %copy-done.96, f32[1,2048]{1,0:T(1,128)S(1)} %broadcast_select_fusion.7.scale_ref, f32[256,128]{1,0:T(8,128)S(1)} %copy-done.113, ...), custom_call_target="tpu_custom_call" | custom-call | flops 42949672960 | bytes 67108864 | tf_op jit(solution)/shard_map/pallas_call | solution.py:404
  264.4 15.9 %collective-permute-done.48 = f32[1,4864]{1,0:T(1,128)S(1)} collective-permute-done((f32[1,4864]{1,0:T(1,128)S(1)}, f32[1,4864]{1,0:T(1,128)S(1)}, u32[]{:S(2)}, u32[]{:S(2)}) %collective-permute-start.48) | collective-permute-done | bytes 19488 | tf_op jit(solution)/shard_map/ppermute | solution.py:50
  286.7 8.9 %collective-permute-done.61.refs_4_ = bf16[256,1536]{1,0:T(8,128)(2,1)S(1)} collective-permute-done((bf16[256,1536]{1,0:T(8,128)(2,1)S(1)}, bf16[256,1536]{1,0:T(8,128)(2,1)S(1)}, u32[]{:S(2)}, u32[]{:S(2)}) %collective-permute-start.61) | collective-permute-done | bytes 786464 | tf_op jit(solution)/shard_map/ppermute | solution.py:50
  296.2 10.7 %collective-permute-done.39.refs_7_ = bf16[256,1024]{1,0:T(8,128)(2,1)S(1)} collective-permute-done((bf16[256,1024]{1,0:T(8,128)(2,1)}, bf16[256,1024]{1,0:T(8,128)(2,1)S(1)}, u32[]{:S(2)}, u32[]{:S(2)}) %collective-permute-start.39) | collective-permute-done | bytes 524320 | tf_op jit(solution)/shard_map/ppermute | solution.py:50
  314.1 8.4 shard_map.349
  328.0 30.2 %collective-permute-done.58 = bf16[4,8,32,256]{3,2,1,0:T(8,128)(2,1)S(1)} collective-permute-done((bf16[4,8,32,256]{3,2,1,0:T(8,128)(2,1)S(1)}, bf16[4,8,32,256]{3,2,1,0:T(8,128)(2,1)S(1)}, u32[]{:S(2)}, u32[]{:S(2)}) %collective-permute-start.58) | collective-permute-done | bytes 524320 | tf_op jit(solution)/shard_map/ppermute | solution.py:50
  373.1 26.0 %collective-permute-done.65 = bf16[256,512]{1,0:T(8,128)(2,1)S(1)} collective-permute-done((bf16[256,512]{1,0:T(8,128)(2,1)S(1)}, bf16[256,512]{1,0:T(8,128)(2,1)S(1)}, u32[]{:S(2)}, u32[]{:S(2)}) %collective-permute-start.65) | collective-permute-done | bytes 262176 | tf_op jit(solution)/shard_map/ppermute | solution.py:50
  402.3 14.3 %collective-permute-done.55 = bf16[16,6144]{1,0:T(8,128)(2,1)S(1)} collective-permute-done((bf16[16,6144]{1,0:T(8,128)(2,1)S(1)}, bf16[16,6144]{1,0:T(8,128)(2,1)S(1)}, u32[]{:S(2)}, u32[]{:S(2)}) %collective-permute-start.55) | collective-permute-done | bytes 196640 | tf_op jit(solution)/shard_map/ppermute | solution.py:50
  425.8 8.7 collective-permute-start.76
  450.7 13.6 %collective-permute-done.80.refs_6_.refs_14_ = bf16[256,1280]{1,0:T(8,128)(2,1)} collective-permute-done((bf16[256,1280]{1,0:T(8,128)(2,1)}, bf16[256,1280]{1,0:T(8,128)(2,1)}, u32[]{:S(2)}, u32[]{:S(2)}) %collective-permute-start.80) | collective-permute-done | bytes 655392 | tf_op jit(solution)/shard_map/ppermute | solution.py:50
  484.1 25.9 %shard_map.351 = (bf16[1024,768]{1,0:T(8,128)(2,1)}, bf16[1088,1536]{1,0:T(8,128)(2,1)}, f32[1,1536]{1,0:T(1,128)S(1)}, f32[16,1536]{1,0:T(8,128)S(1)}, f32[1024,128]{1,0:T(8,128)S(1)}, /*index=5*/f32[32,128]{1,0:T(8,128)S(1)}) custom-call(s32[3]{0:T(128)S(1)} %pad_add_fusion.place_ref, bf16[1024,2048]{1,0:T(8,128)(2,1)} %pad_maximum_fusion.inputs_ref, ...), custom_call_target="tpu_custom_call" | custom-call | flops 1024 | bytes 1024 | tf_op jit(solution)/shard_map/pallas_call | solution.py:862
  510.1 22.6 %shard_map.352 = (bf16[1024,640]{1,0:T(8,128)(2,1)}, bf16[1088,1280]{1,0:T(8,128)(2,1)}, f32[1,1280]{1,0:T(1,128)S(1)}, f32[16,1280]{1,0:T(8,128)S(1)}, f32[1024,128]{1,0:T(8,128)S(1)}, /*index=5*/f32[32,128]{1,0:T(8,128)S(1)}) custom-call(s32[3]{0:T(128)S(1)} %pad_add_fusion.place_ref, bf16[1024,2048]{1,0:T(8,128)(2,1)} %pad_maximum_fusion.inputs_ref, ...), custom_call_target="tpu_custom_call" | custom-call | flops 1024 | bytes 1024 | tf_op jit(solution)/shard_map/pallas_call | solution.py:862
  534.2 40.8 %shard_map.354 = (f32[512,2048]{1,0:T(8,128)}, bf16[512,2048]{1,0:T(8,128)(2,1)}, f32[32,2048]{1,0:T(8,128)}) custom-call(s32[3]{0:T(128)} %copy-done.142, bf16[1088,1536]{1,0:T(8,128)(2,1)} %get-tuple-element.124.one_ref, bf16[1088,1280]{1,0:T(8,128)(2,1)} %get-tuple-element.125.two_ref, f32[1024,128]{1,0:T(8,128)} %add.594.narrow_ref, ...), custom_call_target="tpu_custom_call" | custom-call | flops 1024 | bytes 1024 | tf_op jit(solution)/shard_map/pallas_call | solution.py:1136
  589.4 13.3 %shard_map.353 = (f32[512,2048]{1,0:T(8,128)S(1)}, bf16[512,2048]{1,0:T(8,128)(2,1)}, f32[1024,128]{1,0:T(8,128)S(1)}) custom-call(bf16[1024,768]{1,0:T(8,128)(2,1)S(1)} %copy-done.104, bf16[1024,640]{1,0:T(8,128)(2,1)S(1)} %copy-done.106, bf16[1408,2176]{1,0:T(8,128)(2,1)} %constant_dynamic-update-slice_fusion.8.first_ref.down_ref.refs_2_.refs_3_, ...), custom_call_target="tpu_custom_call" | custom-call | flops 1024 | bytes 1024 | tf_op jit(solution)/shard_map/pallas_call | solution.py:926
  629.0 19.5 %collective-permute-done.85 = bf16[256,2048]{1,0:T(8,128)(2,1)S(1)} collective-permute-done((bf16[256,2048]{1,0:T(8,128)(2,1)S(1)}, bf16[256,2048]{1,0:T(8,128)(2,1)S(1)}, u32[]{:S(2)}, u32[]{:S(2)}) %collective-permute-start.85) | collective-permute-done | bytes 1048608 | tf_op jit(solution)/shard_map/ppermute | solution.py:50
  655.1 7.9 shard_map.356.refs_0_
  667.0 24.9 %shard_map.358 = (f32[256,2048]{1,0:T(8,128)S(1)}, bf16[2048,512]{1,0:T(8,128)(2,1)S(1)}) custom-call(s32[8]{0:T(128)S(1)} %copy-done.160, bf16[256,2048]{1,0:T(8,128)(2,1)S(1)} %copy-done.162, f32[256,128]{1,0:T(8,128)S(1)} %copy-done.114, f32[256,128]{1,0:T(8,128)S(1)} %copy-done.112, s32[8,1,256]{2,1,0:T(1,128)S(1)} %copy-done.153, ...), custom_call_target="tpu_custom_call" | custom-call | flops 42949672960 | bytes 67108864 | tf_op jit(solution)/shard_map/pallas_call | solution.py:447
  699.3 9.1 %shard_map.361.refs_0_ = f32[288,2048]{1,0:T(8,128)} custom-call(s32[3]{0:T(128)S(1)} %copy-done.143, bf16[288,2048]{1,0:T(8,128)(2,1)S(1)} %get-tuple-element.144.grad_ref, bf16[256,1408]{1,0:T(8,128)(2,1)S(1)} %copy-done.7, bf16[256,1408]{1,0:T(8,128)(2,1)} %collective-permute-done.4.refs_1_, bf16[256,1408]{1,0:T(8,128)(2,1)S(1)} %copy-done.14, ...), custom_call_target="tpu_custom_call" | custom-call | flops 1024 | bytes 1024 | tf_op jit(solution)/shard_map/pallas_call | solution.py:634
  709.8 7.8 collective-permute-done.86
  723.6 8.9 %collective-permute-done.87 = bf16[2,8,32,512]{3,2,1,0:T(8,128)(2,1)S(1)} collective-permute-done((bf16[2,8,32,512]{3,2,1,0:T(8,128)(2,1)S(1)}, bf16[2,8,32,512]{3,2,1,0:T(8,128)(2,1)S(1)}, u32[]{:S(2)}, u32[]{:S(2)}) %collective-permute-start.87) | collective-permute-done | bytes 524320 | tf_op jit(solution)/shard_map/ppermute | solution.py:50
  735.1 10.0 %collective-permute-done.88 = bf16[8,32,512]{2,1,0:T(8,128)(2,1)S(1)} collective-permute-done((bf16[8,32,512]{2,1,0:T(8,128)(2,1)S(1)}, bf16[8,32,512]{2,1,0:T(8,128)(2,1)S(1)}, u32[]{:S(2)}, u32[]{:S(2)}) %collective-permute-start.88) | collective-permute-done | bytes 262176 | tf_op jit(solution)/shard_map/ppermute | solution.py:50
  790.8 13.6 %collective-permute-done.100 = f32[8,32,768]{2,1,0:T(8,128)S(1)} collective-permute-done((f32[8,32,768]{2,1,0:T(8,128)S(1)}, f32[8,32,768]{2,1,0:T(8,128)S(1)}, u32[]{:S(2)}, u32[]{:S(2)}) %collective-permute-start.100) | collective-permute-done | bytes 786464 | tf_op jit(solution)/shard_map/ppermute | solution.py:50
  816.8 10.7 %collective-permute-start.102 = (f32[2,32,768]{2,1,0:T(8,128)S(1)}, f32[2,32,768]{2,1,0:T(8,128)S(1)}, u32[]{:S(2)}, u32[]{:S(2)}) collective-permute-start(f32[2,32,768]{2,1,0:T(8,128)S(1)} %dynamic-slice_bitcast_fusion.3), channel_id=1, source_target_pairs={{0,2},{1,3},{2,0},{3,1},{4,6},{5,7},{6,4},{7,5},{8,10},{9,11},{10,... | collective-permute-start | bytes 589832 | tf_op jit(solution)/shard_map/ppermute | solution.py:50
  851.9 9.8 %collective-permute-done.106 = f32[8,128]{1,0:T(8,128)S(1)} collective-permute-done((f32[8,128]{1,0:T(8,128)S(1)}, f32[8,128]{1,0:T(8,128)S(1)}, u32[]{:S(2)}, u32[]{:S(2)}) %collective-permute-start.106) | collective-permute-done | bytes 4128 | tf_op jit(solution)/shard_map/ppermute | solution.py:50
  (1001 shorter events, 380.1 us)
Async XLA Ops:
  9.6 46.4 %collective-permute-start.6 = (bf16[256,1408]{1,0:T(8,128)(2,1)S(1)}, bf16[256,1408]{1,0:T(8,128)(2,1)S(1)}, u32[]{:S(2)}, u32[]{:S(2)}) collective-permute-start(bf16[256,1408]{1,0:T(8,128)(2,1)S(1)} %get-tuple-element.91.refs_0_), channel_id=1, source_target_pairs={{0,4},{1,5},{2,6},{3,7},{4,0},{5,1},{6,2},{7,3},{8,12},{9,13},{10,... | collective-permute-start | bytes 2162696 | tf_op jit(solution)/shard_map/ppermute | solution.py:50
  13.6 40.7 %collective-permute-start.5 = (bf16[256,1408]{1,0:T(8,128)(2,1)S(1)}, bf16[256,1408]{1,0:T(8,128)(2,1)S(1)}, u32[]{:S(2)}, u32[]{:S(2)}) collective-permute-start(bf16[256,1408]{1,0:T(8,128)(2,1)S(1)} %get-tuple-element.91.refs_0_), channel_id=1, source_target_pairs={{0,2},{1,3},{2,0},{3,1},{4,6},{5,7},{6,4},{7,5},{8,10},{9,11},{10,... | collective-permute-start | bytes 2162696 | tf_op jit(solution)/shard_map/ppermute | solution.py:50
  15.2 36.7 %collective-permute-start.4 = (bf16[256,1408]{1,0:T(8,128)(2,1)S(1)}, bf16[256,1408]{1,0:T(8,128)(2,1)}, u32[]{:S(2)}, u32[]{:S(2)}) collective-permute-start(bf16[256,1408]{1,0:T(8,128)(2,1)S(1)} %get-tuple-element.91.refs_0_), channel_id=1, source_target_pairs={{0,1},{1,0},{2,3},{3,2},{4,5},{5,4},{6,7},{7,6},{8,9},{9,8},{10,11... | collective-permute-start | bytes 2162696 | tf_op jit(solution)/shard_map/ppermute | solution.py:50
  56.0 53.0 %collective-permute-start.7 = (bf16[256,1408]{1,0:T(8,128)(2,1)S(1)}, bf16[256,1408]{1,0:T(8,128)(2,1)}, u32[]{:S(2)}, u32[]{:S(2)}) collective-permute-start(bf16[256,1408]{1,0:T(8,128)(2,1)S(1)} %collective-permute-done.5.refs_2_), channel_id=1, source_target_pairs={{0,1},{1,0},{2,3},{3,2},{4,5},{5,4},{6,7},{7,6},{8,9},{9,8},{10,11... | collective-permute-start | bytes 2162696 | tf_op jit(solution)/shard_map/ppermute | solution.py:50
  59.9 51.8 %collective-permute-start.8 = (bf16[256,1408]{1,0:T(8,128)(2,1)S(1)}, bf16[256,1408]{1,0:T(8,128)(2,1)}, u32[]{:S(2)}, u32[]{:S(2)}) collective-permute-start(bf16[256,1408]{1,0:T(8,128)(2,1)S(1)} %collective-permute-done.6.refs_4_), channel_id=1, source_target_pairs={{0,1},{1,0},{2,3},{3,2},{4,5},{5,4},{6,7},{7,6},{8,9},{9,8},{10,11... | collective-permute-start | bytes 2162696 | tf_op jit(solution)/shard_map/ppermute | solution.py:50
  72.1 38.6 %collective-permute-start.9 = (bf16[256,1408]{1,0:T(8,128)(2,1)S(1)}, bf16[256,1408]{1,0:T(8,128)(2,1)}, u32[]{:S(2)}, u32[]{:S(2)}) collective-permute-start(bf16[256,1408]{1,0:T(8,128)(2,1)S(1)} %collective-permute-done.6.refs_4_), channel_id=1, source_target_pairs={{0,2},{1,3},{2,0},{3,1},{4,6},{5,7},{6,4},{7,5},{8,10},{9,11},{10,... | collective-permute-start | bytes 2162696 | tf_op jit(solution)/shard_map/ppermute | solution.py:50
  105.0 37.6 %collective-permute-start.31 = (bf16[176,2176]{1,0:T(8,128)(2,1)}, bf16[176,2176]{1,0:T(8,128)(2,1)}, u32[]{:S(2)}, u32[]{:S(2)}) collective-permute-start(bf16[176,2176]{1,0:T(8,128)(2,1)} %get-tuple-element.100), channel_id=1, source_target_pairs={{0,2},{1,3},{2,0},{3,1},{4,6},{5,7},{6,4},{7,5},{8,10},{9,11},{10,... | collective-permute-start | bytes 2297864 | tf_op jit(solution)/shard_map/ppermute | solution.py:50
  108.9 37.0 %collective-permute-start.32 = (bf16[176,2176]{1,0:T(8,128)(2,1)}, bf16[176,2176]{1,0:T(8,128)(2,1)}, u32[]{:S(2)}, u32[]{:S(2)}) collective-permute-start(bf16[176,2176]{1,0:T(8,128)(2,1)} %get-tuple-element.100), channel_id=1, source_target_pairs={{0,4},{1,5},{2,6},{3,7},{4,0},{5,1},{6,2},{7,3},{8,12},{9,13},{10,... | collective-permute-start | bytes 2297864 | tf_op jit(solution)/shard_map/ppermute | solution.py:50
  161.3 44.6 %collective-permute-start.23 = (bf16[8,1,32,512]{3,2,1,0:T(8,128)(2,1)}, bf16[8,1,32,512]{3,2,1,0:T(8,128)(2,1)S(1)}, u32[]{:S(2)}, u32[]{:S(2)}) collective-permute-start(bf16[8,1,32,512]{3,2,1,0:T(8,128)(2,1)} %bitcast.167), channel_id=1, source_target_pairs={{0,1},{1,0},{2,3},{3,2},{4,5},{5,4},{6,7},{7,6},{8,9},{9,8},{10,11... | collective-permute-start | bytes 786440 | tf_op jit(solution)/shard_map/ppermute | solution.py:50
  163.2 42.6 %collective-permute-start.25 = (bf16[8,1,32,512]{3,2,1,0:T(8,128)(2,1)}, bf16[8,1,32,512]{3,2,1,0:T(8,128)(2,1)S(1)}, u32[]{:S(2)}, u32[]{:S(2)}) collective-permute-start(bf16[8,1,32,512]{3,2,1,0:T(8,128)(2,1)} %bitcast.169), channel_id=1, source_target_pairs={{0,4},{1,5},{2,6},{3,7},{4,0},{5,1},{6,2},{7,3},{8,12},{9,13},{10,... | collective-permute-start | bytes 786440 | tf_op jit(solution)/shard_map/ppermute | solution.py:50
  175.2 59.0 %collective-permute-start.69 = (bf16[176,2176]{1,0:T(8,128)(2,1)}, bf16[176,2176]{1,0:T(8,128)(2,1)}, u32[]{:S(2)}, u32[]{:S(2)}) collective-permute-start(bf16[176,2176]{1,0:T(8,128)(2,1)} %collective-permute-done.31), channel_id=1, source_target_pairs={{0,1},{1,0},{2,3},{3,2},{4,5},{5,4},{6,7},{7,6},{8,9},{9,8},{10,11... | collective-permute-start | bytes 2297864 | tf_op jit(solution)/shard_map/ppermute | solution.py:50
  178.6 55.7 %collective-permute-start.70 = (bf16[176,2176]{1,0:T(8,128)(2,1)}, bf16[176,2176]{1,0:T(8,128)(2,1)}, u32[]{:S(2)}, u32[]{:S(2)}) collective-permute-start(bf16[176,2176]{1,0:T(8,128)(2,1)} %collective-permute-done.32), channel_id=1, source_target_pairs={{0,1},{1,0},{2,3},{3,2},{4,5},{5,4},{6,7},{7,6},{8,9},{9,8},{10,11... | collective-permute-start | bytes 2297864 | tf_op jit(solution)/shard_map/ppermute | solution.py:50
  221.2 61.3 %collective-permute-start.59 = (bf16[256,1536]{1,0:T(8,128)(2,1)S(1)}, bf16[256,1536]{1,0:T(8,128)(2,1)S(1)}, u32[]{:S(2)}, u32[]{:S(2)}) collective-permute-start(bf16[256,1536]{1,0:T(8,128)(2,1)S(1)} %copy-done.59), channel_id=1, source_target_pairs={{0,2},{1,3},{2,0},{3,1},{4,6},{5,7},{6,4},{7,5},{8,10},{9,11},{10,... | collective-permute-start | bytes 2359304 | tf_op jit(solution)/shard_map/ppermute | solution.py:50
  309.9 49.5 %collective-permute-start.71 = (bf16[176,2176]{1,0:T(8,128)(2,1)}, bf16[176,2176]{1,0:T(8,128)(2,1)S(1)}, u32[]{:S(2)}, u32[]{:S(2)}) collective-permute-start(bf16[176,2176]{1,0:T(8,128)(2,1)} %collective-permute-done.32), channel_id=1, source_target_pairs={{0,2},{1,3},{2,0},{3,1},{4,6},{5,7},{6,4},{7,5},{8,10},{9,11},{10,... | collective-permute-start | bytes 2297864 | tf_op jit(solution)/shard_map/ppermute | solution.py:50
  310.9 52.1 %collective-permute-start.60 = (bf16[256,1536]{1,0:T(8,128)(2,1)S(1)}, bf16[256,1536]{1,0:T(8,128)(2,1)S(1)}, u32[]{:S(2)}, u32[]{:S(2)}) collective-permute-start(bf16[256,1536]{1,0:T(8,128)(2,1)S(1)} %collective-permute-done.59.refs_2_), channel_id=1, source_target_pairs={{0,1},{1,0},{2,3},{3,2},{4,5},{5,4},{6,7},{7,6},{8,9},{9,8},{10,11... | collective-permute-start | bytes 2359304 | tf_op jit(solution)/shard_map/ppermute | solution.py:50
  311.9 53.7 %collective-permute-start.62 = (bf16[256,1536]{1,0:T(8,128)(2,1)S(1)}, bf16[256,1536]{1,0:T(8,128)(2,1)}, u32[]{:S(2)}, u32[]{:S(2)}) collective-permute-start(bf16[256,1536]{1,0:T(8,128)(2,1)S(1)} %collective-permute-done.61.refs_4_), channel_id=1, source_target_pairs={{0,1},{1,0},{2,3},{3,2},{4,5},{5,4},{6,7},{7,6},{8,9},{9,8},{10,11... | collective-permute-start | bytes 2359304 | tf_op jit(solution)/shard_map/ppermute | solution.py:50
  312.9 53.8 %collective-permute-start.63 = (bf16[256,1536]{1,0:T(8,128)(2,1)S(1)}, bf16[256,1536]{1,0:T(8,128)(2,1)S(1)}, u32[]{:S(2)}, u32[]{:S(2)}) collective-permute-start(bf16[256,1536]{1,0:T(8,128)(2,1)S(1)} %collective-permute-done.61.refs_4_), channel_id=1, source_target_pairs={{0,2},{1,3},{2,0},{3,1},{4,6},{5,7},{6,4},{7,5},{8,10},{9,11},{10,... | collective-permute-start | bytes 2359304 | tf_op jit(solution)/shard_map/ppermute | solution.py:50
  362.9 36.2 %collective-permute-start.65 = (bf16[256,512]{1,0:T(8,128)(2,1)S(1)}, bf16[256,512]{1,0:T(8,128)(2,1)S(1)}, u32[]{:S(2)}, u32[]{:S(2)}) collective-permute-start(bf16[256,512]{1,0:T(8,128)(2,1)S(1)} %bitcast.178), channel_id=1, source_target_pairs={{0,4},{1,5},{2,6},{3,7},{4,0},{5,1},{6,2},{7,3},{8,12},{9,13},{10,... | collective-permute-start | bytes 786440 | tf_op jit(solution)/shard_map/ppermute | solution.py:50
  363.8 36.0 %collective-permute-start.64 = (bf16[256,512]{1,0:T(8,128)(2,1)S(1)}, bf16[256,512]{1,0:T(8,128)(2,1)S(1)}, u32[]{:S(2)}, u32[]{:S(2)}) collective-permute-start(bf16[256,512]{1,0:T(8,128)(2,1)S(1)} %bitcast.177), channel_id=1, source_target_pairs={{0,2},{1,3},{2,0},{3,1},{4,6},{5,7},{6,4},{7,5},{8,10},{9,11},{10,... | collective-permute-start | bytes 786440 | tf_op jit(solution)/shard_map/ppermute | solution.py:50
  365.6 69.1 %collective-permute-start.72 = (bf16[176,2176]{1,0:T(8,128)(2,1)S(1)}, bf16[176,2176]{1,0:T(8,128)(2,1)S(1)}, u32[]{:S(2)}, u32[]{:S(2)}) collective-permute-start(bf16[176,2176]{1,0:T(8,128)(2,1)S(1)} %collective-permute-done.71), channel_id=1, source_target_pairs={{0,1},{1,0},{2,3},{3,2},{4,5},{5,4},{6,7},{7,6},{8,9},{9,8},{10,11... | collective-permute-start | bytes 2297864 | tf_op jit(solution)/shard_map/ppermute | solution.py:50
  366.7 59.0 %collective-permute-start.78 = (bf16[256,1280]{1,0:T(8,128)(2,1)S(1)}, bf16[256,1280]{1,0:T(8,128)(2,1)}, u32[]{:S(2)}, u32[]{:S(2)}) collective-permute-start(bf16[256,1280]{1,0:T(8,128)(2,1)S(1)} %copy-done.60), channel_id=1, source_target_pairs={{0,4},{1,5},{2,6},{3,7},{4,0},{5,1},{6,2},{7,3},{8,12},{9,13},{10,... | collective-permute-start | bytes 1966088 | tf_op jit(solution)/shard_map/ppermute | solution.py:50
  370.6 46.7 %collective-permute-start.52 = (bf16[256,2048]{1,0:T(8,128)(2,1)S(1)}, bf16[256,2048]{1,0:T(8,128)(2,1)S(1)}, u32[]{:S(2)}, u32[]{:S(2)}) collective-permute-start(bf16[256,2048]{1,0:T(8,128)(2,1)S(1)} %multiply_convert_fusion), channel_id=1, source_target_pairs={{0,16},{8,24},{16,0},{24,8},{1,17},{9,25},{17,1},{25,9},{2,18},{10... | collective-permute-start | bytes 3145736 | tf_op jit(solution)/shard_map/ppermute | solution.py:50
  424.8 39.9 %collective-permute-start.68 = (bf16[512,2048]{1,0:T(8,128)(2,1)}, bf16[512,2048]{1,0:T(8,128)(2,1)}, u32[]{:S(2)}, u32[]{:S(2)}) collective-permute-start(bf16[512,2048]{1,0:T(8,128)(2,1)} %pad_maximum_fusion.3), channel_id=1, source_target_pairs={{0,8},{8,0},{16,24},{24,16},{1,9},{9,1},{17,25},{25,17},{2,10},{10... | collective-permute-start | bytes 6291464 | tf_op jit(solution)/shard_map/ppermute | solution.py:50
  435.9 45.0 %collective-permute-start.74 = (bf16[256,1536]{1,0:T(8,128)(2,1)}, bf16[256,1536]{1,0:T(8,128)(2,1)}, u32[]{:S(2)}, u32[]{:S(2)}) collective-permute-start(bf16[256,1536]{1,0:T(8,128)(2,1)} %collective-permute-done.62.refs_5_), channel_id=1, source_target_pairs={{0,2},{1,3},{2,0},{3,1},{4,6},{5,7},{6,4},{7,5},{8,10},{9,11},{10,... | collective-permute-start | bytes 2359304 | tf_op jit(solution)/shard_map/ppermute | solution.py:50
  440.7 69.3 %collective-permute-start.75 = (bf16[256,1280]{1,0:T(8,128)(2,1)S(1)}, bf16[256,1280]{1,0:T(8,128)(2,1)}, u32[]{:S(2)}, u32[]{:S(2)}) collective-permute-start(bf16[256,1280]{1,0:T(8,128)(2,1)S(1)} %copy-done.60), channel_id=1, source_target_pairs={{0,1},{1,0},{2,3},{3,2},{4,5},{5,4},{6,7},{7,6},{8,9},{9,8},{10,11... | collective-permute-start | bytes 1966088 | tf_op jit(solution)/shard_map/ppermute | solution.py:50
  450.2 59.9 %collective-permute-start.79 = (bf16[256,1280]{1,0:T(8,128)(2,1)}, bf16[256,1280]{1,0:T(8,128)(2,1)}, u32[]{:S(2)}, u32[]{:S(2)}) collective-permute-start(bf16[256,1280]{1,0:T(8,128)(2,1)} %collective-permute-done.78.refs_4_.refs_12_), channel_id=1, source_target_pairs={{0,1},{1,0},{2,3},{3,2},{4,5},{5,4},{6,7},{7,6},{8,9},{9,8},{10,11... | collective-permute-start | bytes 1966088 | tf_op jit(solution)/shard_map/ppermute | solution.py:50
  464.2 45.8 %collective-permute-start.77 = (bf16[256,1280]{1,0:T(8,128)(2,1)}, bf16[256,1280]{1,0:T(8,128)(2,1)}, u32[]{:S(2)}, u32[]{:S(2)}) collective-permute-start(bf16[256,1280]{1,0:T(8,128)(2,1)} %collective-permute-done.76.refs_2_.refs_10_), channel_id=1, source_target_pairs={{0,1},{1,0},{2,3},{3,2},{4,5},{5,4},{6,7},{7,6},{8,9},{9,8},{10,11... | collective-permute-start | bytes 1966088 | tf_op jit(solution)/shard_map/ppermute | solution.py:50
  464.7 45.4 %collective-permute-start.81 = (bf16[256,1280]{1,0:T(8,128)(2,1)}, bf16[256,1280]{1,0:T(8,128)(2,1)}, u32[]{:S(2)}, u32[]{:S(2)}) collective-permute-start(bf16[256,1280]{1,0:T(8,128)(2,1)} %collective-permute-done.80.refs_6_.refs_14_), channel_id=1, source_target_pairs={{0,1},{1,0},{2,3},{3,2},{4,5},{5,4},{6,7},{7,6},{8,9},{9,8},{10,11... | collective-permute-start | bytes 1966088 | tf_op jit(solution)/shard_map/ppermute | solution.py:50
  651.0 57.5 %collective-permute-start.97 = (f32[1,2048]{1,0:T(1,128)S(1)}, f32[1,2048]{1,0:T(1,128)S(1)}, u32[]{:S(2)}, u32[]{:S(2)}) collective-permute-start(f32[1,2048]{1,0:T(1,128)S(1)} %bitcast.189), channel_id=1, source_target_pairs={{0,16},{8,24},{16,0},{24,8},{1,17},{9,25},{17,1},{25,9},{2,18},{10... | collective-permute-start | bytes 24584 | tf_op jit(solution)/shard_map/ppermute | solution.py:50
  790.4 37.0 %collective-permute-start.89 = (bf16[256,512]{1,0:T(8,128)(2,1)S(1)}, bf16[256,512]{1,0:T(8,128)(2,1)S(1)}, u32[]{:S(2)}, u32[]{:S(2)}) collective-permute-start(bf16[256,512]{1,0:T(8,128)(2,1)S(1)} %get-tuple-element.200), channel_id=1, source_target_pairs={{0,2},{1,3},{2,0},{3,1},{4,6},{5,7},{6,4},{7,5},{8,10},{9,11},{10,... | collective-permute-start | bytes 786440 | tf_op jit(solution)/shard_map/ppermute | solution.py:50
  807.4 37.2 %collective-permute-start.91 = (bf16[256,512]{1,0:T(8,128)(2,1)S(1)}, bf16[256,512]{1,0:T(8,128)(2,1)S(1)}, u32[]{:S(2)}, u32[]{:S(2)}) collective-permute-start(bf16[256,512]{1,0:T(8,128)(2,1)S(1)} %get-tuple-element.198), channel_id=1, source_target_pairs={{0,6},{1,7},{2,4},{3,5},{4,2},{5,3},{6,0},{7,1},{8,14},{9,15},{10,... | collective-permute-start | bytes 786440 | tf_op jit(solution)/shard_map/ppermute | solution.py:50
  810.3 51.4 %collective-permute-start.96 = (bf16[8,4,32,256]{3,2,1,0:T(8,128)(2,1)}, bf16[8,4,32,256]{3,2,1,0:T(8,128)(2,1)}, u32[]{:S(2)}, u32[]{:S(2)}) collective-permute-start(bf16[8,4,32,256]{3,2,1,0:T(8,128)(2,1)} %constant_dynamic-slice_fusion.1), channel_id=1, source_target_pairs={{0,1},{1,0},{2,3},{3,2},{4,5},{5,4},{6,7},{7,6},{8,9},{9,8},{10,11... | collective-permute-start | bytes 1572872 | tf_op jit(solution)/shard_map/ppermute | solution.py:50
  (342 other events, 5888.3 us)

commit v4 on v3

--- a/solution.py
+++ b/solution.py
@@ -410,7 +410,7 @@
             jax.ShapeDtypeStruct((KVH, CHUNKS, 1, rows), F32),
         ],
         compiler_params=pltpu.CompilerParams(vmem_limit_bytes=40 << 20),
-        cost_estimate=pl.CostEstimate(flops=40 << 30, bytes_accessed=64 << 20, transcendentals=0),
+        cost_estimate=pl.CostEstimate(flops=COST, bytes_accessed=COST, transcendentals=0),
     )(first_block, z, scale, cosine, sine, places, starts, kv, kvt)
 
 
@@ -1389,27 +1389,28 @@
     across = wide_count // 4
     deep, side = wide // across, wide % across
 
-    def to_tokens(features, gate=()):
-        pieces = features.reshape(CHUNKS, 4, across, block, share)
-        rows = jnp.zeros((4, CHUNKS, block, across * share), features.dtype)
+    def to_tokens(features):
+        many = features.shape[0]
+        pieces = features.reshape(many, CHUNKS, 4, across, block, share)
+        rows = jnp.zeros((4, many, CHUNKS, block, across * share), features.dtype)
         for slot in range(across):
-            piece = lax.dynamic_index_in_dim(pieces, side ^ slot, 2, keepdims=False)
-            piece = jnp.swapaxes(piece, 0, 1)
+            piece = lax.dynamic_index_in_dim(pieces, side ^ slot, 3, keepdims=False)
+            piece = jnp.moveaxis(piece, 2, 0)
             if slot:
                 piece = swap(piece, "wide", slot)
-            rows = lax.dynamic_update_slice(rows, piece, (0, 0, 0, (side ^ slot) * share))
-        whole = jnp.zeros((count, D), features.dtype)
+            rows = lax.dynamic_update_slice(rows, piece, (0, 0, 0, 0, (side ^ slot) * share))
+        whole = jnp.zeros((many, count, D), features.dtype)
         for slot in range(4):
             piece = lax.dynamic_index_in_dim(rows, deep ^ slot, 0, keepdims=False)
-            piece = piece.reshape(count, across * share)
+            piece = piece.reshape(many, count, across * share)
             if slot:
                 piece = swap(piece, "wide", slot * across)
-            if gate:
-                piece = after(piece, *gate)
-            whole = lax.dynamic_update_slice(whole, piece, (0, (deep ^ slot) * across * share))
+            whole = lax.dynamic_update_slice(
+                whole, piece, (0, 0, (deep ^ slot) * across * share)
+            )
         return whole
 
-    def from_tokens(rows):
+    def from_tokens_deep(rows):
         cols = across * share
         held = jnp.zeros((CHUNKS, 4, block, cols), rows.dtype)
         for slot in range(4):
@@ -1418,7 +1419,13 @@
                 piece = swap(piece, "wide", slot * across)
             piece = piece.reshape(CHUNKS, 1, block, cols)
             held = lax.dynamic_update_slice(held, piece, (0, deep ^ slot, 0, 0))
-        whole = jnp.zeros((CHUNKS, 4, across, block, share), rows.dtype)
+        return held
+
+    def from_tokens(rows):
+        return from_tokens_side(from_tokens_deep(rows))
+
+    def from_tokens_side(held):
+        whole = jnp.zeros((CHUNKS, 4, across, block, share), held.dtype)
         for slot in range(across):
             piece = lax.dynamic_slice_in_dim(held, (side ^ slot) * share, share, 3)
             if slot:
@@ -1449,7 +1456,8 @@
 
     KV, QUERY, OUT, MLP, DOWN = range(5)
 
-    residual = to_tokens(tokens).astype(F32)
+    both_rows = to_tokens(jnp.stack([tokens, cotangent]))
+    residual, upstream = both_rows[0].astype(F32), both_rows[1].astype(F32)
     gain_parts = jnp.stack([gain_attn, gain_ffn], axis=1)
     split = [lax.reduce_precision(gain_parts, 8, 7)]
     split.append(lax.reduce_precision(gain_parts - split[0], 8, 7))
@@ -1458,35 +1466,46 @@
         place, w_query, w_key, w_value, jnp.concatenate([adapt_main, *split], axis=1), adapt_outer
     )
     qkv_slots = [gather_slots(qkv_shard)]
-    mags = after(magnitudes, residual)[None]
-
-    def column_terms(squares, pieces):
-        norms = jnp.sqrt(all_sum(squares, ["wide"]))
-        rows = jnp.concatenate([piece[0] for piece in pieces], axis=1)
-        rows = jnp.concatenate([rows, norms])
-        out = []
-        for held in (rows, other_core(rows)):
-            mags_row, norm = held[:1], held[1:2]
-            scale, slope = mags_row / norm, -mags_row / (norm * norm * norm)
-            start = 0
-            split = []
-            for piece in pieces:
-                stop = start + piece[0].shape[1]
-                split.append((scale[:, start:stop], slope[:, start:stop], norm[:, start:stop]))
-                start = stop
-            out.append(split)
-        return out
-
-    soon = column_terms(
-        squares, [(by_core(sides(mags, 1), sides(mags, 2)),), (own_half(sides(mags, 0)),)]
-    )
-    scale_by, slope_by, norms_by = ([list(soon[k][n][i] for n in range(2)) for k in range(2)] for i in range(3))
+    mags = magnitudes[None]
+    out_shard, mlp_shard, down_shard, rest_squares, rest_cross, picked = later_work(
+        place, after(w_output, *near(qkv_slots[0])), w_gate, w_up, w_down, adapt_main, adapt_down,
+        adapt_outer, jnp.broadcast_to(mags, (8, OUTS)), part,
+    )
+    squares = jnp.concatenate([squares, rest_squares], axis=1)
+    crosses = jnp.concatenate([soon_cross, rest_cross], axis=1)
+    for bit in bits_of(wide_count):
+        sent = jnp.concatenate([crosses.astype(BF), *two_parts(squares)])
+        sent = swap(sent, "wide", bit).astype(F32)
+        crosses = crosses + sent[:RANK]
+        squares = squares + (sent[RANK : RANK + 1] + sent[RANK + 1 :])
+    norms_own = jnp.sqrt(squares)
+    mags_own = jnp.concatenate(
+        [
+            by_core(sides(mags, 1), sides(mags, 2)),
+            own_half(sides(mags, 0)),
+            own_half(sides(mags, 3)),
+            picked[RANK : RANK + 1],
+            own_half(sides(mags, 6)),
+        ],
+        axis=1,
+    )
+    own_rows = jnp.concatenate([crosses, mags_own, norms_own])
+    rows_by = [own_rows, other_core(own_rows)]
+    cross_by = [rows[:RANK] for rows in rows_by]
+    scale_by, slope_by, norms_by = [], [], []
+    for rows in rows_by:
+        mags_row, norm = rows[RANK : RANK + 1], rows[RANK + 1 :]
+        scale, slope = mags_row / norm, -mags_row / (norm * norm * norm)
+        for found, row in ((scale_by, scale), (slope_by, slope), (norms_by, norm)):
+            found.append([cut(row, n) for n in range(5)])
+    mlp_outer = [picked[:RANK]]
 
     def natural_of(parts, n):
         return in_order([p[n] for p in parts])
 
     scales, slopes, norms = (
-        [natural_of(parts, n) for n in range(2)] for parts in (scale_by, slope_by, norms_by)
+        [natural_of(parts, n) if n != MLP else None for n in range(5)]
+        for parts in (scale_by, slope_by, norms_by)
     )
     outers = [sides(adapt_outer, n) for n in range(7)]
     outer_kv = jnp.concatenate(
@@ -1546,10 +1565,6 @@
     kv = kv_form(kv_z, scales[KV], cosine, sine)
     token_slots = gather_slots(kv.reshape(CHUNKS, 1, block, KVH * 2 * HD))
 
-    out_shard, mlp_shard, down_shard, squares, rest_cross, picked = later_work(
-        place, after(w_output, *near(qkv_slots[0])), w_gate, w_up, w_down, adapt_main, adapt_down, adapt_outer,
-        jnp.broadcast_to(mags, (8, OUTS)), part,
-    )
     kv = jnp.zeros((CHUNKS, wide_count, block, KVH * 2 * HD), BF)
     for slot, held in token_slots.items():
         kv = lax.dynamic_update_slice(kv, held, (0, wide ^ slot, 0, 0))
@@ -1562,33 +1577,19 @@
         first_block, query_z, scales[QUERY], cosine, sine, place_rows, start_rows, kv, kvt
     )
 
-    rest = column_terms(
-        after(squares, attended),
-        [(own_half(sides(mags, 3)),), (picked[RANK : RANK + 1],), (own_half(sides(mags, 6)),)],
-    )
-    mlp_outer = [picked[:RANK]]
-    for found, index in ((scale_by, 0), (slope_by, 1), (norms_by, 2)):
-        for k in range(2):
-            found[k].extend(rest[k][n][index] for n in range(3))
-    for found, parts in ((scales, scale_by), (slopes, slope_by), (norms, norms_by)):
-        found.extend(natural_of(parts, n) if n != MLP else None for n in range(2, 5))
-
-    down_slots = gather_slots(after(down_shard, *near(qkv_slots[0])))
-    out_slots = [gather_slots(after(out_shard, *near(down_slots)), True)]
+    down_slots = gather_slots(after(down_shard, *near(token_slots)))
+    out_slots = [gather_slots(after(out_shard, qkv_slots[0][wide_count - 1]), True)]
     out_slots.append({s: other_core(held) for s, held in out_slots[0].items()})
     down_weights = put_rows(down_slots, jnp.zeros((0, D + EXTRA), BF))
     tiles = 2 * block_cols // 256
     cuts = [0, (tiles + 1) // 2 * 256, 2 * block_cols]
     spans = [slice(cuts[i], cuts[i + 1]) for i in range(2)]
     mlp_slots = []
-    before = near(out_slots[0])
+    before = near(down_slots)
     for i, span in enumerate(spans):
         mlp_slots.append(gather_slots(after(mlp_shard[:, span], *before), i == 0))
         before = near(mlp_slots[-1])
 
-    upstream = to_tokens(
-        after(cotangent, kv, *near(out_slots[0])), far(mlp_slots[0], 2)
-    ).astype(F32)
     output_z, reduced_out = slot_mm(
         place, attended, low_main, outers[3], 3 * RANK, [ordered(out_slots[k]) for k in range(2)]
     )
@@ -1599,8 +1600,8 @@
         pair = jnp.concatenate([rows, partner(rows)])
         return jnp.concatenate([pair, other_core(pair)])
 
-    def to_owner_of_four(keep, sent, *behind):
-        pair = keep + other_core(after(sent, *behind) if behind else sent).astype(F32)
+    def to_owner_of_four(keep, sent):
+        pair = keep + other_core(sent).astype(F32)
         swapped = partner(pair[count:].astype(BF))
         return pair[:count] + swapped.astype(F32), swapped
 
@@ -1609,11 +1610,6 @@
     down_low = of_four(down_low)
     narrow_down = 2.0 * mm_t(down_low, outers[6].astype(BF))
     narrow_down_lanes = lanes_of(narrow_down)
-    crosses = after(jnp.concatenate([soon_cross, rest_cross], axis=1), normed_own)
-    for bit in bits_of(wide_count):
-        crosses = crosses + swap(crosses.astype(BF), "wide", bit).astype(F32)
-    cross_by = [crosses, other_core(crosses)]
-    normed_two = after(normed_two, *cross_by)
     packs = pack_reduced(normed_two, low_main, 4 * RANK, 2 * RANK)
     blocks = [
         mlp_block(
@@ -1649,8 +1645,7 @@
     )
     grad_normed, swapped = to_owner_of_four(keep, sent)
     grad_mid = upstream + norm_rows_back(hidden_one, gains[1], inverse_two, grad_normed)
-    down_z, _ = to_owner_of_four(down_keep, down_sent, swapped)
-    layer_rows = (hidden_one + down_z * scales[DOWN]).astype(BF)
+    down_pair = down_keep + other_core(after(down_sent, swapped)).astype(F32)
 
     def first_grads(rows, inputs, narrow, middle, factors, many):
         size = many * RANK
@@ -1671,40 +1666,27 @@
     grad_mixed, first_out = finish_back(
         [back_out], [RANK], narrow_out, middle_out, low_main, attended, 3 * RANK
     )
-    grad_mixed = grad_mixed.astype(BF)
+    grad_mixed = after(grad_mixed.astype(BF), down_pair)
+    down_far = partner(down_pair[count:].astype(BF))
+    down_z = down_pair[:count] + down_far.astype(F32)
+    layer_rows = (hidden_one + down_z * scales[DOWN]).astype(BF)
 
     query_grad, kv_grad = attend_back(
         first_block, queries, cosine, sine, place_rows, start_rows, kv, kvt, log_total, attended,
         grad_mixed,
     )
     kv_grad = kv_grad.reshape(CHUNKS, wide_count, block, KVH * 2 * HD)
-    kv_grad = jnp.swapaxes(kv_grad, 0, 1).astype(F32)
-    kv_grad = scatter_sum(kv_grad, "wide", BF)
-    kv_grad = kv_back(kv_grad.reshape(count, KVH * 2 * HD), cosine, sine)
-    layer_out = from_tokens(after(layer_rows, kv_grad))
-
-    query_rows_low, scale_query, outer_query, narrow_query, middle_query = grad_terms(
-        query_grad, query_z, scales[QUERY], slopes[QUERY], outers[0], 0, reduced_one
-    )
-    back_query = slot_back(place, query_rows_low, [ordered(qkv_slots[k]) for k in range(2)])
-    kv_rows_low, scale_kv, outer_kv_grad, narrow_kv, middle_kv = grad_terms(
-        kv_grad, kv_z, scales[KV], slopes[KV], outer_kv,
-        RANK, reduced_one,
-    )
-    back_kv = slot_back(place, kv_rows_low, [ordered(qkv_slots[k]) for k in range(2)], half)
-    grad_normed, first_one = finish_back(
-        [back_query, back_kv],
-        [RANK, pairs],
-        narrow_query + narrow_kv,
-        jnp.concatenate([middle_query, middle_kv]),
-        low_main,
-        normed_one,
-        0,
-    )
-    grad_tokens = from_tokens(
-        (grad_mid + norm_rows_back(residual, gains[0], inverse_one, grad_normed)).astype(BF)
-    )
-
+    kv_grad = jnp.swapaxes(after(kv_grad, down_far), 0, 1).astype(F32)
+    bits = bits_of(wide_count)
+    kv_half = KVH * HD
+    kv_grad = jnp.concatenate(
+        [
+            scatter_sum(kv_grad[..., :kv_half], "wide", BF),
+            scatter_sum(kv_grad[..., kv_half:], "wide", BF, [bits[-2], *bits[:-2], bits[-1]]),
+        ],
+        axis=-1,
+    )
+    layer_deep = from_tokens_deep(after(layer_rows, kv_grad))
     scale_down = jnp.sum(upstream * down_z, axis=0, keepdims=True)
     pair_down = scale_down + partner(scale_down)
     pair_down = pair_down + other_core(pair_down)
@@ -1719,6 +1701,33 @@
         down_weights[:, D : D + RANK],
         1,
     )
+    kv_grad = kv_back(
+        after(kv_grad, first_down).reshape(count, KVH * 2 * HD), cosine, sine
+    )
+    layer_out = from_tokens_side(after(layer_deep, kv_grad))
+
+    query_rows_low, scale_query, outer_query, narrow_query, middle_query = grad_terms(
+        query_grad, query_z, scales[QUERY], slopes[QUERY], outers[0], 0, reduced_one
+    )
+    back_query = slot_back(place, query_rows_low, [ordered(qkv_slots[k]) for k in range(2)])
+    kv_rows_low, scale_kv, outer_kv_grad, narrow_kv, middle_kv = grad_terms(
+        kv_grad, kv_z, scales[KV], slopes[KV], outer_kv,
+        RANK, reduced_one,
+    )
+    back_kv = slot_back(place, kv_rows_low, [ordered(qkv_slots[k]) for k in range(2)], half)
+    grad_normed, first_one = finish_back(
+        [back_query, after(back_kv, layer_deep)],
+        [RANK, pairs],
+        narrow_query + narrow_kv,
+        jnp.concatenate([middle_query, middle_kv]),
+        low_main,
+        normed_one,
+        0,
+    )
+    grad_tokens = from_tokens(
+        (grad_mid + norm_rows_back(residual, gains[0], inverse_one, grad_normed)).astype(BF)
+    )
+
     outer_down = 2.0 * fold_parts(
         t_mm(jnp.concatenate(two_parts(reduced_down), axis=1), down_low), RANK
     )
@@ -1763,7 +1772,7 @@
         (tall, down_width, lanes, share, hidden_share, outer_share),
     )
     packed = packed.reshape((tok_count, wide_count) + packed.shape[1:])
-    packed = scatter_sum(scatter_sum(packed, "tok"), "wide")
+    packed = scatter_sum(scatter_sum(packed, "tok", BF), "wide", BF)
     main_part = jnp.swapaxes(packed[:tall].reshape(tall, fit, share), 0, 1)
     main_part = main_part.reshape(main_width, share).T
     down_part = packed[tall : tall + down_width, :hidden_share].T

time: 892 us -> 848 us (0.951)
  starting transfers between devices: 115 us -> 92 us
  local copies, waits for them, and re-layouts: 119 us -> 104 us
    ppermute x109 -> x100, starting transfers between devices: 115 us -> 92 us  [swap(): return lax.ppermute(array, axis, [(i, i ^ distance) for i in range(count)])]
    slice x4 -> x18, local copies, waits for them, and re-layouts: 2.59 us -> 14.2 us  [cut(): return array[..., ends[n]:ends[n + 1]]]
    unnamed x529 -> x462, local copies, waits for them, and re-layouts: 49.2 us -> 51.2 us
    ppermute x109 -> x100, waiting for transfers between devices: 338 us -> 337 us  [swap(): return lax.ppermute(array, axis, [(i, i ^ distance) for i in range(count)])]
  transfers between devices with their start and end apart: 109 -> 100, of which waited for: 44 -> 42; matrix products, arithmetic and copies ran while one was open for 13% -> 12% of each run, Pallas kernels for 17% -> 17%
where the time goes in v4:
time: 848 us; the launch traced here: 838 us
  waiting for transfers between devices  337 us (40%)
  Pallas kernels  227 us (27%)
  local copies, waits for them, and re-layouts  104 us (12%)
  starting transfers between devices  92 us (11%)
  other arithmetic  58.5 us (7%)
  matrix products  11.5 us (1%)
  between operations  9.21 us (1%)
    ppermute x100, waiting for transfers between devices, swap(): return lax.ppermute(array, axis, [(i, i ^ distance) for i in range(count)])  337 us
    ppermute x100, starting transfers between devices, swap(): return lax.ppermute(array, axis, [(i, i ^ distance) for i in range(count)])  92 us
    unnamed x462, local copies, waits for them, and re-layouts  51.2 us
    pallas_call x2, Pallas kernels, mlp_block(): pl.pallas_call(functools.partial(mlp_kernel, offset=offset), grid_spec=pl...  48.6 us
    pallas_call x1, Pallas kernels, mlp_back(): pl.pallas_call(functools.partial(mlp_back_kernel, offset=offset, rank=ran...  40.8 us
    pallas_call x1, Pallas kernels, attend_back(): pl.pallas_call(functools.partial(backward_kernel, block=block, span=span,...  23.6 us
    pallas_call x3, Pallas kernels, slot_back(): pl.pallas_call(functools.partial(slot_back_kernel, skip=skip), grid_spec=...  22.4 us
    pallas_call x3, Pallas kernels, slot_mm(): pl.pallas_call(functools.partial(slot_kernel, offset=offset), grid_spec=p...  22.1 us
  transfers between devices with their start and end apart: 100, of which 42 were waited for; matrix products, arithmetic and copies ran while one was open for 12% of the time, Pallas kernels for 17%

profile of v4, /device:TPU:0, one launch (start us, length us, event | category | flops | bytes accessed | tf_op | source)
XLA Modules:
  0.0 838.0 jit_solution(10211762233146777405)
XLA Ops:
  30.4 14.3 %collective-permute-done.6.refs_4_ = bf16[256,1408]{1,0:T(8,128)(2,1)S(1)} collective-permute-done((bf16[256,1408]{1,0:T(8,128)(2,1)S(1)}, bf16[256,1408]{1,0:T(8,128)(2,1)S(1)}, u32[]{:S(2)}, u32[]{:S(2)}) %collective-permute-start.6) | collective-permute-done | bytes 720928 | tf_op jit(solution)/shard_map/ppermute | solution.py:50
  45.0 13.6 %shard_map.345 = (bf16[256,1024]{1,0:T(8,128)(2,1)S(1)}, bf16[256,2816]{1,0:T(8,128)(2,1)}, bf16[176,2176]{1,0:T(8,128)(2,1)S(1)}, f32[1,4864]{1,0:T(1,128)S(1)}...) custom-call(s32[3]{0:T(128)S(1)} %pad_add_fusion.place_ref, bf16[256,2048]{1,0:T(8,128)(2,1)S(1)} %copy-done.105, ...), custom_call_target="tpu_custom_call" | custom-call | flops 1024 | bytes 1024 | tf_op jit(solution)/shard_map/pallas_call | solution.py:1326
  72.7 9.7 %collective-permute-done.20 = bf16[18,6144]{1,0:T(8,128)(2,1)S(1)} collective-permute-done((bf16[18,6144]{1,0:T(8,128)(2,1)S(1)}, bf16[18,6144]{1,0:T(8,128)(2,1)S(1)}, u32[]{:S(2)}, u32[]{:S(2)}) %collective-permute-start.20) | collective-permute-done | bytes 221216 | tf_op jit(solution)/shard_map/ppermute | solution.py:50
  84.5 10.9 %collective-permute-done.21 = bf16[18,6144]{1,0:T(8,128)(2,1)S(1)} collective-permute-done((bf16[18,6144]{1,0:T(8,128)(2,1)S(1)}, bf16[18,6144]{1,0:T(8,128)(2,1)S(1)}, u32[]{:S(2)}, u32[]{:S(2)}) %collective-permute-start.21) | collective-permute-done | bytes 221216 | tf_op jit(solution)/shard_map/ppermute | solution.py:50
  105.8 12.0 %collective-permute-done.1 = bf16[2,256,512]{2,1,0:T(8,128)(2,1)S(1)} collective-permute-done((bf16[2,256,512]{2,1,0:T(8,128)(2,1)S(1)}, bf16[2,256,512]{2,1,0:T(8,128)(2,1)S(1)}, u32[]{:S(2)}, u32[]{:S(2)}) %collective-permute-start.1) | collective-permute-done | bytes 524320 | tf_op jit(solution)/shard_map/ppermute | solution.py:50
  117.8 23.6 %collective-permute-done.2 = bf16[2,256,512]{2,1,0:T(8,128)(2,1)S(1)} collective-permute-done((bf16[2,256,512]{2,1,0:T(8,128)(2,1)S(1)}, bf16[2,256,512]{2,1,0:T(8,128)(2,1)S(1)}, u32[]{:S(2)}, u32[]{:S(2)}) %collective-permute-start.2) | collective-permute-done | bytes 524320 | tf_op jit(solution)/shard_map/ppermute | solution.py:50
  147.2 15.4 %collective-permute-done.10.refs_7_ = bf16[256,1408]{1,0:T(8,128)(2,1)S(1)} collective-permute-done((bf16[256,1408]{1,0:T(8,128)(2,1)S(1)}, bf16[256,1408]{1,0:T(8,128)(2,1)S(1)}, u32[]{:S(2)}, u32[]{:S(2)}) %collective-permute-start.10) | collective-permute-done | bytes 720928 | tf_op jit(solution)/shard_map/ppermute | solution.py:50
  180.5 12.5 %collective-permute-done.33.refs_4_ = bf16[256,1024]{1,0:T(8,128)(2,1)} collective-permute-done((bf16[256,1024]{1,0:T(8,128)(2,1)S(1)}, bf16[256,1024]{1,0:T(8,128)(2,1)}, u32[]{:S(2)}, u32[]{:S(2)}) %collective-permute-start.33) | collective-permute-done | bytes 524320 | tf_op jit(solution)/shard_map/ppermute | solution.py:50
  211.4 7.4 collective-permute-done.32.refs_3_
  239.9 9.1 %shard_map.344 = (f32[256,2048]{1,0:T(8,128)}, f32[256,128]{1,0:T(8,128)}) custom-call(s32[3]{0:T(128)S(1)} %pad_add_fusion.place_ref, bf16[256,2048]{1,0:T(8,128)(2,1)S(1)} %copy-done.5, bf16[2048,128]{1,0:T(8,128)(2,1)S(1)} %slice_dynamic-update-slice_fusion.first_ref.refs_3_.refs_4_, f32[16,2048]{1,0:T(8,128)S(1)} %get-tuple-element.194.outer_ref, ...), custom_call_target="tpu_custom_call" | custom-call | flops 1024 | bytes 1024 | tf_op jit(solution)/shard_map/pallas_call | solution.py:527
  258.1 19.1 %shard_map.348 = (bf16[256,2048]{1,0:T(8,128)(2,1)S(1)}, bf16[256,2048]{1,0:T(8,128)(2,1)S(1)}, f32[4,8,1,256]{3,2,1,0:T(1,128)S(1)}) custom-call(s32[8]{0:T(128)S(1)} %and_select_fusion.1.first_ref, f32[256,2048]{1,0:T(8,128)S(1)} %copy-done.66, f32[1,2048]{1,0:T(1,128)S(1)} %broadcast_select_fusion.7.scale_ref, f32[256,128]{1,0:T(8,128)S(1)} %copy-done.91, ...), custom_call_target="tpu_custom_call" | custom-call | flops 1024 | bytes 1024 | tf_op jit(solution)/shard_map/pallas_call | solution.py:404
  279.2 9.6 %shard_map.349 = (f32[256,2048]{1,0:T(8,128)S(1)}, f32[256,128]{1,0:T(8,128)S(1)}) custom-call(s32[3]{0:T(128)S(1)} %pad_add_fusion.place_ref, bf16[256,2048]{1,0:T(8,128)(2,1)S(1)} %get-tuple-element.96.inputs_ref.refs_4_.out_ref, bf16[2048,128]{1,0:T(8,128)(2,1)S(1)} %slice_dynamic-update-slice_fusion.first_ref.refs_3_.refs_4_, ...), custom_call_target="tpu_custom_call" | custom-call | flops 1024 | bytes 1024 | tf_op jit(solution)/shard_map/pallas_call | solution.py:527
  298.4 12.6 %collective-permute-done.50 = bf16[176,2176]{1,0:T(8,128)(2,1)S(1)} collective-permute-done((bf16[176,2176]{1,0:T(8,128)(2,1)S(1)}, bf16[176,2176]{1,0:T(8,128)(2,1)S(1)}, u32[]{:S(2)}, u32[]{:S(2)}) %collective-permute-start.50) | collective-permute-done | bytes 765984 | tf_op jit(solution)/shard_map/ppermute | solution.py:50
  329.9 25.5 %collective-permute-done.54 = bf16[176,2176]{1,0:T(8,128)(2,1)} collective-permute-done((bf16[176,2176]{1,0:T(8,128)(2,1)}, bf16[176,2176]{1,0:T(8,128)(2,1)}, u32[]{:S(2)}, u32[]{:S(2)}) %collective-permute-start.54) | collective-permute-done | bytes 765984 | tf_op jit(solution)/shard_map/ppermute | solution.py:50
  356.7 14.0 %collective-permute-done.57.refs_2_ = bf16[256,1536]{1,0:T(8,128)(2,1)} collective-permute-done((bf16[256,1536]{1,0:T(8,128)(2,1)S(1)}, bf16[256,1536]{1,0:T(8,128)(2,1)}, u32[]{:S(2)}, u32[]{:S(2)}) %collective-permute-start.57) | collective-permute-done | bytes 786464 | tf_op jit(solution)/shard_map/ppermute | solution.py:50
  377.5 13.5 %collective-permute-done.53 = bf16[176,2176]{1,0:T(8,128)(2,1)S(1)} collective-permute-done((bf16[176,2176]{1,0:T(8,128)(2,1)}, bf16[176,2176]{1,0:T(8,128)(2,1)S(1)}, u32[]{:S(2)}, u32[]{:S(2)}) %collective-permute-start.53) | collective-permute-done | bytes 765984 | tf_op jit(solution)/shard_map/ppermute | solution.py:50
  391.9 10.4 %collective-permute-done.66.refs_4_.refs_12_ = bf16[256,1280]{1,0:T(8,128)(2,1)} collective-permute-done((bf16[256,1280]{1,0:T(8,128)(2,1)S(1)}, bf16[256,1280]{1,0:T(8,128)(2,1)}, u32[]{:S(2)}, u32[]{:S(2)}) %collective-permute-start.66) | collective-permute-done | bytes 655392 | tf_op jit(solution)/shard_map/ppermute | solution.py:50
  404.3 12.1 %collective-permute-done.64.refs_2_.refs_10_ = bf16[256,1280]{1,0:T(8,128)(2,1)} collective-permute-done((bf16[256,1280]{1,0:T(8,128)(2,1)S(1)}, bf16[256,1280]{1,0:T(8,128)(2,1)}, u32[]{:S(2)}, u32[]{:S(2)}) %collective-permute-start.64) | collective-permute-done | bytes 655392 | tf_op jit(solution)/shard_map/ppermute | solution.py:50
  430.3 8.7 %collective-permute-done.58.refs_3_ = bf16[256,1536]{1,0:T(8,128)(2,1)} collective-permute-done((bf16[256,1536]{1,0:T(8,128)(2,1)}, bf16[256,1536]{1,0:T(8,128)(2,1)}, u32[]{:S(2)}, u32[]{:S(2)}) %collective-permute-start.58) | collective-permute-done | bytes 786464 | tf_op jit(solution)/shard_map/ppermute | solution.py:50
  441.0 11.1 %collective-permute-done.68.refs_6_.refs_14_ = bf16[256,1280]{1,0:T(8,128)(2,1)} collective-permute-done((bf16[256,1280]{1,0:T(8,128)(2,1)}, bf16[256,1280]{1,0:T(8,128)(2,1)}, u32[]{:S(2)}, u32[]{:S(2)}) %collective-permute-start.68) | collective-permute-done | bytes 655392 | tf_op jit(solution)/shard_map/ppermute | solution.py:50
  470.5 25.9 %shard_map.351 = (bf16[1024,768]{1,0:T(8,128)(2,1)}, bf16[1088,1536]{1,0:T(8,128)(2,1)}, f32[1,1536]{1,0:T(1,128)S(1)}, f32[16,1536]{1,0:T(8,128)S(1)}, f32[1024,128]{1,0:T(8,128)S(1)}, /*index=5*/f32[32,128]{1,0:T(8,128)S(1)}) custom-call(s32[3]{0:T(128)S(1)} %pad_add_fusion.place_ref, bf16[1024,2048]{1,0:T(8,128)(2,1)} %pad_maximum_fusion.inputs_ref, ...), custom_call_target="tpu_custom_call" | custom-call | flops 1024 | bytes 1024 | tf_op jit(solution)/shard_map/pallas_call | solution.py:862
  496.9 22.7 %shard_map.352 = (bf16[1024,640]{1,0:T(8,128)(2,1)}, bf16[1088,1280]{1,0:T(8,128)(2,1)}, f32[1,1280]{1,0:T(1,128)S(1)}, f32[16,1280]{1,0:T(8,128)S(1)}, f32[1024,128]{1,0:T(8,128)S(1)}, /*index=5*/f32[32,128]{1,0:T(8,128)S(1)}) custom-call(s32[3]{0:T(128)S(1)} %pad_add_fusion.place_ref, bf16[1024,2048]{1,0:T(8,128)(2,1)} %pad_maximum_fusion.inputs_ref, ...), custom_call_target="tpu_custom_call" | custom-call | flops 1024 | bytes 1024 | tf_op jit(solution)/shard_map/pallas_call | solution.py:862
  521.1 40.8 %shard_map.354 = (f32[512,2048]{1,0:T(8,128)}, bf16[512,2048]{1,0:T(8,128)(2,1)}, f32[32,2048]{1,0:T(8,128)}) custom-call(s32[3]{0:T(128)} %copy-done.130, bf16[1088,1536]{1,0:T(8,128)(2,1)} %get-tuple-element.111.one_ref, bf16[1088,1280]{1,0:T(8,128)(2,1)} %get-tuple-element.112.two_ref, f32[1024,128]{1,0:T(8,128)} %add.601.narrow_ref, ...), custom_call_target="tpu_custom_call" | custom-call | flops 1024 | bytes 1024 | tf_op jit(solution)/shard_map/pallas_call | solution.py:1136
  574.7 13.2 %shard_map.353 = (f32[512,2048]{1,0:T(8,128)S(1)}, bf16[512,2048]{1,0:T(8,128)(2,1)}, f32[1024,128]{1,0:T(8,128)S(1)}) custom-call(bf16[1024,768]{1,0:T(8,128)(2,1)S(1)} %copy-done.94, bf16[1024,640]{1,0:T(8,128)(2,1)S(1)} %copy-done.96, bf16[1408,2176]{1,0:T(8,128)(2,1)} %constant_dynamic-update-slice_fusion.19.first_ref.down_ref.refs_2_.refs_3_, ...), custom_call_target="tpu_custom_call" | custom-call | flops 1024 | bytes 1024 | tf_op jit(solution)/shard_map/pallas_call | solution.py:926
  590.0 7.1 collective-permute-done.71
  612.4 21.2 %collective-permute-done.73 = bf16[256,2048]{1,0:T(8,128)(2,1)S(1)} collective-permute-done((bf16[256,2048]{1,0:T(8,128)(2,1)S(1)}, bf16[256,2048]{1,0:T(8,128)(2,1)S(1)}, u32[]{:S(2)}, u32[]{:S(2)}) %collective-permute-start.73) | collective-permute-done | bytes 1048608 | tf_op jit(solution)/shard_map/ppermute | solution.py:50
  638.3 8.1 shard_map.356.refs_0_
  650.3 23.6 %shard_map.358 = (f32[256,2048]{1,0:T(8,128)S(1)}, bf16[2048,512]{1,0:T(8,128)(2,1)S(1)}) custom-call(s32[8]{0:T(128)S(1)} %and_select_fusion.1.first_ref, bf16[256,2048]{1,0:T(8,128)(2,1)S(1)} %copy-done.138, f32[256,128]{1,0:T(8,128)S(1)} %copy-done.92, f32[256,128]{1,0:T(8,128)S(1)} %copy-done.90, s32[8,1,256]{2,1,0:T(1,128)S(1)} %tile.39.place_ref, ...), custom_call_target="tpu_custom_call" | custom-call | flops 42949672960 | bytes 67108864 | tf_op jit(solution)/shard_map/pallas_call | solution.py:447
  681.2 9.6 %shard_map.361.refs_0_ = f32[288,2048]{1,0:T(8,128)} custom-call(s32[3]{0:T(128)S(1)} %copy-done.131, bf16[288,2048]{1,0:T(8,128)(2,1)S(1)} %get-tuple-element.135.grad_ref, bf16[256,1408]{1,0:T(8,128)(2,1)S(1)} %get-tuple-element.87.refs_0_, bf16[256,1408]{1,0:T(8,128)(2,1)} %collective-permute-done.4.refs_1_, bf16[256,1408]{1,0:T(8,128)(2,1)S(1)} %copy-done.13, ...), custom_call_target="tpu_custom_call" | custom-call | flops 1024 | bytes 1024 | tf_op jit(solution)/shard_map/pallas_call | solution.py:634
  714.0 8.8 %collective-permute-done.76 = bf16[8,32,256]{2,1,0:T(8,128)(2,1)S(1)} collective-permute-done((bf16[8,32,256]{2,1,0:T(8,128)(2,1)S(1)}, bf16[8,32,256]{2,1,0:T(8,128)(2,1)S(1)}, u32[]{:S(2)}, u32[]{:S(2)}) %collective-permute-start.76) | collective-permute-done | bytes 131104 | tf_op jit(solution)/shard_map/ppermute | solution.py:50
  777.1 12.6 %collective-permute-done.92 = bf16[2,2,32,768]{3,2,1,0:T(8,128)(2,1)S(1)} collective-permute-done((bf16[2,2,32,768]{3,2,1,0:T(8,128)(2,1)S(1)}, bf16[2,2,32,768]{3,2,1,0:T(8,128)(2,1)S(1)}, u32[]{:S(2)}, u32[]{:S(2)}) %collective-permute-start.92) | collective-permute-done | bytes 196640 | tf_op jit(solution)/shard_map/ppermute | solution.py:50
  811.2 10.4 %collective-permute-done.97 = f32[8,128]{1,0:T(8,128)S(1)} collective-permute-done((f32[8,128]{1,0:T(8,128)S(1)}, f32[8,128]{1,0:T(8,128)S(1)}, u32[]{:S(2)}, u32[]{:S(2)}) %collective-permute-start.97) | collective-permute-done | bytes 4128 | tf_op jit(solution)/shard_map/ppermute | solution.py:50
  (904 shorter events, 359.8 us)
Async XLA Ops:
  8.9 35.8 %collective-permute-start.6 = (bf16[256,1408]{1,0:T(8,128)(2,1)S(1)}, bf16[256,1408]{1,0:T(8,128)(2,1)S(1)}, u32[]{:S(2)}, u32[]{:S(2)}) collective-permute-start(bf16[256,1408]{1,0:T(8,128)(2,1)S(1)} %get-tuple-element.87.refs_0_), channel_id=1, source_target_pairs={{0,4},{1,5},{2,6},{3,7},{4,0},{5,1},{6,2},{7,3},{8,12},{9,13},{10,... | collective-permute-start | bytes 2162696 | tf_op jit(solution)/shard_map/ppermute | solution.py:50
  16.1 146.6 %collective-permute-start.11 = (bf16[256,1408]{1,0:T(8,128)(2,1)S(1)}, bf16[256,1408]{1,0:T(8,128)(2,1)}, u32[]{:S(2)}, u32[]{:S(2)}) collective-permute-start(bf16[256,1408]{1,0:T(8,128)(2,1)S(1)} %get-tuple-element.87.refs_0_), channel_id=1, source_target_pairs={{0,8},{8,0},{16,24},{24,16},{1,9},{9,1},{17,25},{25,17},{2,10},{10... | collective-permute-start | bytes 2162696 | tf_op jit(solution)/shard_map/ppermute | solution.py:50
  19.9 50.9 %collective-permute-start = (bf16[4,2,8,32,256]{4,3,2,1,0:T(8,128)(2,1)}, bf16[4,2,8,32,256]{4,3,2,1,0:T(8,128)(2,1)}, u32[]{:S(2)}, u32[]{:S(2)}) collective-permute-start(bf16[4,2,8,32,256]{4,3,2,1,0:T(8,128)(2,1)} %bitcast.176), channel_id=1, source_target_pairs={{0,1},{1,0},{2,3},{3,2},{4,5},{5,4},{6,7},{7,6},{8,9},{9,8},{10,11... | collective-permute-start | bytes 3145736 | tf_op jit(solution)/shard_map/ppermute | solution.py:50
  60.5 42.6 %collective-permute-start.7 = (bf16[256,1408]{1,0:T(8,128)(2,1)S(1)}, bf16[256,1408]{1,0:T(8,128)(2,1)S(1)}, u32[]{:S(2)}, u32[]{:S(2)}) collective-permute-start(bf16[256,1408]{1,0:T(8,128)(2,1)S(1)} %collective-permute-done.5.refs_2_), channel_id=1, source_target_pairs={{0,1},{1,0},{2,3},{3,2},{4,5},{5,4},{6,7},{7,6},{8,9},{9,8},{10,11... | collective-permute-start | bytes 2162696 | tf_op jit(solution)/shard_map/ppermute | solution.py:50
  61.1 42.2 %collective-permute-start.8 = (bf16[256,1408]{1,0:T(8,128)(2,1)S(1)}, bf16[256,1408]{1,0:T(8,128)(2,1)S(1)}, u32[]{:S(2)}, u32[]{:S(2)}) collective-permute-start(bf16[256,1408]{1,0:T(8,128)(2,1)S(1)} %collective-permute-done.6.refs_4_), channel_id=1, source_target_pairs={{0,1},{1,0},{2,3},{3,2},{4,5},{5,4},{6,7},{7,6},{8,9},{9,8},{10,11... | collective-permute-start | bytes 2162696 | tf_op jit(solution)/shard_map/ppermute | solution.py:50
  70.7 34.9 %collective-permute-start.9 = (bf16[256,1408]{1,0:T(8,128)(2,1)S(1)}, bf16[256,1408]{1,0:T(8,128)(2,1)S(1)}, u32[]{:S(2)}, u32[]{:S(2)}) collective-permute-start(bf16[256,1408]{1,0:T(8,128)(2,1)S(1)} %collective-permute-done.6.refs_4_), channel_id=1, source_target_pairs={{0,2},{1,3},{2,0},{3,1},{4,6},{5,7},{6,4},{7,5},{8,10},{9,11},{10,... | collective-permute-start | bytes 2162696 | tf_op jit(solution)/shard_map/ppermute | solution.py:50
  103.1 38.3 %collective-permute-start.2 = (bf16[2,256,512]{2,1,0:T(8,128)(2,1)S(1)}, bf16[2,256,512]{2,1,0:T(8,128)(2,1)S(1)}, u32[]{:S(2)}, u32[]{:S(2)}) collective-permute-start(bf16[2,256,512]{2,1,0:T(8,128)(2,1)S(1)} %bitcast.206), channel_id=1, source_target_pairs={{0,4},{1,5},{2,6},{3,7},{4,0},{5,1},{6,2},{7,3},{8,12},{9,13},{10,... | collective-permute-start | bytes 1572872 | tf_op jit(solution)/shard_map/ppermute | solution.py:50
  103.3 38.2 %collective-permute-start.3 = (bf16[2,256,512]{2,1,0:T(8,128)(2,1)S(1)}, bf16[2,256,512]{2,1,0:T(8,128)(2,1)S(1)}, u32[]{:S(2)}, u32[]{:S(2)}) collective-permute-start(bf16[2,256,512]{2,1,0:T(8,128)(2,1)S(1)} %bitcast.205), channel_id=1, source_target_pairs={{0,6},{1,7},{2,4},{3,5},{4,2},{5,3},{6,0},{7,1},{8,14},{9,15},{10,... | collective-permute-start | bytes 1572872 | tf_op jit(solution)/shard_map/ppermute | solution.py:50
  105.7 57.6 %collective-permute-start.15 = (bf16[256,1408]{1,0:T(8,128)(2,1)S(1)}, bf16[256,1408]{1,0:T(8,128)(2,1)S(1)}, u32[]{:S(2)}, u32[]{:S(2)}) collective-permute-start(bf16[256,1408]{1,0:T(8,128)(2,1)S(1)} %collective-permute-done.6.refs_4_), channel_id=1, source_target_pairs={{0,8},{8,0},{16,24},{24,16},{1,9},{9,1},{17,25},{25,17},{2,10},{10... | collective-permute-start | bytes 2162696 | tf_op jit(solution)/shard_map/ppermute | solution.py:50
  117.8 45.8 %collective-permute-start.13 = (bf16[256,1408]{1,0:T(8,128)(2,1)S(1)}, bf16[256,1408]{1,0:T(8,128)(2,1)S(1)}, u32[]{:S(2)}, u32[]{:S(2)}) collective-permute-start(bf16[256,1408]{1,0:T(8,128)(2,1)S(1)} %collective-permute-done.5.refs_2_), channel_id=1, source_target_pairs={{0,8},{8,0},{16,24},{24,16},{1,9},{9,1},{17,25},{25,17},{2,10},{10... | collective-permute-start | bytes 2162696 | tf_op jit(solution)/shard_map/ppermute | solution.py:50
  211.3 38.7 %collective-permute-start.39 = (bf16[256,1024]{1,0:T(8,128)(2,1)}, bf16[256,1024]{1,0:T(8,128)(2,1)S(1)}, u32[]{:S(2)}, u32[]{:S(2)}) collective-permute-start(bf16[256,1024]{1,0:T(8,128)(2,1)} %collective-permute-done.31.refs_2_), channel_id=1, source_target_pairs={{0,8},{8,0},{16,24},{24,16},{1,9},{9,1},{17,25},{25,17},{2,10},{10... | collective-permute-start | bytes 1572872 | tf_op jit(solution)/shard_map/ppermute | solution.py:50
  218.8 32.3 %collective-permute-start.36 = (bf16[256,1024]{1,0:T(8,128)(2,1)}, bf16[256,1024]{1,0:T(8,128)(2,1)}, u32[]{:S(2)}, u32[]{:S(2)}) collective-permute-start(bf16[256,1024]{1,0:T(8,128)(2,1)} %collective-permute-done.34.refs_5_), channel_id=1, source_target_pairs={{0,2},{1,3},{2,0},{3,1},{4,6},{5,7},{6,4},{7,5},{8,10},{9,11},{10,... | collective-permute-start | bytes 1572872 | tf_op jit(solution)/shard_map/ppermute | solution.py:50
  279.0 32.0 %collective-permute-start.50 = (bf16[176,2176]{1,0:T(8,128)(2,1)S(1)}, bf16[176,2176]{1,0:T(8,128)(2,1)S(1)}, u32[]{:S(2)}, u32[]{:S(2)}) collective-permute-start(bf16[176,2176]{1,0:T(8,128)(2,1)S(1)} %copy-done.110), channel_id=1, source_target_pairs={{0,2},{1,3},{2,0},{3,1},{4,6},{5,7},{6,4},{7,5},{8,10},{9,11},{10,... | collective-permute-start | bytes 2297864 | tf_op jit(solution)/shard_map/ppermute | solution.py:50
  279.1 37.5 %collective-permute-start.51 = (bf16[176,2176]{1,0:T(8,128)(2,1)S(1)}, bf16[176,2176]{1,0:T(8,128)(2,1)}, u32[]{:S(2)}, u32[]{:S(2)}) collective-permute-start(bf16[176,2176]{1,0:T(8,128)(2,1)S(1)} %copy-done.110), channel_id=1, source_target_pairs={{0,4},{1,5},{2,6},{3,7},{4,0},{5,1},{6,2},{7,3},{8,12},{9,13},{10,... | collective-permute-start | bytes 2297864 | tf_op jit(solution)/shard_map/ppermute | solution.py:50
  291.9 35.8 %collective-permute-start.45 = (bf16[256,2048]{1,0:T(8,128)(2,1)}, bf16[256,2048]{1,0:T(8,128)(2,1)}, u32[]{:S(2)}, u32[]{:S(2)}) collective-permute-start(bf16[256,2048]{1,0:T(8,128)(2,1)} %multiply_convert_fusion), channel_id=1, source_target_pairs={{0,16},{8,24},{16,0},{24,8},{1,17},{9,25},{17,1},{25,9},{2,18},{10... | collective-permute-start | bytes 3145736 | tf_op jit(solution)/shard_map/ppermute | solution.py:50
  316.5 39.2 %collective-permute-start.56 = (bf16[256,1536]{1,0:T(8,128)(2,1)S(1)}, bf16[256,1536]{1,0:T(8,128)(2,1)S(1)}, u32[]{:S(2)}, u32[]{:S(2)}) collective-permute-start(bf16[256,1536]{1,0:T(8,128)(2,1)S(1)} %slice.369.refs_0_), channel_id=1, source_target_pairs={{0,1},{1,0},{2,3},{3,2},{4,5},{5,4},{6,7},{7,6},{8,9},{9,8},{10,11... | collective-permute-start | bytes 2359304 | tf_op jit(solution)/shard_map/ppermute | solution.py:50
  318.2 37.2 %collective-permute-start.54 = (bf16[176,2176]{1,0:T(8,128)(2,1)}, bf16[176,2176]{1,0:T(8,128)(2,1)}, u32[]{:S(2)}, u32[]{:S(2)}) collective-permute-start(bf16[176,2176]{1,0:T(8,128)(2,1)} %collective-permute-done.51), channel_id=1, source_target_pairs={{0,2},{1,3},{2,0},{3,1},{4,6},{5,7},{6,4},{7,5},{8,10},{9,11},{10,... | collective-permute-start | bytes 2297864 | tf_op jit(solution)/shard_map/ppermute | solution.py:50
  321.5 49.2 %collective-permute-start.57 = (bf16[256,1536]{1,0:T(8,128)(2,1)S(1)}, bf16[256,1536]{1,0:T(8,128)(2,1)}, u32[]{:S(2)}, u32[]{:S(2)}) collective-permute-start(bf16[256,1536]{1,0:T(8,128)(2,1)S(1)} %slice.369.refs_0_), channel_id=1, source_target_pairs={{0,2},{1,3},{2,0},{3,1},{4,6},{5,7},{6,4},{7,5},{8,10},{9,11},{10,... | collective-permute-start | bytes 2359304 | tf_op jit(solution)/shard_map/ppermute | solution.py:50
  323.5 50.2 %collective-permute-start.47 = (bf16[256,2048]{1,0:T(8,128)(2,1)}, bf16[256,2048]{1,0:T(8,128)(2,1)S(1)}, u32[]{:S(2)}, u32[]{:S(2)}) collective-permute-start(bf16[256,2048]{1,0:T(8,128)(2,1)} %get-tuple-element.183), channel_id=1, source_target_pairs={{0,16},{8,24},{16,0},{24,8},{1,17},{9,25},{17,1},{25,9},{2,18},{10... | collective-permute-start | bytes 3145736 | tf_op jit(solution)/shard_map/ppermute | solution.py:50
  327.7 44.6 %collective-permute-start.59 = (bf16[256,1536]{1,0:T(8,128)(2,1)S(1)}, bf16[256,1536]{1,0:T(8,128)(2,1)}, u32[]{:S(2)}, u32[]{:S(2)}) collective-permute-start(bf16[256,1536]{1,0:T(8,128)(2,1)S(1)} %slice.369.refs_0_), channel_id=1, source_target_pairs={{0,4},{1,5},{2,6},{3,7},{4,0},{5,1},{6,2},{7,3},{8,12},{9,13},{10,... | collective-permute-start | bytes 2359304 | tf_op jit(solution)/shard_map/ppermute | solution.py:50
  355.7 63.7 %collective-permute-start.46 = (bf16[512,2048]{1,0:T(8,128)(2,1)S(1)}, bf16[512,2048]{1,0:T(8,128)(2,1)S(1)}, u32[]{:S(2)}, u32[]{:S(2)}) collective-permute-start(bf16[512,2048]{1,0:T(8,128)(2,1)S(1)} %pad_maximum_fusion.2), channel_id=1, source_target_pairs={{0,8},{8,0},{16,24},{24,16},{1,9},{9,1},{17,25},{25,17},{2,10},{10... | collective-permute-start | bytes 6291464 | tf_op jit(solution)/shard_map/ppermute | solution.py:50
  372.3 45.0 %collective-permute-start.55 = (bf16[176,2176]{1,0:T(8,128)(2,1)}, bf16[176,2176]{1,0:T(8,128)(2,1)S(1)}, u32[]{:S(2)}, u32[]{:S(2)}) collective-permute-start(bf16[176,2176]{1,0:T(8,128)(2,1)} %collective-permute-done.54), channel_id=1, source_target_pairs={{0,1},{1,0},{2,3},{3,2},{4,5},{5,4},{6,7},{7,6},{8,9},{9,8},{10,11... | collective-permute-start | bytes 2297864 | tf_op jit(solution)/shard_map/ppermute | solution.py:50
  375.4 77.8 %collective-permute-start.48 = (bf16[512,2048]{1,0:T(8,128)(2,1)}, bf16[512,2048]{1,0:T(8,128)(2,1)}, u32[]{:S(2)}, u32[]{:S(2)}) collective-permute-start(bf16[512,2048]{1,0:T(8,128)(2,1)} %pad_maximum_fusion.3), channel_id=1, source_target_pairs={{0,8},{8,0},{16,24},{24,16},{1,9},{9,1},{17,25},{25,17},{2,10},{10... | collective-permute-start | bytes 6291464 | tf_op jit(solution)/shard_map/ppermute | solution.py:50
  419.4 32.7 %collective-permute-start.68 = (bf16[256,1280]{1,0:T(8,128)(2,1)}, bf16[256,1280]{1,0:T(8,128)(2,1)}, u32[]{:S(2)}, u32[]{:S(2)}) collective-permute-start(bf16[256,1280]{1,0:T(8,128)(2,1)} %collective-permute-done.66.refs_4_.refs_12_), channel_id=1, source_target_pairs={{0,2},{1,3},{2,0},{3,1},{4,6},{5,7},{6,4},{7,5},{8,10},{9,11},{10,... | collective-permute-start | bytes 1966088 | tf_op jit(solution)/shard_map/ppermute | solution.py:50
  424.9 42.8 %collective-permute-start.62 = (bf16[256,1536]{1,0:T(8,128)(2,1)}, bf16[256,1536]{1,0:T(8,128)(2,1)}, u32[]{:S(2)}, u32[]{:S(2)}) collective-permute-start(bf16[256,1536]{1,0:T(8,128)(2,1)} %collective-permute-done.60.refs_5_), channel_id=1, source_target_pairs={{0,2},{1,3},{2,0},{3,1},{4,6},{5,7},{6,4},{7,5},{8,10},{9,11},{10,... | collective-permute-start | bytes 2359304 | tf_op jit(solution)/shard_map/ppermute | solution.py:50
  439.0 57.4 %collective-permute-start.63 = (bf16[256,1280]{1,0:T(8,128)(2,1)S(1)}, bf16[256,1280]{1,0:T(8,128)(2,1)}, u32[]{:S(2)}, u32[]{:S(2)}) collective-permute-start(bf16[256,1280]{1,0:T(8,128)(2,1)S(1)} %slice.370.refs_0_.refs_8_), channel_id=1, source_target_pairs={{0,1},{1,0},{2,3},{3,2},{4,5},{5,4},{6,7},{7,6},{8,9},{9,8},{10,11... | collective-permute-start | bytes 1966088 | tf_op jit(solution)/shard_map/ppermute | solution.py:50
  439.9 56.5 %collective-permute-start.67 = (bf16[256,1280]{1,0:T(8,128)(2,1)}, bf16[256,1280]{1,0:T(8,128)(2,1)}, u32[]{:S(2)}, u32[]{:S(2)}) collective-permute-start(bf16[256,1280]{1,0:T(8,128)(2,1)} %collective-permute-done.66.refs_4_.refs_12_), channel_id=1, source_target_pairs={{0,1},{1,0},{2,3},{3,2},{4,5},{5,4},{6,7},{7,6},{8,9},{9,8},{10,11... | collective-permute-start | bytes 1966088 | tf_op jit(solution)/shard_map/ppermute | solution.py:50
  452.1 44.3 %collective-permute-start.65 = (bf16[256,1280]{1,0:T(8,128)(2,1)}, bf16[256,1280]{1,0:T(8,128)(2,1)}, u32[]{:S(2)}, u32[]{:S(2)}) collective-permute-start(bf16[256,1280]{1,0:T(8,128)(2,1)} %collective-permute-done.64.refs_2_.refs_10_), channel_id=1, source_target_pairs={{0,1},{1,0},{2,3},{3,2},{4,5},{5,4},{6,7},{7,6},{8,9},{9,8},{10,11... | collective-permute-start | bytes 1966088 | tf_op jit(solution)/shard_map/ppermute | solution.py:50
  453.2 43.8 %collective-permute-start.69 = (bf16[256,1280]{1,0:T(8,128)(2,1)}, bf16[256,1280]{1,0:T(8,128)(2,1)}, u32[]{:S(2)}, u32[]{:S(2)}) collective-permute-start(bf16[256,1280]{1,0:T(8,128)(2,1)} %collective-permute-done.68.refs_6_.refs_14_), channel_id=1, source_target_pairs={{0,1},{1,0},{2,3},{3,2},{4,5},{5,4},{6,7},{7,6},{8,9},{9,8},{10,11... | collective-permute-start | bytes 1966088 | tf_op jit(solution)/shard_map/ppermute | solution.py:50
  648.9 42.0 %collective-permute-start.83 = (f32[1,2048]{1,0:T(1,128)S(1)}, f32[1,2048]{1,0:T(1,128)S(1)}, u32[]{:S(2)}, u32[]{:S(2)}) collective-permute-start(f32[1,2048]{1,0:T(1,128)S(1)} %bitcast.215), channel_id=1, source_target_pairs={{0,16},{8,24},{16,0},{24,8},{1,17},{9,25},{17,1},{25,9},{2,18},{10... | collective-permute-start | bytes 24584 | tf_op jit(solution)/shard_map/ppermute | solution.py:50
  769.0 36.1 %collective-permute-start.88 = (bf16[256,512]{1,0:T(8,128)(2,1)S(1)}, bf16[256,512]{1,0:T(8,128)(2,1)S(1)}, u32[]{:S(2)}, u32[]{:S(2)}) collective-permute-start(bf16[256,512]{1,0:T(8,128)(2,1)S(1)} %get-tuple-element.197), channel_id=1, source_target_pairs={{0,6},{1,7},{2,4},{3,5},{4,2},{5,3},{6,0},{7,1},{8,14},{9,15},{10,... | collective-permute-start | bytes 786440 | tf_op jit(solution)/shard_map/ppermute | solution.py:50
  771.5 50.4 %collective-permute-start.85 = (bf16[8,4,32,256]{3,2,1,0:T(8,128)(2,1)}, bf16[8,4,32,256]{3,2,1,0:T(8,128)(2,1)}, u32[]{:S(2)}, u32[]{:S(2)}) collective-permute-start(bf16[8,4,32,256]{3,2,1,0:T(8,128)(2,1)} %constant_dynamic-slice_fusion.6), channel_id=1, source_target_pairs={{0,1},{1,0},{2,3},{3,2},{4,5},{5,4},{6,7},{7,6},{8,9},{9,8},{10,11... | collective-permute-start | bytes 1572872 | tf_op jit(solution)/shard_map/ppermute | solution.py:50
  (295 other events, 5148.9 us)

commit v5 on v4

--- a/solution.py
+++ b/solution.py
@@ -1600,11 +1600,6 @@
         pair = jnp.concatenate([rows, partner(rows)])
         return jnp.concatenate([pair, other_core(pair)])
 
-    def to_owner_of_four(keep, sent):
-        pair = keep + other_core(sent).astype(F32)
-        swapped = partner(pair[count:].astype(BF))
-        return pair[:count] + swapped.astype(F32), swapped
-
     normed_two = of_four(normed_own)
     down_low = (upstream * scales[DOWN]).astype(BF)
     down_low = of_four(down_low)
@@ -1628,9 +1623,6 @@
         )
         for i, span in enumerate(spans)
     ]
-    bounds = [(span.start // 2, span.stop // 2) for span in spans]
-    down_keep, down_sent, reduced_down = down_forward([b[0] for b in blocks], bounds, down_weights, outers[6])
-    reduced_down = reduced_down[:, :RANK]
 
     pairs = 2 * RANK
     keep, sent, first_pairs = mlp_back(
@@ -1643,7 +1635,12 @@
         [ordered(slots) for slots in mlp_slots],
         4 * RANK,
     )
-    grad_normed, swapped = to_owner_of_four(keep, sent)
+    pair = keep + other_core(sent).astype(F32)
+    swapped = partner(pair[count:].astype(BF))
+    grad_normed = pair[:count] + swapped.astype(F32)
+    bounds = [(span.start // 2, span.stop // 2) for span in spans]
+    down_keep, down_sent, reduced_down = down_forward([b[0] for b in blocks], bounds, down_weights, after(outers[6], pair))
+    reduced_down = reduced_down[:, :RANK]
     grad_mid = upstream + norm_rows_back(hidden_one, gains[1], inverse_two, grad_normed)
     down_pair = down_keep + other_core(after(down_sent, swapped)).astype(F32)
 

time: 848 us -> 848 us (level)
    unnamed x462 -> x456, local copies, waits for them, and re-layouts: 51.2 us -> 50.5 us
  transfers between devices with their start and end apart: 100 -> 100, of which waited for: 42 -> 43; matrix products, arithmetic and copies ran while one was open for 12% -> 12% of each run, Pallas kernels for 17% -> 17%
where the time goes in v5:
time: 848 us; the launch traced here: 838 us
  waiting for transfers between devices  332 us (39%)
  Pallas kernels  227 us (27%)
  local copies, waits for them, and re-layouts  103 us (12%)
  starting transfers between devices  91.9 us (11%)
  other arithmetic  61.2 us (7%)
  matrix products  13.8 us (2%)
  between operations  9.19 us (1%)
    ppermute x100, waiting for transfers between devices, swap(): return lax.ppermute(array, axis, [(i, i ^ distance) for i in range(count)])  332 us
    ppermute x100, starting transfers between devices, swap(): return lax.ppermute(array, axis, [(i, i ^ distance) for i in range(count)])  91.9 us
    unnamed x456, local copies, waits for them, and re-layouts  50.5 us
    pallas_call x2, Pallas kernels, mlp_block(): pl.pallas_call(functools.partial(mlp_kernel, offset=offset), grid_spec=pl...  48.5 us
    pallas_call x1, Pallas kernels, mlp_back(): pl.pallas_call(functools.partial(mlp_back_kernel, offset=offset, rank=ran...  40.8 us
    pallas_call x1, Pallas kernels, attend_back(): pl.pallas_call(functools.partial(backward_kernel, block=block, span=span,...  23.6 us
    pallas_call x3, Pallas kernels, slot_back(): pl.pallas_call(functools.partial(slot_back_kernel, skip=skip), grid_spec=...  22.4 us
    pallas_call x3, Pallas kernels, slot_mm(): pl.pallas_call(functools.partial(slot_kernel, offset=offset), grid_spec=p...  22 us
  transfers between devices with their start and end apart: 100, of which 43 were waited for; matrix products, arithmetic and copies ran while one was open for 12% of the time, Pallas kernels for 17%

profile of v5, /device:TPU:0, one launch (start us, length us, event | category | flops | bytes accessed | tf_op | source)
XLA Modules:
  0.0 838.0 jit_solution(65405269109062723)
XLA Ops:
  30.4 14.4 %collective-permute-done.6.refs_4_ = bf16[256,1408]{1,0:T(8,128)(2,1)S(1)} collective-permute-done((bf16[256,1408]{1,0:T(8,128)(2,1)S(1)}, bf16[256,1408]{1,0:T(8,128)(2,1)S(1)}, u32[]{:S(2)}, u32[]{:S(2)}) %collective-permute-start.6) | collective-permute-done | bytes 720928 | tf_op jit(solution)/shard_map/ppermute | solution.py:50
  45.0 13.6 %shard_map.345 = (bf16[256,1024]{1,0:T(8,128)(2,1)S(1)}, bf16[256,2816]{1,0:T(8,128)(2,1)}, bf16[176,2176]{1,0:T(8,128)(2,1)S(1)}, f32[1,4864]{1,0:T(1,128)S(1)}...) custom-call(s32[3]{0:T(128)S(1)} %pad_add_fusion.place_ref, bf16[256,2048]{1,0:T(8,128)(2,1)S(1)} %copy-done.104, ...), custom_call_target="tpu_custom_call" | custom-call | flops 1024 | bytes 1024 | tf_op jit(solution)/shard_map/pallas_call | solution.py:1326
  72.7 9.7 %collective-permute-done.20 = bf16[18,6144]{1,0:T(8,128)(2,1)S(1)} collective-permute-done((bf16[18,6144]{1,0:T(8,128)(2,1)S(1)}, bf16[18,6144]{1,0:T(8,128)(2,1)S(1)}, u32[]{:S(2)}, u32[]{:S(2)}) %collective-permute-start.20) | collective-permute-done | bytes 221216 | tf_op jit(solution)/shard_map/ppermute | solution.py:50
  84.5 10.9 %collective-permute-done.21 = bf16[18,6144]{1,0:T(8,128)(2,1)S(1)} collective-permute-done((bf16[18,6144]{1,0:T(8,128)(2,1)S(1)}, bf16[18,6144]{1,0:T(8,128)(2,1)S(1)}, u32[]{:S(2)}, u32[]{:S(2)}) %collective-permute-start.21) | collective-permute-done | bytes 221216 | tf_op jit(solution)/shard_map/ppermute | solution.py:50
  105.8 12.0 %collective-permute-done.1 = bf16[2,256,512]{2,1,0:T(8,128)(2,1)S(1)} collective-permute-done((bf16[2,256,512]{2,1,0:T(8,128)(2,1)S(1)}, bf16[2,256,512]{2,1,0:T(8,128)(2,1)S(1)}, u32[]{:S(2)}, u32[]{:S(2)}) %collective-permute-start.1) | collective-permute-done | bytes 524320 | tf_op jit(solution)/shard_map/ppermute | solution.py:50
  117.8 23.6 %collective-permute-done.2 = bf16[2,256,512]{2,1,0:T(8,128)(2,1)S(1)} collective-permute-done((bf16[2,256,512]{2,1,0:T(8,128)(2,1)S(1)}, bf16[2,256,512]{2,1,0:T(8,128)(2,1)S(1)}, u32[]{:S(2)}, u32[]{:S(2)}) %collective-permute-start.2) | collective-permute-done | bytes 524320 | tf_op jit(solution)/shard_map/ppermute | solution.py:50
  147.2 15.4 %collective-permute-done.10.refs_7_ = bf16[256,1408]{1,0:T(8,128)(2,1)S(1)} collective-permute-done((bf16[256,1408]{1,0:T(8,128)(2,1)S(1)}, bf16[256,1408]{1,0:T(8,128)(2,1)S(1)}, u32[]{:S(2)}, u32[]{:S(2)}) %collective-permute-start.10) | collective-permute-done | bytes 720928 | tf_op jit(solution)/shard_map/ppermute | solution.py:50
  180.5 12.5 %collective-permute-done.33.refs_4_ = bf16[256,1024]{1,0:T(8,128)(2,1)} collective-permute-done((bf16[256,1024]{1,0:T(8,128)(2,1)S(1)}, bf16[256,1024]{1,0:T(8,128)(2,1)}, u32[]{:S(2)}, u32[]{:S(2)}) %collective-permute-start.33) | collective-permute-done | bytes 524320 | tf_op jit(solution)/shard_map/ppermute | solution.py:50
  211.4 7.4 collective-permute-done.32.refs_3_
  239.9 9.1 %shard_map.344 = (f32[256,2048]{1,0:T(8,128)}, f32[256,128]{1,0:T(8,128)}) custom-call(s32[3]{0:T(128)S(1)} %pad_add_fusion.place_ref, bf16[256,2048]{1,0:T(8,128)(2,1)S(1)} %copy-done.5, bf16[2048,128]{1,0:T(8,128)(2,1)S(1)} %slice_dynamic-update-slice_fusion.first_ref.refs_3_.refs_4_, f32[16,2048]{1,0:T(8,128)S(1)} %get-tuple-element.196.outer_ref, ...), custom_call_target="tpu_custom_call" | custom-call | flops 1024 | bytes 1024 | tf_op jit(solution)/shard_map/pallas_call | solution.py:527
  258.3 19.1 %shard_map.348 = (bf16[256,2048]{1,0:T(8,128)(2,1)S(1)}, bf16[256,2048]{1,0:T(8,128)(2,1)S(1)}, f32[4,8,1,256]{3,2,1,0:T(1,128)S(1)}) custom-call(s32[8]{0:T(128)S(1)} %and_select_fusion.1.first_ref, f32[256,2048]{1,0:T(8,128)S(1)} %copy-done.66, f32[1,2048]{1,0:T(1,128)S(1)} %broadcast_select_fusion.7.scale_ref, f32[256,128]{1,0:T(8,128)S(1)} %copy-done.91, ...), custom_call_target="tpu_custom_call" | custom-call | flops 1024 | bytes 1024 | tf_op jit(solution)/shard_map/pallas_call | solution.py:404
  281.9 9.6 %shard_map.349 = (f32[256,2048]{1,0:T(8,128)S(1)}, f32[256,128]{1,0:T(8,128)S(1)}) custom-call(s32[3]{0:T(128)S(1)} %pad_add_fusion.place_ref, bf16[256,2048]{1,0:T(8,128)(2,1)S(1)} %get-tuple-element.97.inputs_ref.refs_4_.out_ref, bf16[2048,128]{1,0:T(8,128)(2,1)S(1)} %slice_dynamic-update-slice_fusion.first_ref.refs_3_.refs_4_, f32[16,2048]{1,0:T(8,128)S(1)} %copy-done.99, ...), custom_call_target="tpu_custom_call" | custom-call | flops 1024 | bytes 1024 | tf_op jit(solution)/shard_map/pallas_call | solution.py:527
  298.5 16.3 %collective-permute-done.50 = bf16[176,2176]{1,0:T(8,128)(2,1)S(1)} collective-permute-done((bf16[176,2176]{1,0:T(8,128)(2,1)S(1)}, bf16[176,2176]{1,0:T(8,128)(2,1)S(1)}, u32[]{:S(2)}, u32[]{:S(2)}) %collective-permute-start.50) | collective-permute-done | bytes 765984 | tf_op jit(solution)/shard_map/ppermute | solution.py:50
  330.1 24.9 %collective-permute-done.54 = bf16[176,2176]{1,0:T(8,128)(2,1)} collective-permute-done((bf16[176,2176]{1,0:T(8,128)(2,1)}, bf16[176,2176]{1,0:T(8,128)(2,1)}, u32[]{:S(2)}, u32[]{:S(2)}) %collective-permute-start.54) | collective-permute-done | bytes 765984 | tf_op jit(solution)/shard_map/ppermute | solution.py:50
  356.5 13.1 %collective-permute-done.57.refs_2_ = bf16[256,1536]{1,0:T(8,128)(2,1)} collective-permute-done((bf16[256,1536]{1,0:T(8,128)(2,1)S(1)}, bf16[256,1536]{1,0:T(8,128)(2,1)}, u32[]{:S(2)}, u32[]{:S(2)}) %collective-permute-start.57) | collective-permute-done | bytes 786464 | tf_op jit(solution)/shard_map/ppermute | solution.py:50
  376.4 13.5 %collective-permute-done.53 = bf16[176,2176]{1,0:T(8,128)(2,1)S(1)} collective-permute-done((bf16[176,2176]{1,0:T(8,128)(2,1)}, bf16[176,2176]{1,0:T(8,128)(2,1)S(1)}, u32[]{:S(2)}, u32[]{:S(2)}) %collective-permute-start.53) | collective-permute-done | bytes 765984 | tf_op jit(solution)/shard_map/ppermute | solution.py:50
  390.9 9.7 %collective-permute-done.66.refs_4_.refs_12_ = bf16[256,1280]{1,0:T(8,128)(2,1)} collective-permute-done((bf16[256,1280]{1,0:T(8,128)(2,1)S(1)}, bf16[256,1280]{1,0:T(8,128)(2,1)}, u32[]{:S(2)}, u32[]{:S(2)}) %collective-permute-start.66) | collective-permute-done | bytes 655392 | tf_op jit(solution)/shard_map/ppermute | solution.py:50
  401.9 11.0 %collective-permute-done.64.refs_2_.refs_10_ = bf16[256,1280]{1,0:T(8,128)(2,1)} collective-permute-done((bf16[256,1280]{1,0:T(8,128)(2,1)S(1)}, bf16[256,1280]{1,0:T(8,128)(2,1)}, u32[]{:S(2)}, u32[]{:S(2)}) %collective-permute-start.64) | collective-permute-done | bytes 655392 | tf_op jit(solution)/shard_map/ppermute | solution.py:50
  428.1 9.1 %collective-permute-done.58.refs_3_ = bf16[256,1536]{1,0:T(8,128)(2,1)} collective-permute-done((bf16[256,1536]{1,0:T(8,128)(2,1)}, bf16[256,1536]{1,0:T(8,128)(2,1)}, u32[]{:S(2)}, u32[]{:S(2)}) %collective-permute-start.58) | collective-permute-done | bytes 786464 | tf_op jit(solution)/shard_map/ppermute | solution.py:50
  439.2 8.7 %collective-permute-done.68.refs_6_.refs_14_ = bf16[256,1280]{1,0:T(8,128)(2,1)} collective-permute-done((bf16[256,1280]{1,0:T(8,128)(2,1)}, bf16[256,1280]{1,0:T(8,128)(2,1)}, u32[]{:S(2)}, u32[]{:S(2)}) %collective-permute-start.68) | collective-permute-done | bytes 655392 | tf_op jit(solution)/shard_map/ppermute | solution.py:50
  464.8 25.9 %shard_map.351 = (bf16[1024,768]{1,0:T(8,128)(2,1)}, bf16[1088,1536]{1,0:T(8,128)(2,1)}, f32[1,1536]{1,0:T(1,128)S(1)}, f32[16,1536]{1,0:T(8,128)S(1)}, f32[1024,128]{1,0:T(8,128)S(1)}, /*index=5*/f32[32,128]{1,0:T(8,128)S(1)}) custom-call(s32[3]{0:T(128)S(1)} %pad_add_fusion.place_ref, bf16[1024,2048]{1,0:T(8,128)(2,1)} %pad_maximum_fusion.inputs_ref, ...), custom_call_target="tpu_custom_call" | custom-call | flops 1024 | bytes 1024 | tf_op jit(solution)/shard_map/pallas_call | solution.py:862
  495.1 22.6 %shard_map.352 = (bf16[1024,640]{1,0:T(8,128)(2,1)}, bf16[1088,1280]{1,0:T(8,128)(2,1)}, f32[1,1280]{1,0:T(1,128)S(1)}, f32[16,1280]{1,0:T(8,128)S(1)}, f32[1024,128]{1,0:T(8,128)S(1)}, /*index=5*/f32[32,128]{1,0:T(8,128)S(1)}) custom-call(s32[3]{0:T(128)S(1)} %pad_add_fusion.place_ref, bf16[1024,2048]{1,0:T(8,128)(2,1)} %pad_maximum_fusion.inputs_ref, ...), custom_call_target="tpu_custom_call" | custom-call | flops 1024 | bytes 1024 | tf_op jit(solution)/shard_map/pallas_call | solution.py:862
  519.3 40.8 %shard_map.353 = (f32[512,2048]{1,0:T(8,128)}, bf16[512,2048]{1,0:T(8,128)(2,1)}, f32[32,2048]{1,0:T(8,128)}) custom-call(s32[3]{0:T(128)} %copy-done.129, bf16[1088,1536]{1,0:T(8,128)(2,1)} %get-tuple-element.110.one_ref, bf16[1088,1280]{1,0:T(8,128)(2,1)} %get-tuple-element.111.two_ref, f32[1024,128]{1,0:T(8,128)} %add.601.narrow_ref, ...), custom_call_target="tpu_custom_call" | custom-call | flops 1024 | bytes 1024 | tf_op jit(solution)/shard_map/pallas_call | solution.py:1136
  573.5 13.2 %shard_map.354 = (f32[512,2048]{1,0:T(8,128)S(1)}, bf16[512,2048]{1,0:T(8,128)(2,1)}, f32[1024,128]{1,0:T(8,128)S(1)}) custom-call(bf16[1024,768]{1,0:T(8,128)(2,1)S(1)} %copy-done.94, bf16[1024,640]{1,0:T(8,128)(2,1)S(1)} %copy-done.96, bf16[1408,2176]{1,0:T(8,128)(2,1)} %constant_dynamic-update-slice_fusion.19.first_ref.down_ref.refs_2_.refs_3_, ...), custom_call_target="tpu_custom_call" | custom-call | flops 1024 | bytes 1024 | tf_op jit(solution)/shard_map/pallas_call | solution.py:926
  586.7 7.6 collective-permute-done.71
  611.8 19.9 %collective-permute-done.73 = bf16[256,2048]{1,0:T(8,128)(2,1)} collective-permute-done((bf16[256,2048]{1,0:T(8,128)(2,1)}, bf16[256,2048]{1,0:T(8,128)(2,1)}, u32[]{:S(2)}, u32[]{:S(2)}) %collective-permute-start.73) | collective-permute-done | bytes 1048608 | tf_op jit(solution)/shard_map/ppermute | solution.py:50
  638.5 8.1 shard_map.356.refs_0_
  650.5 23.6 %shard_map.358 = (f32[256,2048]{1,0:T(8,128)S(1)}, bf16[2048,512]{1,0:T(8,128)(2,1)S(1)}) custom-call(s32[8]{0:T(128)S(1)} %and_select_fusion.1.first_ref, bf16[256,2048]{1,0:T(8,128)(2,1)S(1)} %copy-done.135, f32[256,128]{1,0:T(8,128)S(1)} %copy-done.92, f32[256,128]{1,0:T(8,128)S(1)} %copy-done.90, s32[8,1,256]{2,1,0:T(1,128)S(1)} %tile.39.place_ref, ...), custom_call_target="tpu_custom_call" | custom-call | flops 42949672960 | bytes 67108864 | tf_op jit(solution)/shard_map/pallas_call | solution.py:447
  681.4 9.6 %shard_map.361.refs_0_ = f32[288,2048]{1,0:T(8,128)} custom-call(s32[3]{0:T(128)S(1)} %copy-done.130, bf16[288,2048]{1,0:T(8,128)(2,1)S(1)} %get-tuple-element.137.grad_ref, bf16[256,1408]{1,0:T(8,128)(2,1)S(1)} %get-tuple-element.88.refs_0_, bf16[256,1408]{1,0:T(8,128)(2,1)} %collective-permute-done.4.refs_1_, bf16[256,1408]{1,0:T(8,128)(2,1)S(1)} %copy-done.13, ...), custom_call_target="tpu_custom_call" | custom-call | flops 1024 | bytes 1024 | tf_op jit(solution)/shard_map/pallas_call | solution.py:634
  714.2 9.0 %collective-permute-done.76 = bf16[8,32,256]{2,1,0:T(8,128)(2,1)S(1)} collective-permute-done((bf16[8,32,256]{2,1,0:T(8,128)(2,1)S(1)}, bf16[8,32,256]{2,1,0:T(8,128)(2,1)S(1)}, u32[]{:S(2)}, u32[]{:S(2)}) %collective-permute-start.76) | collective-permute-done | bytes 131104 | tf_op jit(solution)/shard_map/ppermute | solution.py:50
  777.2 12.4 %collective-permute-done.92 = bf16[2,2,32,768]{3,2,1,0:T(8,128)(2,1)S(1)} collective-permute-done((bf16[2,2,32,768]{3,2,1,0:T(8,128)(2,1)S(1)}, bf16[2,2,32,768]{3,2,1,0:T(8,128)(2,1)S(1)}, u32[]{:S(2)}, u32[]{:S(2)}) %collective-permute-start.92) | collective-permute-done | bytes 196640 | tf_op jit(solution)/shard_map/ppermute | solution.py:50
  811.4 10.2 %collective-permute-done.97 = f32[8,128]{1,0:T(8,128)S(1)} collective-permute-done((f32[8,128]{1,0:T(8,128)S(1)}, f32[8,128]{1,0:T(8,128)S(1)}, u32[]{:S(2)}, u32[]{:S(2)}) %collective-permute-start.97) | collective-permute-done | bytes 4128 | tf_op jit(solution)/shard_map/ppermute | solution.py:50
  (898 shorter events, 362.3 us)
Async XLA Ops:
  8.9 35.8 %collective-permute-start.6 = (bf16[256,1408]{1,0:T(8,128)(2,1)S(1)}, bf16[256,1408]{1,0:T(8,128)(2,1)S(1)}, u32[]{:S(2)}, u32[]{:S(2)}) collective-permute-start(bf16[256,1408]{1,0:T(8,128)(2,1)S(1)} %get-tuple-element.88.refs_0_), channel_id=1, source_target_pairs={{0,4},{1,5},{2,6},{3,7},{4,0},{5,1},{6,2},{7,3},{8,12},{9,13},{10,... | collective-permute-start | bytes 2162696 | tf_op jit(solution)/shard_map/ppermute | solution.py:50
  16.1 146.6 %collective-permute-start.11 = (bf16[256,1408]{1,0:T(8,128)(2,1)S(1)}, bf16[256,1408]{1,0:T(8,128)(2,1)}, u32[]{:S(2)}, u32[]{:S(2)}) collective-permute-start(bf16[256,1408]{1,0:T(8,128)(2,1)S(1)} %get-tuple-element.88.refs_0_), channel_id=1, source_target_pairs={{0,8},{8,0},{16,24},{24,16},{1,9},{9,1},{17,25},{25,17},{2,10},{10... | collective-permute-start | bytes 2162696 | tf_op jit(solution)/shard_map/ppermute | solution.py:50
  19.9 50.9 %collective-permute-start = (bf16[4,2,8,32,256]{4,3,2,1,0:T(8,128)(2,1)}, bf16[4,2,8,32,256]{4,3,2,1,0:T(8,128)(2,1)}, u32[]{:S(2)}, u32[]{:S(2)}) collective-permute-start(bf16[4,2,8,32,256]{4,3,2,1,0:T(8,128)(2,1)} %bitcast.176), channel_id=1, source_target_pairs={{0,1},{1,0},{2,3},{3,2},{4,5},{5,4},{6,7},{7,6},{8,9},{9,8},{10,11... | collective-permute-start | bytes 3145736 | tf_op jit(solution)/shard_map/ppermute | solution.py:50
  60.5 42.6 %collective-permute-start.7 = (bf16[256,1408]{1,0:T(8,128)(2,1)S(1)}, bf16[256,1408]{1,0:T(8,128)(2,1)S(1)}, u32[]{:S(2)}, u32[]{:S(2)}) collective-permute-start(bf16[256,1408]{1,0:T(8,128)(2,1)S(1)} %collective-permute-done.5.refs_2_), channel_id=1, source_target_pairs={{0,1},{1,0},{2,3},{3,2},{4,5},{5,4},{6,7},{7,6},{8,9},{9,8},{10,11... | collective-permute-start | bytes 2162696 | tf_op jit(solution)/shard_map/ppermute | solution.py:50
  61.1 42.2 %collective-permute-start.8 = (bf16[256,1408]{1,0:T(8,128)(2,1)S(1)}, bf16[256,1408]{1,0:T(8,128)(2,1)S(1)}, u32[]{:S(2)}, u32[]{:S(2)}) collective-permute-start(bf16[256,1408]{1,0:T(8,128)(2,1)S(1)} %collective-permute-done.6.refs_4_), channel_id=1, source_target_pairs={{0,1},{1,0},{2,3},{3,2},{4,5},{5,4},{6,7},{7,6},{8,9},{9,8},{10,11... | collective-permute-start | bytes 2162696 | tf_op jit(solution)/shard_map/ppermute | solution.py:50
  70.7 34.9 %collective-permute-start.9 = (bf16[256,1408]{1,0:T(8,128)(2,1)S(1)}, bf16[256,1408]{1,0:T(8,128)(2,1)S(1)}, u32[]{:S(2)}, u32[]{:S(2)}) collective-permute-start(bf16[256,1408]{1,0:T(8,128)(2,1)S(1)} %collective-permute-done.6.refs_4_), channel_id=1, source_target_pairs={{0,2},{1,3},{2,0},{3,1},{4,6},{5,7},{6,4},{7,5},{8,10},{9,11},{10,... | collective-permute-start | bytes 2162696 | tf_op jit(solution)/shard_map/ppermute | solution.py:50
  103.1 38.3 %collective-permute-start.2 = (bf16[2,256,512]{2,1,0:T(8,128)(2,1)S(1)}, bf16[2,256,512]{2,1,0:T(8,128)(2,1)S(1)}, u32[]{:S(2)}, u32[]{:S(2)}) collective-permute-start(bf16[2,256,512]{2,1,0:T(8,128)(2,1)S(1)} %bitcast.206), channel_id=1, source_target_pairs={{0,4},{1,5},{2,6},{3,7},{4,0},{5,1},{6,2},{7,3},{8,12},{9,13},{10,... | collective-permute-start | bytes 1572872 | tf_op jit(solution)/shard_map/ppermute | solution.py:50
  103.3 38.2 %collective-permute-start.3 = (bf16[2,256,512]{2,1,0:T(8,128)(2,1)S(1)}, bf16[2,256,512]{2,1,0:T(8,128)(2,1)S(1)}, u32[]{:S(2)}, u32[]{:S(2)}) collective-permute-start(bf16[2,256,512]{2,1,0:T(8,128)(2,1)S(1)} %bitcast.205), channel_id=1, source_target_pairs={{0,6},{1,7},{2,4},{3,5},{4,2},{5,3},{6,0},{7,1},{8,14},{9,15},{10,... | collective-permute-start | bytes 1572872 | tf_op jit(solution)/shard_map/ppermute | solution.py:50
  105.7 57.6 %collective-permute-start.15 = (bf16[256,1408]{1,0:T(8,128)(2,1)S(1)}, bf16[256,1408]{1,0:T(8,128)(2,1)S(1)}, u32[]{:S(2)}, u32[]{:S(2)}) collective-permute-start(bf16[256,1408]{1,0:T(8,128)(2,1)S(1)} %collective-permute-done.6.refs_4_), channel_id=1, source_target_pairs={{0,8},{8,0},{16,24},{24,16},{1,9},{9,1},{17,25},{25,17},{2,10},{10... | collective-permute-start | bytes 2162696 | tf_op jit(solution)/shard_map/ppermute | solution.py:50
  117.8 45.8 %collective-permute-start.13 = (bf16[256,1408]{1,0:T(8,128)(2,1)S(1)}, bf16[256,1408]{1,0:T(8,128)(2,1)S(1)}, u32[]{:S(2)}, u32[]{:S(2)}) collective-permute-start(bf16[256,1408]{1,0:T(8,128)(2,1)S(1)} %collective-permute-done.5.refs_2_), channel_id=1, source_target_pairs={{0,8},{8,0},{16,24},{24,16},{1,9},{9,1},{17,25},{25,17},{2,10},{10... | collective-permute-start | bytes 2162696 | tf_op jit(solution)/shard_map/ppermute | solution.py:50
  211.3 38.7 %collective-permute-start.39 = (bf16[256,1024]{1,0:T(8,128)(2,1)}, bf16[256,1024]{1,0:T(8,128)(2,1)S(1)}, u32[]{:S(2)}, u32[]{:S(2)}) collective-permute-start(bf16[256,1024]{1,0:T(8,128)(2,1)} %collective-permute-done.31.refs_2_), channel_id=1, source_target_pairs={{0,8},{8,0},{16,24},{24,16},{1,9},{9,1},{17,25},{25,17},{2,10},{10... | collective-permute-start | bytes 1572872 | tf_op jit(solution)/shard_map/ppermute | solution.py:50
  218.8 32.3 %collective-permute-start.36 = (bf16[256,1024]{1,0:T(8,128)(2,1)}, bf16[256,1024]{1,0:T(8,128)(2,1)}, u32[]{:S(2)}, u32[]{:S(2)}) collective-permute-start(bf16[256,1024]{1,0:T(8,128)(2,1)} %collective-permute-done.34.refs_5_), channel_id=1, source_target_pairs={{0,2},{1,3},{2,0},{3,1},{4,6},{5,7},{6,4},{7,5},{8,10},{9,11},{10,... | collective-permute-start | bytes 1572872 | tf_op jit(solution)/shard_map/ppermute | solution.py:50
  279.5 35.3 %collective-permute-start.50 = (bf16[176,2176]{1,0:T(8,128)(2,1)S(1)}, bf16[176,2176]{1,0:T(8,128)(2,1)S(1)}, u32[]{:S(2)}, u32[]{:S(2)}) collective-permute-start(bf16[176,2176]{1,0:T(8,128)(2,1)S(1)} %copy-done.109), channel_id=1, source_target_pairs={{0,2},{1,3},{2,0},{3,1},{4,6},{5,7},{6,4},{7,5},{8,10},{9,11},{10,... | collective-permute-start | bytes 2297864 | tf_op jit(solution)/shard_map/ppermute | solution.py:50
  280.5 35.6 %collective-permute-start.51 = (bf16[176,2176]{1,0:T(8,128)(2,1)S(1)}, bf16[176,2176]{1,0:T(8,128)(2,1)}, u32[]{:S(2)}, u32[]{:S(2)}) collective-permute-start(bf16[176,2176]{1,0:T(8,128)(2,1)S(1)} %copy-done.109), channel_id=1, source_target_pairs={{0,4},{1,5},{2,6},{3,7},{4,0},{5,1},{6,2},{7,3},{8,12},{9,13},{10,... | collective-permute-start | bytes 2297864 | tf_op jit(solution)/shard_map/ppermute | solution.py:50
  294.5 32.7 %collective-permute-start.45 = (bf16[256,2048]{1,0:T(8,128)(2,1)}, bf16[256,2048]{1,0:T(8,128)(2,1)}, u32[]{:S(2)}, u32[]{:S(2)}) collective-permute-start(bf16[256,2048]{1,0:T(8,128)(2,1)} %multiply_convert_fusion), channel_id=1, source_target_pairs={{0,16},{8,24},{16,0},{24,8},{1,17},{9,25},{17,1},{25,9},{2,18},{10... | collective-permute-start | bytes 3145736 | tf_op jit(solution)/shard_map/ppermute | solution.py:50
  316.2 39.2 %collective-permute-start.56 = (bf16[256,1536]{1,0:T(8,128)(2,1)S(1)}, bf16[256,1536]{1,0:T(8,128)(2,1)S(1)}, u32[]{:S(2)}, u32[]{:S(2)}) collective-permute-start(bf16[256,1536]{1,0:T(8,128)(2,1)S(1)} %slice.369.refs_0_), channel_id=1, source_target_pairs={{0,1},{1,0},{2,3},{3,2},{4,5},{5,4},{6,7},{7,6},{8,9},{9,8},{10,11... | collective-permute-start | bytes 2359304 | tf_op jit(solution)/shard_map/ppermute | solution.py:50
  317.8 37.2 %collective-permute-start.54 = (bf16[176,2176]{1,0:T(8,128)(2,1)}, bf16[176,2176]{1,0:T(8,128)(2,1)}, u32[]{:S(2)}, u32[]{:S(2)}) collective-permute-start(bf16[176,2176]{1,0:T(8,128)(2,1)} %collective-permute-done.51), channel_id=1, source_target_pairs={{0,2},{1,3},{2,0},{3,1},{4,6},{5,7},{6,4},{7,5},{8,10},{9,11},{10,... | collective-permute-start | bytes 2297864 | tf_op jit(solution)/shard_map/ppermute | solution.py:50
  321.6 48.1 %collective-permute-start.57 = (bf16[256,1536]{1,0:T(8,128)(2,1)S(1)}, bf16[256,1536]{1,0:T(8,128)(2,1)}, u32[]{:S(2)}, u32[]{:S(2)}) collective-permute-start(bf16[256,1536]{1,0:T(8,128)(2,1)S(1)} %slice.369.refs_0_), channel_id=1, source_target_pairs={{0,2},{1,3},{2,0},{3,1},{4,6},{5,7},{6,4},{7,5},{8,10},{9,11},{10,... | collective-permute-start | bytes 2359304 | tf_op jit(solution)/shard_map/ppermute | solution.py:50
  323.1 49.5 %collective-permute-start.47 = (bf16[256,2048]{1,0:T(8,128)(2,1)}, bf16[256,2048]{1,0:T(8,128)(2,1)S(1)}, u32[]{:S(2)}, u32[]{:S(2)}) collective-permute-start(bf16[256,2048]{1,0:T(8,128)(2,1)} %get-tuple-element.185), channel_id=1, source_target_pairs={{0,16},{8,24},{16,0},{24,8},{1,17},{9,25},{17,1},{25,9},{2,18},{10... | collective-permute-start | bytes 3145736 | tf_op jit(solution)/shard_map/ppermute | solution.py:50
  327.2 43.6 %collective-permute-start.59 = (bf16[256,1536]{1,0:T(8,128)(2,1)S(1)}, bf16[256,1536]{1,0:T(8,128)(2,1)}, u32[]{:S(2)}, u32[]{:S(2)}) collective-permute-start(bf16[256,1536]{1,0:T(8,128)(2,1)S(1)} %slice.369.refs_0_), channel_id=1, source_target_pairs={{0,4},{1,5},{2,6},{3,7},{4,0},{5,1},{6,2},{7,3},{8,12},{9,13},{10,... | collective-permute-start | bytes 2359304 | tf_op jit(solution)/shard_map/ppermute | solution.py:50
  355.4 59.7 %collective-permute-start.46 = (bf16[512,2048]{1,0:T(8,128)(2,1)S(1)}, bf16[512,2048]{1,0:T(8,128)(2,1)S(1)}, u32[]{:S(2)}, u32[]{:S(2)}) collective-permute-start(bf16[512,2048]{1,0:T(8,128)(2,1)S(1)} %pad_maximum_fusion.2), channel_id=1, source_target_pairs={{0,8},{8,0},{16,24},{24,16},{1,9},{9,1},{17,25},{25,17},{2,10},{10... | collective-permute-start | bytes 6291464 | tf_op jit(solution)/shard_map/ppermute | solution.py:50
  370.8 42.2 %collective-permute-start.55 = (bf16[176,2176]{1,0:T(8,128)(2,1)}, bf16[176,2176]{1,0:T(8,128)(2,1)S(1)}, u32[]{:S(2)}, u32[]{:S(2)}) collective-permute-start(bf16[176,2176]{1,0:T(8,128)(2,1)} %collective-permute-done.54), channel_id=1, source_target_pairs={{0,1},{1,0},{2,3},{3,2},{4,5},{5,4},{6,7},{7,6},{8,9},{9,8},{10,11... | collective-permute-start | bytes 2297864 | tf_op jit(solution)/shard_map/ppermute | solution.py:50
  374.3 75.5 %collective-permute-start.48 = (bf16[512,2048]{1,0:T(8,128)(2,1)}, bf16[512,2048]{1,0:T(8,128)(2,1)}, u32[]{:S(2)}, u32[]{:S(2)}) collective-permute-start(bf16[512,2048]{1,0:T(8,128)(2,1)} %pad_maximum_fusion.3), channel_id=1, source_target_pairs={{0,8},{8,0},{16,24},{24,16},{1,9},{9,1},{17,25},{25,17},{2,10},{10... | collective-permute-start | bytes 6291464 | tf_op jit(solution)/shard_map/ppermute | solution.py:50
  415.1 32.8 %collective-permute-start.68 = (bf16[256,1280]{1,0:T(8,128)(2,1)}, bf16[256,1280]{1,0:T(8,128)(2,1)}, u32[]{:S(2)}, u32[]{:S(2)}) collective-permute-start(bf16[256,1280]{1,0:T(8,128)(2,1)} %collective-permute-done.66.refs_4_.refs_12_), channel_id=1, source_target_pairs={{0,2},{1,3},{2,0},{3,1},{4,6},{5,7},{6,4},{7,5},{8,10},{9,11},{10,... | collective-permute-start | bytes 1966088 | tf_op jit(solution)/shard_map/ppermute | solution.py:50
  421.3 40.6 %collective-permute-start.62 = (bf16[256,1536]{1,0:T(8,128)(2,1)}, bf16[256,1536]{1,0:T(8,128)(2,1)}, u32[]{:S(2)}, u32[]{:S(2)}) collective-permute-start(bf16[256,1536]{1,0:T(8,128)(2,1)} %collective-permute-done.60.refs_5_), channel_id=1, source_target_pairs={{0,2},{1,3},{2,0},{3,1},{4,6},{5,7},{6,4},{7,5},{8,10},{9,11},{10,... | collective-permute-start | bytes 2359304 | tf_op jit(solution)/shard_map/ppermute | solution.py:50
  437.2 53.5 %collective-permute-start.63 = (bf16[256,1280]{1,0:T(8,128)(2,1)S(1)}, bf16[256,1280]{1,0:T(8,128)(2,1)}, u32[]{:S(2)}, u32[]{:S(2)}) collective-permute-start(bf16[256,1280]{1,0:T(8,128)(2,1)S(1)} %slice.370.refs_0_.refs_8_), channel_id=1, source_target_pairs={{0,1},{1,0},{2,3},{3,2},{4,5},{5,4},{6,7},{7,6},{8,9},{9,8},{10,11... | collective-permute-start | bytes 1966088 | tf_op jit(solution)/shard_map/ppermute | solution.py:50
  437.5 53.2 %collective-permute-start.67 = (bf16[256,1280]{1,0:T(8,128)(2,1)}, bf16[256,1280]{1,0:T(8,128)(2,1)}, u32[]{:S(2)}, u32[]{:S(2)}) collective-permute-start(bf16[256,1280]{1,0:T(8,128)(2,1)} %collective-permute-done.66.refs_4_.refs_12_), channel_id=1, source_target_pairs={{0,1},{1,0},{2,3},{3,2},{4,5},{5,4},{6,7},{7,6},{8,9},{9,8},{10,11... | collective-permute-start | bytes 1966088 | tf_op jit(solution)/shard_map/ppermute | solution.py:50
  447.9 42.8 %collective-permute-start.65 = (bf16[256,1280]{1,0:T(8,128)(2,1)}, bf16[256,1280]{1,0:T(8,128)(2,1)}, u32[]{:S(2)}, u32[]{:S(2)}) collective-permute-start(bf16[256,1280]{1,0:T(8,128)(2,1)} %collective-permute-done.64.refs_2_.refs_10_), channel_id=1, source_target_pairs={{0,1},{1,0},{2,3},{3,2},{4,5},{5,4},{6,7},{7,6},{8,9},{9,8},{10,11... | collective-permute-start | bytes 1966088 | tf_op jit(solution)/shard_map/ppermute | solution.py:50
  449.8 45.3 %collective-permute-start.69 = (bf16[256,1280]{1,0:T(8,128)(2,1)}, bf16[256,1280]{1,0:T(8,128)(2,1)}, u32[]{:S(2)}, u32[]{:S(2)}) collective-permute-start(bf16[256,1280]{1,0:T(8,128)(2,1)} %collective-permute-done.68.refs_6_.refs_14_), channel_id=1, source_target_pairs={{0,1},{1,0},{2,3},{3,2},{4,5},{5,4},{6,7},{7,6},{8,9},{9,8},{10,11... | collective-permute-start | bytes 1966088 | tf_op jit(solution)/shard_map/ppermute | solution.py:50
  649.1 42.0 %collective-permute-start.83 = (f32[1,2048]{1,0:T(1,128)S(1)}, f32[1,2048]{1,0:T(1,128)S(1)}, u32[]{:S(2)}, u32[]{:S(2)}) collective-permute-start(f32[1,2048]{1,0:T(1,128)S(1)} %bitcast.215), channel_id=1, source_target_pairs={{0,16},{8,24},{16,0},{24,8},{1,17},{9,25},{17,1},{25,9},{2,18},{10... | collective-permute-start | bytes 24584 | tf_op jit(solution)/shard_map/ppermute | solution.py:50
  768.3 36.8 %collective-permute-start.88 = (bf16[256,512]{1,0:T(8,128)(2,1)S(1)}, bf16[256,512]{1,0:T(8,128)(2,1)S(1)}, u32[]{:S(2)}, u32[]{:S(2)}) collective-permute-start(bf16[256,512]{1,0:T(8,128)(2,1)S(1)} %get-tuple-element.199), channel_id=1, source_target_pairs={{0,6},{1,7},{2,4},{3,5},{4,2},{5,3},{6,0},{7,1},{8,14},{9,15},{10,... | collective-permute-start | bytes 786440 | tf_op jit(solution)/shard_map/ppermute | solution.py:50
  771.5 50.4 %collective-permute-start.85 = (bf16[8,4,32,256]{3,2,1,0:T(8,128)(2,1)}, bf16[8,4,32,256]{3,2,1,0:T(8,128)(2,1)}, u32[]{:S(2)}, u32[]{:S(2)}) collective-permute-start(bf16[8,4,32,256]{3,2,1,0:T(8,128)(2,1)} %constant_dynamic-slice_fusion.6), channel_id=1, source_target_pairs={{0,1},{1,0},{2,3},{3,2},{4,5},{5,4},{6,7},{7,6},{8,9},{9,8},{10,11... | collective-permute-start | bytes 1572872 | tf_op jit(solution)/shard_map/ppermute | solution.py:50
  (292 other events, 5304.2 us)
